TPU v7x, 128 devices: a whole 4x4x4 slice. The times are simulated.
128 devices in a mesh: gx: 4 (over z), gy: 32 (over y, x, core).
Axes of the slice: x: 4, y: 4, z: 4, core: 2. Of those that a mesh axis runs over, the one named last changes fastest.
Arguments:
- embeddings: bfloat16 [1572864, 256], P(('gx', 'gy'))
- start: float32 [32, 1572864], P(None, ('gx', 'gy'))
- requests: int32 [128, 32], P(('gx', 'gy')), may hold values from -1 to 23, as said below
- pairs: int32 [128, 64, 2], P(('gx', 'gy')), may hold values from 0 to 55, as said below
- counts: int32 [128], P(('gx', 'gy')), may hold values from 24 to 64, as said below
Outputs:
- spectral: float32 [32, 1572864], P(None, ('gx', 'gy'))
Inputs may be any that keep to these rules, and one draw needn't show every extreme that they name: requests[d, q] is -1 where q is d's own index along gy; every entry that is not -1 is used by some live slot of d. A live slot (a, s) has a < 24; if s < 24 then a <= s, else requests[d, s - 24] >= 0; every block of a device has a live slot (a, a); local pairs of one device are distinct; slots at or beyond counts[d] are (0, 0). counts[d] = 24 + (entries of requests[d] that are not -1) + (slots pairing two different blocks of d); in every gx group some device has all 64 slots live.
All inputs are finite; a program needn't handle non-finite values.
Results may differ from a plain program's by a relative error of at most 0.0046.
Values may be sent and summed in bfloat16 or wider, within the bound.
No kernel may reach another device: no remote copies, remote signals or barrier semaphores. Data moves between devices by JAX's collectives and lax.ppermute only.
A program may use at most 192 MiB of HBM per device.

v0:
```python
import jax
import jax.numpy as jnp
from jax import lax
from jax.sharding import PartitionSpec as P

D = 256
VECS = 32
BLK = 512
ITERS = 2


tiles_per_turn = 8


def normalize(raw_rows):
    values = raw_rows.astype(jnp.float32)
    scaled = values * lax.rsqrt(jnp.sum(values * values, axis=-1, keepdims=True) + 1e-06)
    return scaled.astype(jnp.bfloat16)


def to_blocks(matrix, block_count):
    return matrix.reshape(matrix.shape[0], block_count, BLK).transpose(1, 0, 2)


def columns(slot_index, near_src, far_src):
    block_count = near_src.shape[0]
    inside = slot_index < block_count
    own_pick = near_src[jnp.clip(slot_index, 0, block_count - 1)]
    far_pick = far_src[jnp.clip(slot_index - block_count, 0, far_src.shape[0] - 1)]
    return jnp.where(inside[:, None, None], own_pick, far_pick)


def per_device(embeddings, start, requests, pairs, counts):
    peer_count = lax.axis_size("gy")
    row_total = embeddings.shape[0]
    block_count = row_total // BLK
    rows_all = row_total * lax.axis_size("gx") * peer_count
    unit_blocks = normalize(embeddings).reshape(block_count, BLK, D)
    wanted = lax.all_to_all(
        requests.reshape(peer_count, 1), "gy", split_axis=0, concat_axis=0, tiled=True
    )[:, 0]
    served = wanted >= 0
    served_weight = served.astype(jnp.float32)
    wanted_block = jnp.maximum(wanted, 0)

    def outgoing(source):
        picked = source[wanted_block]
        return jnp.where(served[:, None, None], picked, jnp.zeros_like(picked))

    near_vecs = to_blocks(start.astype(jnp.bfloat16), block_count)
    far_vecs = None
    far_rows = lax.all_to_all(outgoing(unit_blocks), "gy", split_axis=0, concat_axis=0, tiled=True)
    slot_total = pairs.shape[1]
    padded = -(-slot_total // tiles_per_turn) * tiles_per_turn
    row_slot = pairs[0, :, 0]
    col_slot = pairs[0, :, 1]
    live_count = counts[0]
    slot_live = jnp.arange(padded, dtype=jnp.int32) < live_count
    turn_count = (live_count + tiles_per_turn - 1) // tiles_per_turn
    row_slot = jnp.clip(row_slot, 0, block_count - 1)
    live_weight = slot_live.astype(jnp.float32)
    both_weight = (slot_live & (row_slot != col_slot)).astype(jnp.float32)

    def build_group(turn_id, tile_stack):
        offset = turn_id * tiles_per_turn
        row_part = lax.dynamic_slice_in_dim(row_slot, offset, tiles_per_turn)
        col_part = lax.dynamic_slice_in_dim(col_slot, offset, tiles_per_turn)
        left_rows = unit_blocks[row_part]
        right_rows = columns(col_part, unit_blocks, far_rows)
        product = jnp.einsum(
            "grd,gcd->grc", left_rows, right_rows, preferred_element_type=jnp.float32
        )
        return lax.dynamic_update_slice_in_dim(
            tile_stack, (product * product * product).astype(jnp.bfloat16), offset, 0
        )

    tile_stack = lax.fori_loop(
        0, turn_count, build_group, jnp.zeros((padded, BLK, BLK), jnp.bfloat16)
    )
    vectors = start
    for iteration in range(ITERS):
        if iteration > 0:
            near_vecs = to_blocks(vectors.astype(jnp.bfloat16), block_count)
        far_vecs = lax.all_to_all(
            outgoing(near_vecs), "gy", split_axis=0, concat_axis=0, tiled=True
        )
        partial_value = jnp.zeros((block_count + peer_count, VECS, BLK), jnp.float32)
        near_src = near_vecs
        far_src = far_vecs

        def add_group(turn_id, running):
            offset = turn_id * tiles_per_turn
            row_part = lax.dynamic_slice_in_dim(row_slot, offset, tiles_per_turn)
            col_part = lax.dynamic_slice_in_dim(col_slot, offset, tiles_per_turn)
            live_part = lax.dynamic_slice_in_dim(live_weight, offset, tiles_per_turn)
            both_part = lax.dynamic_slice_in_dim(both_weight, offset, tiles_per_turn)
            tile_group = lax.dynamic_slice_in_dim(tile_stack, offset, tiles_per_turn)
            row_vecs = near_src[row_part]
            col_vecs = columns(col_part, near_src, far_src)
            to_row = (
                jnp.einsum("gkc,grc->gkr", col_vecs, tile_group, preferred_element_type=jnp.float32)
                * live_part[:, None, None]
            )
            to_col = (
                jnp.einsum("gkr,grc->gkc", row_vecs, tile_group, preferred_element_type=jnp.float32)
                * both_part[:, None, None]
            )
            return running.at[row_part].add(to_row).at[col_part].add(to_col)

        partial_value = lax.fori_loop(0, turn_count, add_group, partial_value)
        returned = lax.all_to_all(
            partial_value[block_count:], "gy", split_axis=0, concat_axis=0, tiled=True
        )
        own_rows = (
            partial_value[:block_count]
            .at[wanted_block]
            .add(returned * served_weight[:, None, None])
        )
        flat_rows = own_rows.transpose(1, 0, 2).reshape(VECS, row_total)
        local_gram = jnp.dot(
            flat_rows,
            flat_rows.T,
            precision=lax.Precision.HIGHEST,
            preferred_element_type=jnp.float32,
        )
        gram_matrix = lax.psum(local_gram, ("gx", "gy"))
        lower_factor = jnp.linalg.cholesky(gram_matrix / rows_all)
        vectors = lax.linalg.triangular_solve(lower_factor, flat_rows, left_side=True, lower=True)
    return vectors


def solution(mesh):
    return jax.shard_map(
        per_device,
        mesh=mesh,
        in_specs=(
            P(("gx", "gy"), None),
            P(None, ("gx", "gy")),
            P(("gx", "gy"), None),
            P(("gx", "gy"), None, None),
            P(("gx", "gy")),
        ),
        out_specs=P(None, ("gx", "gy")),
        check_vma=False,
    )
```

profile of v0, /device:TPU:1, one launch (start us, length us, event | category | flops | bytes accessed | tf_op | source)
XLA Modules:
  0.0 815.8 jit_solution(12413218704562712450)
XLA Ops:
  1.3 8.6 %all-to-all-start = ((s32[32,1,1]{2,1,0:T(1,128)}), s32[32,1,1]{2,1,0:T(1,128)S(1)}, u32[]{:S(2)}, u32[]{:S(2)}) async-start(s32[32,1,1]{2,1,0:T(1,128)} %copy.39), calls=%async_computation | async-start | bytes 32768 | tf_op jit(solution)/shard_map/all_to_all | solution.py:39
  9.9 4.8 fusion.32
  19.4 7.7 gather_fusion.10
  27.8 7.2 broadcast_select_fusion
  35.1 7.6 all-to-all-start.2
  45.3 97.1 %all-to-all-done.2 = bf16[32,512,256]{2,1,0:T(8,128)(2,1)} async-done(((bf16[32,512,256]{2,1,0:T(8,128)(2,1)}), bf16[32,512,256]{2,1,0:T(8,128)(2,1)}, u32[]{:S(2)}, u32[]{:S(2)}) %all-to-all-start.2) | async-done | bytes 8388640 | tf_op jit(solution)/shard_map/all_to_all | solution.py:52
  142.4 10.7 %all-to-all-start.1 = ((bf16[32,32,512]{2,1,0:T(8,128)(2,1)}), bf16[32,32,512]{2,1,0:T(8,128)(2,1)}, u32[]{:S(2)}, u32[]{:S(2)}) async-start(bf16[32,32,512]{2,1,0:T(8,128)(2,1)} %broadcast_select_fusion.2), calls=%async_computation.1 | async-start | bytes 2097152 | tf_op jit(solution)/shard_map/all_to_all | solution.py:84
  153.1 10.9 %broadcast_in_dim.156 = bf16[64,512,512]{2,1,0:T(8,128)(2,1)} broadcast(bf16[]{:T(256)} %constant.209.clone.1), dimensions={} | broadcast | bytes 33554432 | tf_op jit(solution)/shard_map/broadcast_in_dim | solution.py:78
  164.0 116.1 %while.36 = (s32[]{:T(128)}, bf16[64,512,512]{2,1,0:T(8,128)(2,1)}, s32[]{:T(128)}, s32[64]{0:T(128)S(1)}, bf16[24,512,256]{2,1,0:T(8,128)(2,1)}, /*index=5*/s32...) while((s32[]{:T(128)}, bf16[64,512,512]{2,1,0:T(8,128)(2,1)}, ...), condition=%wide.region_2.3_spmd, body=%wide.region_1.2_spmd.sunk | while | flops 1081085056 | bytes 23081528 | solution.py:77
  172.3 5.4 gather_fusion.2
  177.8 5.5 fusion.75
  186.9 4.8 gather_fusion.1
  191.7 5.4 gather_fusion.2
  197.1 5.6 fusion.75
  211.0 5.4 gather_fusion.2
  216.5 5.6 fusion.75
  230.4 5.4 gather_fusion.2
  235.8 5.5 fusion.75
  249.7 5.4 gather_fusion.2
  255.2 5.5 fusion.75
  269.1 5.4 gather_fusion.2
  274.5 5.6 fusion.75
  282.3 90.2 %while.37 = (s32[]{:T(128)}, f32[56,32,512]{2,1,0:T(8,128)}, s32[]{:T(128)}, s32[64]{0:T(128)S(1)}, s32[64]{0:T(128)S(1)}, /*index=5*/bf16[24,32,512]{2,1,0:T(8,...) while((s32[]{:T(128)}, f32[56,32,512]{2,1,0:T(8,128)}, ...), condition=%wide.region_6.7_spmd, body=%wide.region_3.6_spmd.sunk | while | flops 269094016 | bytes 14955479 | solution.py:110
  375.7 76.3 %all-to-all-start.3 = ((f32[32,32,512]{2,1,0:T(8,128)}), f32[32,32,512]{2,1,0:T(8,128)}, u32[]{:S(2)}, u32[]{:S(2)}) async-start(f32[32,32,512]{2,1,0:T(8,128)} %slice.27), calls=%async_computation.3 | async-start | bytes 4194304 | tf_op jit(solution)/shard_map/all_to_all | solution.py:111
  453.6 26.2 %all-to-all-done.3 = f32[32,32,512]{2,1,0:T(8,128)} async-done(((f32[32,32,512]{2,1,0:T(8,128)}), f32[32,32,512]{2,1,0:T(8,128)}, u32[]{:S(2)}, u32[]{:S(2)}) %all-to-all-start.3) | async-done | bytes 2097184 | tf_op jit(solution)/shard_map/all_to_all | solution.py:111
  489.0 64.3 %psum.14 = f32[32,32]{0,1:T(8,128)S(1)} all-reduce(f32[32,32]{0,1:T(8,128)S(1)} %fusion.38), channel_id=1, replica_groups=mesh['gx'=4,'gy'=32] {'gx','gy'}, use_global_device_ids=true, to_apply=%region_8.9 | all-reduce | flops 1024 | bytes 8192 | tf_op jit(solution)/shard_map/psum | solution.py:126
  563.6 4.8 all-to-all-start.4
  568.4 17.2 %all-to-all-done.4 = bf16[32,32,512]{2,1,0:T(8,128)(2,1)S(1)} async-done(((bf16[32,32,512]{2,1,0:T(8,128)(2,1)}), bf16[32,32,512]{2,1,0:T(8,128)(2,1)S(1)}, u32[]{:S(2)}, u32[]{:S(2)}) %all-to-all-start.4) | async-done | bytes 1048608 | tf_op jit(solution)/shard_map/all_to_all | solution.py:84
  587.9 82.9 %while.38 = (s32[]{:T(128)}, f32[56,32,512]{2,1,0:T(8,128)}, s32[]{:T(128)}, s32[64]{0:T(128)S(1)}, s32[64]{0:T(128)S(1)}, /*index=5*/bf16[24,32,512]{2,1,0:T(8,...) while((s32[]{:T(128)}, f32[56,32,512]{2,1,0:T(8,128)}, ...), condition=%wide.region_14.17_spmd, body=%wide.region_11.16_spmd.sunk | while | flops 269094016 | bytes 14955479 | solution.py:110
  673.9 31.4 %all-to-all-start.5 = ((f32[32,32,512]{2,1,0:T(8,128)}), f32[32,32,512]{2,1,0:T(8,128)}, u32[]{:S(2)}, u32[]{:S(2)}) async-start(f32[32,32,512]{2,1,0:T(8,128)} %slice.29), calls=%async_computation.5 | async-start | bytes 4194304 | tf_op jit(solution)/shard_map/all_to_all | solution.py:111
  706.8 26.2 %all-to-all-done.5 = f32[32,32,512]{2,1,0:T(8,128)} async-done(((f32[32,32,512]{2,1,0:T(8,128)}), f32[32,32,512]{2,1,0:T(8,128)}, u32[]{:S(2)}, u32[]{:S(2)}) %all-to-all-start.5) | async-done | bytes 2097184 | tf_op jit(solution)/shard_map/all_to_all | solution.py:111
  742.2 64.1 %psum.15 = f32[32,32]{0,1:T(8,128)S(1)} all-reduce(f32[32,32]{0,1:T(8,128)S(1)} %fusion.41), channel_id=1, replica_groups=mesh['gx'=4,'gy'=32] {'gx','gy'}, use_global_device_ids=true, to_apply=%region_16.19 | all-reduce | flops 1024 | bytes 8192 | tf_op jit(solution)/shard_map/psum | solution.py:126
  (277 shorter events, 278.7 us)
Async XLA Ops:
  1.3 17.4 %all-to-all-start = ((s32[32,1,1]{2,1,0:T(1,128)}), s32[32,1,1]{2,1,0:T(1,128)S(1)}, u32[]{:S(2)}, u32[]{:S(2)}) async-start(s32[32,1,1]{2,1,0:T(1,128)} %copy.39), calls=%async_computation | async-start | bytes 32768 | tf_op jit(solution)/shard_map/all_to_all | solution.py:39
  9.9 4.9 copy-start
  35.1 8.3 %copy-start.1 = (f32[32,12288]{1,0:T(8,128)S(1)}, f32[32,12288]{1,0:T(8,128)}, u32[]{:S(2)}) copy-start(f32[32,12288]{1,0:T(8,128)} %param.15) | copy-start | bytes 4718596
  35.1 107.3 %all-to-all-start.2 = ((bf16[32,512,256]{2,1,0:T(8,128)(2,1)}), bf16[32,512,256]{2,1,0:T(8,128)(2,1)}, u32[]{:S(2)}, u32[]{:S(2)}) async-start(bf16[32,512,256]{2,1,0:T(8,128)(2,1)} %broadcast_select_fusion), calls=%async_computation.2 | async-start | bytes 16777216 | tf_op jit(solution)/shard_map/all_to_all | solution.py:52
  42.7 0.9 copy-start.2
  142.4 137.7 %all-to-all-start.1 = ((bf16[32,32,512]{2,1,0:T(8,128)(2,1)}), bf16[32,32,512]{2,1,0:T(8,128)(2,1)}, u32[]{:S(2)}, u32[]{:S(2)}) async-start(bf16[32,32,512]{2,1,0:T(8,128)(2,1)} %broadcast_select_fusion.2), calls=%async_computation.1 | async-start | bytes 2097152 | tf_op jit(solution)/shard_map/all_to_all | solution.py:84
  375.7 104.1 %all-to-all-start.3 = ((f32[32,32,512]{2,1,0:T(8,128)}), f32[32,32,512]{2,1,0:T(8,128)}, u32[]{:S(2)}, u32[]{:S(2)}) async-start(f32[32,32,512]{2,1,0:T(8,128)} %slice.27), calls=%async_computation.3 | async-start | bytes 4194304 | tf_op jit(solution)/shard_map/all_to_all | solution.py:111
  563.6 22.0 %all-to-all-start.4 = ((bf16[32,32,512]{2,1,0:T(8,128)(2,1)}), bf16[32,32,512]{2,1,0:T(8,128)(2,1)S(1)}, u32[]{:S(2)}, u32[]{:S(2)}) async-start(bf16[32,32,512]{2,1,0:T(8,128)(2,1)} %broadcast_select_fusion.1), calls=%async_computation.4 | async-start | bytes 2097152 | tf_op jit(solution)/shard_map/all_to_all | solution.py:84
  673.9 59.2 %all-to-all-start.5 = ((f32[32,32,512]{2,1,0:T(8,128)}), f32[32,32,512]{2,1,0:T(8,128)}, u32[]{:S(2)}, u32[]{:S(2)}) async-start(f32[32,32,512]{2,1,0:T(8,128)} %slice.29), calls=%async_computation.5 | async-start | bytes 4194304 | tf_op jit(solution)/shard_map/all_to_all | solution.py:111
where the time goes:
time: 821 us; the launch traced here: 816 us
  waiting for transfers between devices  167 us (20%)
  local copies, waits for them, and re-layouts  147 us (18%)
  starting transfers between devices  139 us (17%)
  blocking collectives  128 us (16%)
  matrix products  117 us (14%)
  other arithmetic  115 us (14%)
    psum x2, blocking collectives, per_device(): gram_matrix = lax.psum(local_gram, ('gx', 'gy'))  128 us
    all_to_all x2, starting transfers between devices, per_device(): lax.all_to_all(partial_value[block_count:], 'gy', split_axis=0, concat_ax...  108 us
    all_to_all x1, waiting for transfers between devices, per_device(): lax.all_to_all(outgoing(unit_blocks), 'gy', split_axis=0, concat_axis=0,...  97.1 us
    scatter-add x24, other arithmetic, add_group(): return running.at[row_part].add(to_row).at[col_part].add(to_col)  64.5 us
    all_to_all x2, waiting for transfers between devices, per_device(): lax.all_to_all(partial_value[block_count:], 'gy', split_axis=0, concat_ax...  52.4 us
    gather x18, local copies, waits for them, and re-layouts, columns(): far_src[jnp.clip(slot_index - block_count, 0, far_src.shape[0] - 1)]  46.3 us
    dot_general x12, matrix products, add_group(): jnp.einsum('gkc,grc->gkr', col_vecs, tile_group, preferred_element_type=j...  42 us
    gather x18, local copies, waits for them, and re-layouts, columns(): own_pick = near_src[jnp.clip(slot_index, 0, block_count - 1)]  35.4 us
  transfers between devices with their start and end apart: 6, of which 4 were waited for; matrix products, arithmetic and copies ran while one was open for 17% of the time, Pallas kernels for 0%

commit v1 on v0

v1 whole, which is shorter than its diff:
```python
import functools

import jax
import jax.numpy as jnp
from jax import lax
from jax.experimental import pallas as pl
from jax.experimental.pallas import tpu as pltpu
from jax.sharding import PartitionSpec as P

D = 256
VECS = 32
BLK = 512
ITERS = 2
HALF = BLK // 2
EXTRA = 9

FAR_ROW = 0
LOCAL = 32
LOCAL_COUNT = 96
TABLE = 128

NT = (((1,), (1,)), ((), ()))
NN = (((1,), (0,)), ((), ()))
SMEM = pl.BlockSpec(memory_space=pltpu.SMEM)
VMEM = pl.BlockSpec(memory_space=pltpu.VMEM)
ANY = pl.BlockSpec(memory_space=pl.ANY)
LOOKAHEAD = 3
BUFFERS = 4


def columns_of(block):
    return pl.ds(pl.multiple_of(block * BLK, BLK), BLK)


def params(limit_mib=48):
    return pltpu.CompilerParams(vmem_limit_bytes=limit_mib * 1024 * 1024)


def cost(flops, bytes_accessed):
    return pl.CostEstimate(flops=flops, bytes_accessed=bytes_accessed, transcendentals=0)


def prepare_kernel(pairs, counts, raw, unit, send, table, held, head, following, sem):
    block = pl.program_id(0)
    block_count = held.shape[0]
    peer_count = send.shape[0]

    @pl.when(block == 0)
    def _():
        def clear(i, _):
            table[i] = -1
            return 0

        lax.fori_loop(0, TABLE, clear, 0)

        def clear_head(i, _):
            head[i] = -1
            return 0

        lax.fori_loop(0, block_count, clear_head, 0)

        def note(k, local_count):
            row = pairs[k, 0]
            col = pairs[k, 1]
            far = col >= block_count

            @pl.when(far)
            def _():
                peer = col - block_count
                table[FAR_ROW + peer] = row
                following[peer] = head[row]
                head[row] = peer

            @pl.when(jnp.logical_not(far))
            def _():
                table[LOCAL + local_count] = row * 64 + col

            return local_count + jnp.where(far, 0, 1)

        table[LOCAL_COUNT] = lax.fori_loop(0, counts[0], note, 0)

    values = raw[...].astype(jnp.float32)
    scaled = values * lax.rsqrt(jnp.sum(values * values, axis=-1, keepdims=True) + 1e-06)
    rounded = scaled.astype(jnp.bfloat16)
    unit[0] = rounded
    held[block] = rounded

    def copy(peer, row):
        return pltpu.make_async_copy(held.at[row], send.at[peer], sem.at[peer])

    def emit(peer):
        copy(peer, block).start()
        return following[peer]

    lax.while_loop(lambda peer: peer >= 0, emit, head[block])

    @pl.when(block == block_count - 1)
    def _():
        def finish(peer, _):
            row = table[FAR_ROW + peer]

            @pl.when(row >= 0)
            def _():
                copy(peer, row).wait()

            return 0

        lax.fori_loop(0, peer_count, finish, 0)


def prepare(embeddings, pairs, counts, peer_count):
    block_count = embeddings.shape[0] // BLK
    return pl.pallas_call(
        prepare_kernel,
        grid=(block_count,),
        in_specs=[SMEM, SMEM, pl.BlockSpec((BLK, D), lambda b: (b, 0))],
        out_specs=[pl.BlockSpec((1, BLK, D), lambda b: (b, 0, 0)), ANY, SMEM],
        out_shape=[
            jax.ShapeDtypeStruct((block_count, BLK, D), jnp.bfloat16),
            jax.ShapeDtypeStruct((peer_count, BLK, D), jnp.bfloat16),
            jax.ShapeDtypeStruct((TABLE,), jnp.int32),
        ],
        scratch_shapes=[
            pltpu.VMEM((block_count, BLK, D), jnp.bfloat16),
            pltpu.SMEM((block_count,), jnp.int32),
            pltpu.SMEM((peer_count,), jnp.int32),
            pltpu.SemaphoreType.DMA((peer_count,)),
        ],
        compiler_params=params(),
        cost_estimate=cost(10**7, 20 * 2**20),
        name="prepare",
    )(pairs, counts, embeddings)


def spread(table, source, out):
    def one(peer, _):
        row = table[FAR_ROW + peer]

        @pl.when(row >= 0)
        def _():
            out[peer] = source[:, columns_of(row)]

        @pl.when(row < 0)
        def _():
            out[peer] = jnp.zeros(out.shape[1:], out.dtype)

        return 0

    lax.fori_loop(0, out.shape[0], one, 0)


def first_vectors_kernel(table, start, rounded, out):
    rounded[...] = start[...].astype(jnp.bfloat16)
    spread(table, rounded, out)


def first_vectors(table, start, peer_count):
    return pl.pallas_call(
        first_vectors_kernel,
        in_specs=[SMEM, VMEM],
        out_specs=[VMEM, VMEM],
        out_shape=[
            jax.ShapeDtypeStruct(start.shape, jnp.bfloat16),
            jax.ShapeDtypeStruct((peer_count, VECS, BLK), jnp.bfloat16),
        ],
        compiler_params=params(),
        cost_estimate=cost(10**6, 4 * 2**20),
        name="first_vectors",
    )(table, start)


def half_tile(left, right):
    product = lax.dot_general(left, right, NT, preferred_element_type=jnp.float32)
    return (product * product * product).astype(jnp.bfloat16)


def dot_nt(vecs, tile):
    return lax.dot_general(vecs, tile, NT, preferred_element_type=jnp.float32)


def dot_nn(vecs, tile):
    return lax.dot_general(vecs, tile, NN, preferred_element_type=jnp.float32)


def apply_local(rounded, total, row, col, tile):
    total[:, columns_of(row)] += dot_nt(rounded[:, columns_of(col)], tile[...])

    @pl.when(row != col)
    def _():
        total[:, columns_of(col)] += dot_nn(rounded[:, columns_of(row)], tile[...])


def local_build_kernel(table, units, rounded, total, tiles, buffer, sem):
    count = table[LOCAL_COUNT]
    total[...] = jnp.zeros_like(total)

    def copy(n):
        return pltpu.make_async_copy(buffer.at[n % 2], tiles.at[n], sem.at[n % 2])

    def one(n, _):
        code = table[LOCAL + n]
        row = code // 64
        col = code % 64

        @pl.when(n >= 2)
        def _():
            copy(n - 2).wait()

        tile = buffer.at[n % 2]
        for h in range(2):
            rows = pl.ds(h * HALF, HALF)
            tile[rows, :] = half_tile(units[row, rows, :], units[col])
        copy(n).start()
        apply_local(rounded, total, row, col, tile)
        return 0

    lax.fori_loop(0, count, one, 0)

    @pl.when(count >= 2)
    def _():
        copy(count - 2).wait()

    @pl.when(count >= 1)
    def _():
        copy(count - 1).wait()


def local_build(table, units, rounded):
    block_count = units.shape[0]
    return pl.pallas_call(
        local_build_kernel,
        in_specs=[SMEM, VMEM, VMEM],
        out_specs=[VMEM, ANY],
        out_shape=[
            jax.ShapeDtypeStruct(rounded.shape, jnp.float32),
            jax.ShapeDtypeStruct((block_count + EXTRA, BLK, BLK), jnp.bfloat16),
        ],
        scratch_shapes=[
            pltpu.VMEM((2, BLK, BLK), jnp.bfloat16),
            pltpu.SemaphoreType.DMA((2,)),
        ],
        compiler_params=params(),
        cost_estimate=cost(33 * 2 * BLK * BLK * (D + 8 * VECS), 26 * 2**20),
        name="local_build",
    )(table, units, rounded)


def note_active(wanted, active):
    def one(peer, count):
        @pl.when(wanted[peer] >= 0)
        def _():
            active[count] = peer

        return count + jnp.where(wanted[peer] >= 0, 1, 0)

    return lax.fori_loop(0, wanted.shape[0], one, 0)


def far_build_kernel(wanted, units, far_rows, rounded, back, tiles, active, near, far, buffer, load_sem, save_sem):
    count = note_active(wanted, active)

    def loads(n):
        peer = active[n]
        return (
            pltpu.make_async_copy(far_rows.at[peer], far.at[n], load_sem.at[0, n]),
            pltpu.make_async_copy(units.at[wanted[peer]], near.at[n], load_sem.at[1, n]),
        )

    def begin(n):
        @pl.when(n < count)
        def _():
            for load in loads(n):
                load.start()

    def copy(n):
        return pltpu.make_async_copy(buffer.at[n % 2], tiles.at[active[n]], save_sem.at[n % 2])

    for n in range(LOOKAHEAD):
        begin(n)

    def one(n, _):
        peer = active[n]
        begin(n + LOOKAHEAD)

        @pl.when(n >= 2)
        def _():
            copy(n - 2).wait()

        for load in loads(n):
            load.wait()
        vecs = rounded[:, columns_of(wanted[peer])]
        tile = buffer.at[n % 2]
        for h in range(2):
            rows = pl.ds(h * HALF, HALF)
            part = half_tile(far[n, rows, :], near[n])
            tile[rows, :] = part
            back[peer, :, rows] = dot_nt(vecs, part).astype(jnp.bfloat16)
        copy(n).start()
        return 0

    lax.fori_loop(0, count, one, 0)

    @pl.when(count >= 2)
    def _():
        copy(count - 2).wait()

    @pl.when(count >= 1)
    def _():
        copy(count - 1).wait()


def far_build(wanted, units, far_rows, rounded):
    peer_count = far_rows.shape[0]
    return pl.pallas_call(
        far_build_kernel,
        in_specs=[SMEM, ANY, ANY, VMEM],
        out_specs=[VMEM, ANY],
        out_shape=[
            jax.ShapeDtypeStruct((peer_count, VECS, BLK), jnp.bfloat16),
            jax.ShapeDtypeStruct((peer_count, BLK, BLK), jnp.bfloat16),
        ],
        scratch_shapes=[
            pltpu.SMEM((peer_count,), jnp.int32),
            pltpu.VMEM((peer_count, BLK, D), jnp.bfloat16),
            pltpu.VMEM((peer_count, BLK, D), jnp.bfloat16),
            pltpu.VMEM((2, BLK, BLK), jnp.bfloat16),
            pltpu.SemaphoreType.DMA((2, peer_count)),
            pltpu.SemaphoreType.DMA((2,)),
        ],
        compiler_params=params(),
        cost_estimate=cost(32 * 2 * BLK * BLK * (D + 4 * VECS), 34 * 2**20),
        name="far_build",
    )(wanted, units, far_rows, rounded)


def stream(count, source_of, buffer, sem, use):
    def load(n):
        return pltpu.make_async_copy(source_of(n), buffer.at[n % BUFFERS], sem.at[n % BUFFERS])

    def begin(n):
        @pl.when(n < count)
        def _():
            load(n).start()

    for n in range(BUFFERS - 1):
        begin(n)

    def one(n, _):
        begin(n + BUFFERS - 1)
        load(n).wait()
        use(n, buffer.at[n % BUFFERS])
        return 0

    lax.fori_loop(0, count, one, 0)


def tile_scratch():
    return [
        pltpu.VMEM((BUFFERS, BLK, BLK), jnp.bfloat16),
        pltpu.SemaphoreType.DMA((BUFFERS,)),
    ]


def far_back_kernel(wanted, tiles, rounded, back, active, buffer, sem):
    count = note_active(wanted, active)

    def use(n, tile):
        peer = active[n]
        vecs = rounded[:, columns_of(wanted[peer])]
        back[peer] = dot_nt(vecs, tile[...]).astype(jnp.bfloat16)

    stream(count, lambda n: tiles.at[active[n]], buffer, sem, use)


def far_back(wanted, tiles, rounded):
    peer_count = tiles.shape[0]
    return pl.pallas_call(
        far_back_kernel,
        in_specs=[SMEM, ANY, VMEM],
        out_specs=VMEM,
        out_shape=jax.ShapeDtypeStruct((peer_count, VECS, BLK), jnp.bfloat16),
        scratch_shapes=[pltpu.SMEM((peer_count,), jnp.int32), *tile_scratch()],
        compiler_params=params(),
        cost_estimate=cost(32 * 2 * BLK * BLK * 4 * VECS, 17 * 2**20),
        name="far_back",
    )(wanted, tiles, rounded)


def far_own_kernel(wanted, tiles, far_vecs, before, total, active, buffer, sem):
    count = note_active(wanted, active)
    total[...] = before[...]

    def use(n, tile):
        peer = active[n]
        total[:, columns_of(wanted[peer])] += dot_nn(far_vecs[peer], tile[...])

    stream(count, lambda n: tiles.at[active[n]], buffer, sem, use)


def far_own(wanted, tiles, far_vecs, before):
    peer_count = tiles.shape[0]
    return pl.pallas_call(
        far_own_kernel,
        in_specs=[SMEM, ANY, VMEM, VMEM],
        out_specs=VMEM,
        out_shape=jax.ShapeDtypeStruct(before.shape, jnp.float32),
        scratch_shapes=[pltpu.SMEM((peer_count,), jnp.int32), *tile_scratch()],
        compiler_params=params(),
        cost_estimate=cost(32 * 2 * BLK * BLK * 4 * VECS, 20 * 2**20),
        name="far_own",
    )(wanted, tiles, far_vecs, before)


def local_apply_kernel(table, tiles, rounded, total, buffer, sem):
    total[...] = jnp.zeros_like(total)

    def use(n, tile):
        code = table[LOCAL + n]
        apply_local(rounded, total, code // 64, code % 64, tile)

    stream(table[LOCAL_COUNT], lambda n: tiles.at[n], buffer, sem, use)


def local_apply(table, tiles, rounded):
    return pl.pallas_call(
        local_apply_kernel,
        in_specs=[SMEM, ANY, VMEM],
        out_specs=VMEM,
        out_shape=jax.ShapeDtypeStruct(rounded.shape, jnp.float32),
        scratch_shapes=tile_scratch(),
        compiler_params=params(),
        cost_estimate=cost(33 * 2 * BLK * BLK * 8 * VECS, 18 * 2**20),
        name="local_apply",
    )(table, tiles, rounded)


def assemble_kernel(table, own, returned, image, gram):
    image[...] = own[...]

    def one(peer, _):
        row = table[FAR_ROW + peer]

        @pl.when(row >= 0)
        def _():
            image[:, columns_of(row)] += returned[peer].astype(jnp.float32)

        return 0

    lax.fori_loop(0, returned.shape[0], one, 0)

    def product(block, total):
        part = image[:, columns_of(block)]
        return total + lax.dot_general(
            part, part, NT, precision=lax.Precision.HIGHEST, preferred_element_type=jnp.float32
        )

    gram[...] = lax.fori_loop(0, image.shape[1] // BLK, product, jnp.zeros((VECS, VECS), jnp.float32))


def assemble(table, own, returned):
    return pl.pallas_call(
        assemble_kernel,
        in_specs=[SMEM, VMEM, VMEM],
        out_specs=[VMEM, VMEM],
        out_shape=[
            jax.ShapeDtypeStruct(own.shape, jnp.float32),
            jax.ShapeDtypeStruct((VECS, VECS), jnp.float32),
        ],
        compiler_params=params(),
        cost_estimate=cost(10**8, 5 * 2**20),
        name="assemble",
    )(table, own, returned)


def inverse_factor(matrix):
    rows = lax.broadcasted_iota(jnp.int32, (VECS, VECS), 0)
    lanes = lax.broadcasted_iota(jnp.int32, (VECS, VECS), 1)
    inverse = jnp.where(rows == lanes, 1.0, 0.0).astype(jnp.float32)
    for k in range(VECS):
        scale = lax.rsqrt(matrix[k : k + 1, k : k + 1])
        pivot_row = matrix[k : k + 1, :] * scale
        inverse_row = inverse[k : k + 1, :] * scale
        factor = jnp.where(rows > k, matrix[:, k : k + 1] * scale, 0.0)
        matrix = matrix - factor * pivot_row
        inverse = jnp.where(rows == k, inverse_row, inverse - factor * inverse_row)
    return inverse


def solve_into(inverse, image, block):
    return lax.dot_general(
        inverse,
        image[:, columns_of(block)],
        NN,
        precision=lax.Precision.HIGHEST,
        preferred_element_type=jnp.float32,
    )


def middle_kernel(rows_all, table, gram, image, rounded, out):
    inverse = inverse_factor(gram[...] * (1.0 / rows_all))

    def one(block, _):
        rounded[:, columns_of(block)] = solve_into(inverse, image, block).astype(jnp.bfloat16)
        return 0

    lax.fori_loop(0, image.shape[1] // BLK, one, 0)
    spread(table, rounded, out)


def middle(rows_all, table, gram, image, peer_count):
    return pl.pallas_call(
        functools.partial(middle_kernel, rows_all),
        in_specs=[SMEM, VMEM, VMEM],
        out_specs=[VMEM, VMEM],
        out_shape=[
            jax.ShapeDtypeStruct(image.shape, jnp.bfloat16),
            jax.ShapeDtypeStruct((peer_count, VECS, BLK), jnp.bfloat16),
        ],
        compiler_params=params(),
        cost_estimate=cost(10**8, 4 * 2**20),
        name="middle",
    )(table, gram, image)


def last_kernel(rows_all, gram, image, vectors):
    inverse = inverse_factor(gram[...] * (1.0 / rows_all))

    def one(block, _):
        vectors[:, columns_of(block)] = solve_into(inverse, image, block)
        return 0

    lax.fori_loop(0, image.shape[1] // BLK, one, 0)


def last(rows_all, gram, image):
    return pl.pallas_call(
        functools.partial(last_kernel, rows_all),
        in_specs=[VMEM, VMEM],
        out_specs=VMEM,
        out_shape=jax.ShapeDtypeStruct(image.shape, jnp.float32),
        compiler_params=params(),
        cost_estimate=cost(10**8, 4 * 2**20),
        name="last",
    )(gram, image)


def sum_everywhere(part):
    for axis, masks in (("gy", (1,)), ("gy", (2, 4, 6)), ("gy", (8, 16, 24)), ("gx", (1, 2, 3))):
        size = lax.axis_size(axis)
        arrived = [lax.ppermute(part, axis, [(i, i ^ mask) for i in range(size)]) for mask in masks]
        part = sum(arrived, part)
    return part


def exchange(blocks):
    return lax.all_to_all(blocks, "gy", split_axis=0, concat_axis=0, tiled=True)


def per_device(embeddings, start, requests, pairs, counts):
    peer_count = lax.axis_size("gy")
    rows_all = embeddings.shape[0] * lax.axis_size("gx") * peer_count
    units, send_rows, table = prepare(embeddings, pairs[0], counts, peer_count)
    far_rows = exchange(send_rows)
    wanted = exchange(requests.reshape(peer_count, 1))[:, 0]
    rounded, send_vecs = first_vectors(table, start, peer_count)
    own, local_tiles = local_build(table, units, rounded)
    far_vecs = exchange(send_vecs)
    back, far_tiles = far_build(wanted, units, far_rows, rounded)
    for iteration in range(ITERS):
        if iteration > 0:
            rounded, send_vecs = middle(rows_all, table, gram, image, peer_count)
            far_vecs = exchange(send_vecs)
            back = far_back(wanted, far_tiles, rounded)
            own = local_apply(table, local_tiles, rounded)
        returned = exchange(back)
        own = far_own(wanted, far_tiles, far_vecs, own)
        image, gram = assemble(table, own, returned)
        gram = sum_everywhere(gram)
    return last(rows_all, gram, image)


def solution(mesh):
    return jax.shard_map(
        per_device,
        mesh=mesh,
        in_specs=(
            P(("gx", "gy"), None),
            P(None, ("gx", "gy")),
            P(("gx", "gy"), None),
            P(("gx", "gy"), None, None),
            P(("gx", "gy")),
        ),
        out_specs=P(None, ("gx", "gy")),
        check_vma=False,
    )
```

time: 821 us -> 335 us (0.41)
  local copies, waits for them, and re-layouts: 147 us -> 2.12 us
  blocking collectives: 128 us -> 0 us
  Pallas kernels: 0 us -> 118 us
  matrix products: 117 us -> 0 us
  other arithmetic: 115 us -> 0.71 us
  starting transfers between devices: 139 us -> 81.8 us
  waiting for transfers between devices: 167 us -> 128 us
    psum x2 -> x0, blocking collectives: 128 us -> none  [per_device(): gram_matrix = lax.psum(local_gram, ('gx', 'gy'))]
    gather x57 -> x0, local copies, waits for them, and re-layouts: 118 us -> none  [the longest x18 46.3 us: columns(): far_src[jnp.clip(slot_index - block_count, 0, far_src.shape[0] - 1)]]
    pallas_call x0 -> x12, Pallas kernels: none -> 118 us  [the longest x1 19.9 us: prepare(): pl.pallas_call(prepare_kernel, grid=(block_count,), in_specs=[SMEM, SMEM,...]
    dot_general x32 -> x0, matrix products: 113 us -> none  [the longest x12 42 us: add_group(): jnp.einsum('gkc,grc->gkr', col_vecs, tile_group, preferred_element_type=j...]
    all_to_all x6, starting transfers between devices: 139 us -> 45.9 us  [exchange(): return lax.all_to_all(blocks, 'gy', split_axis=0, concat_axis=0, tiled=True)]
    scatter-add x26 -> x0, other arithmetic: 73.8 us -> none  [the longest x24 64.5 us: add_group(): return running.at[row_part].add(to_row).at[col_part].add(to_col)]
    all_to_all x6, waiting for transfers between devices: 167 us -> 110 us  [exchange(): return lax.all_to_all(blocks, 'gy', split_axis=0, concat_axis=0, tiled=True)]
    ppermute x0 -> x20, starting transfers between devices: none -> 35.9 us  [sum_everywhere(): lax.ppermute(part, axis, [(i, i ^ mask) for i in range(size)])]
  transfers between devices with their start and end apart: 6 -> 26, of which waited for: 4 -> 17; matrix products, arithmetic and copies ran while one was open for 17% -> 0% of each run, Pallas kernels for 0% -> 26%
where the time goes in v1:
time: 335 us; the launch traced here: 331 us
  waiting for transfers between devices  128 us (38%)
  Pallas kernels  118 us (35%)
  starting transfers between devices  81.8 us (24%)
    all_to_all x6, waiting for transfers between devices, exchange(): return lax.all_to_all(blocks, 'gy', split_axis=0, concat_axis=0, tiled=True)  110 us
    all_to_all x6, starting transfers between devices, exchange(): return lax.all_to_all(blocks, 'gy', split_axis=0, concat_axis=0, tiled=True)  45.9 us
    ppermute x20, starting transfers between devices, sum_everywhere(): lax.ppermute(part, axis, [(i, i ^ mask) for i in range(size)])  35.9 us
    pallas_call x1, Pallas kernels, prepare(): pl.pallas_call(prepare_kernel, grid=(block_count,), in_specs=[SMEM, SMEM,...  19.9 us
    pallas_call x1, Pallas kernels, local_build(): pl.pallas_call(local_build_kernel, in_specs=[SMEM, VMEM, VMEM], out_specs...  19.3 us
    ppermute x20, waiting for transfers between devices, sum_everywhere(): lax.ppermute(part, axis, [(i, i ^ mask) for i in range(size)])  18 us
    pallas_call x1, Pallas kernels, far_build(): pl.pallas_call(far_build_kernel, in_specs=[SMEM, ANY, ANY, VMEM], out_spe...  13.3 us
    pallas_call x2, Pallas kernels, assemble(): pl.pallas_call(assemble_kernel, in_specs=[SMEM, VMEM, VMEM], out_specs=[V...  13.3 us
  transfers between devices with their start and end apart: 26, of which 17 were waited for; matrix products, arithmetic and copies ran while one was open for 0% of the time, Pallas kernels for 26%

profile of v1, /device:TPU:1, one launch (start us, length us, event | category | flops | bytes accessed | tf_op | source)
XLA Modules:
  0.0 331.4 jit_solution(11729578771053632406)
XLA Ops:
  1.3 8.6 %all-to-all-start = ((s32[32,1,1]{2,1,0:T(1,128)}), s32[32,1,1]{2,1,0:T(1,128)S(1)}, u32[]{:S(2)}, u32[]{:S(2)}) async-start(s32[32,1,1]{2,1,0:T(1,128)} %copy.10), calls=%async_computation | async-start | bytes 32768 | tf_op jit(solution)/shard_map/all_to_all | solution.py:556
  11.4 19.9 %prepare.1 = (bf16[24,512,256]{2,1,0:T(8,128)(2,1)}, bf16[32,512,256]{2,1,0:T(8,128)(2,1)}, s32[128]{0:T(128)S(1)}) custom-call(s32[64,2]{1,0:T(8,128)S(1)} %copy.9.pairs, s32[1]{0:T(128)S(6)} %copy.11.counts, bf16[12288,256]{1,0:T(8,128)(2,1)} %raw.1), custom_call_target="tpu_custom_call" | custom-call | flops 10000000 | bytes 20971520 | tf_op jit(solution)/shard_map/prepare/pallas_call | solution.py:113
  31.2 7.5 %all-to-all-start.1 = ((bf16[32,512,256]{2,1,0:T(8,128)(2,1)}), bf16[32,512,256]{2,1,0:T(8,128)(2,1)}, u32[]{:S(2)}, u32[]{:S(2)}) async-start(bf16[32,512,256]{2,1,0:T(8,128)(2,1)} %get-tuple-element.22), calls=%async_computation.1 | async-start | bytes 16777216 | tf_op jit(solution)/shard_map/all_to_all | solution.py:556
  38.8 2.2 first_vectors.1
  41.0 97.5 %all-to-all-done.1.far_rows = bf16[32,512,256]{2,1,0:T(8,128)(2,1)} async-done(((bf16[32,512,256]{2,1,0:T(8,128)(2,1)}), bf16[32,512,256]{2,1,0:T(8,128)(2,1)}, u32[]{:S(2)}, u32[]{:S(2)}) %all-to-all-start.1) | async-done | bytes 8388640 | tf_op jit(solution)/shard_map/all_to_all | solution.py:556
  138.5 10.0 %all-to-all-start.2 = ((bf16[32,32,512]{2,1,0:T(8,128)(2,1)}), bf16[32,32,512]{2,1,0:T(8,128)(2,1)S(1)}, u32[]{:S(2)}, u32[]{:S(2)}) async-start(bf16[32,32,512]{2,1,0:T(8,128)(2,1)} %get-tuple-element.25), calls=%async_computation.2 | async-start | bytes 2097152 | tf_op jit(solution)/shard_map/all_to_all | solution.py:556
  149.2 13.3 %far_build.1 = (bf16[32,32,512]{2,1,0:T(8,128)(2,1)}, bf16[32,512,512]{2,1,0:T(8,128)(2,1)}) custom-call(s32[32]{0:T(128)S(1)} %reduce.wanted, bf16[24,512,256]{2,1,0:T(8,128)(2,1)} %get-tuple-element.21.units, bf16[32,512,256]{2,1,0:T(8,128)(2,1)} %all-to-all-done.1.far_rows, bf16[32,12288]{1,0:T(8,128)(2,1)S(1)} %get-tuple-element.23.rounded), custom_call_target="tpu_custom_call" | custom-call | flops 6442450944 | bytes 35651584 | tf_op jit(solution)/shard_map/far_build/pallas_call | solution.py:314
  162.5 3.4 %all-to-all-done.2.far_vecs = bf16[32,32,512]{2,1,0:T(8,128)(2,1)S(1)} async-done(((bf16[32,32,512]{2,1,0:T(8,128)(2,1)}), bf16[32,32,512]{2,1,0:T(8,128)(2,1)S(1)}, u32[]{:S(2)}, u32[]{:S(2)}) %all-to-all-start.2) | async-done | bytes 1048608 | tf_op jit(solution)/shard_map/all_to_all | solution.py:556
  165.8 5.7 %all-to-all-start.3 = ((bf16[32,32,512]{2,1,0:T(8,128)(2,1)}), bf16[32,32,512]{2,1,0:T(8,128)(2,1)}, u32[]{:S(2)}, u32[]{:S(2)}) async-start(bf16[32,32,512]{2,1,0:T(8,128)(2,1)} %get-tuple-element.27), calls=%async_computation.3 | async-start | bytes 2097152 | tf_op jit(solution)/shard_map/all_to_all | solution.py:556
  171.6 19.3 %local_build.1 = (f32[32,12288]{1,0:T(8,128)S(1)}, bf16[33,512,512]{2,1,0:T(8,128)(2,1)}) custom-call(s32[128]{0:T(128)S(1)} %get-tuple-element.20.table, bf16[24,512,256]{2,1,0:T(8,128)(2,1)} %get-tuple-element.21.units, bf16[32,12288]{1,0:T(8,128)(2,1)S(1)} %get-tuple-element.23.rounded), custom_call_target="tpu_custom_call" | custom-call | flops 8858370048 | bytes 27262976 | tf_op jit(solution)/shard_map/local_build/pallas_call | solution.py:230
  190.9 6.5 %far_own.2.own = f32[32,12288]{1,0:T(8,128)S(1)} custom-call(s32[32]{0:T(128)S(1)} %reduce.wanted, bf16[32,512,512]{2,1,0:T(8,128)(2,1)} %get-tuple-element.24.tiles, bf16[32,32,512]{2,1,0:T(8,128)(2,1)S(1)} %all-to-all-done.2.far_vecs, f32[32,12288]{1,0:T(8,128)S(1)} %get-tuple-element.26.before), custom_call_target="tpu_custom_call" | custom-call | flops 2147483648 | bytes 20971520 | tf_op jit(solution)/shard_map/far_own/pallas_call | solution.py:402
  197.5 6.6 %assemble.2 = (f32[32,12288]{1,0:T(8,128)S(1)}, f32[32,32]{1,0:T(8,128)S(1)}) custom-call(s32[128]{0:T(128)S(1)} %get-tuple-element.20.table, f32[32,12288]{1,0:T(8,128)S(1)} %far_own.2.own, bf16[32,32,512]{2,1,0:T(8,128)(2,1)} %all-to-all-done.3.returned), custom_call_target="tpu_custom_call" | custom-call | flops 100000000 | bytes 5242880 | tf_op jit(solution)/shard_map/assemble/pallas_call | solution.py:461
  204.1 2.1 collective-permute-start
  207.1 3.2 collective-permute-start.3
  210.3 3.9 %collective-permute-start.2 = (f32[32,32]{1,0:T(8,128)S(1)}, f32[32,32]{1,0:T(8,128)S(1)}, u32[]{:S(2)}, u32[]{:S(2)}) collective-permute-start(f32[32,32]{1,0:T(8,128)S(1)} %add.60), channel_id=1, source_target_pairs={{0,4},{1,5},{2,6},{3,7},{4,0},{5,1},{6,2},{7,3},{8,12},{9,13},{10,... | collective-permute-start | bytes 12296 | tf_op jit(solution)/shard_map/ppermute | solution.py:550
  222.4 4.8 %collective-permute-start.9 = (f32[32,32]{1,0:T(8,128)S(1)}, f32[32,32]{1,0:T(8,128)S(1)}, u32[]{:S(2)}, u32[]{:S(2)}) collective-permute-start(f32[32,32]{1,0:T(8,128)S(1)} %add_add_fusion.4), channel_id=1, source_target_pairs={{0,96},{32,64},{64,32},{96,0},{1,97},{33,65},{65,33},{97,1},{2,98}... | collective-permute-start | bytes 12296 | tf_op jit(solution)/shard_map/ppermute | solution.py:550
  227.2 3.9 %collective-permute-start.8 = (f32[32,32]{1,0:T(8,128)S(1)}, f32[32,32]{1,0:T(8,128)S(1)}, u32[]{:S(2)}, u32[]{:S(2)}) collective-permute-start(f32[32,32]{1,0:T(8,128)S(1)} %add_add_fusion.4), channel_id=1, source_target_pairs={{0,64},{32,96},{64,0},{96,32},{1,65},{33,97},{65,1},{97,33},{2,66}... | collective-permute-start | bytes 12296 | tf_op jit(solution)/shard_map/ppermute | solution.py:550
  233.8 9.3 %middle.1 = (bf16[32,12288]{1,0:T(8,128)(2,1)S(1)}, bf16[32,32,512]{2,1,0:T(8,128)(2,1)}) custom-call(s32[128]{0:T(128)S(1)} %get-tuple-element.20.table, f32[32,32]{1,0:T(8,128)S(1)} %add_add_fusion.3.gram, f32[32,12288]{1,0:T(8,128)S(1)} %get-tuple-element.29.image), custom_call_target="tpu_custom_call" | custom-call | flops 100000000 | bytes 4194304 | tf_op jit(solution)/shard_map/middle/pallas_call | solution.py:511
  243.1 9.4 %all-to-all-start.4 = ((bf16[32,32,512]{2,1,0:T(8,128)(2,1)}), bf16[32,32,512]{2,1,0:T(8,128)(2,1)S(1)}, u32[]{:S(2)}, u32[]{:S(2)}) async-start(bf16[32,32,512]{2,1,0:T(8,128)(2,1)} %get-tuple-element.30), calls=%async_computation.4 | async-start | bytes 2097152 | tf_op jit(solution)/shard_map/all_to_all | solution.py:556
  252.5 7.9 %far_back.1 = bf16[32,32,512]{2,1,0:T(8,128)(2,1)} custom-call(s32[32]{0:T(128)S(1)} %reduce.wanted, bf16[32,512,512]{2,1,0:T(8,128)(2,1)} %get-tuple-element.24.tiles, bf16[32,12288]{1,0:T(8,128)(2,1)S(1)} %get-tuple-element.32.rounded), custom_call_target="tpu_custom_call" | custom-call | flops 2147483648 | bytes 17825792 | tf_op jit(solution)/shard_map/far_back/pallas_call | solution.py:377
  260.4 9.3 %all-to-all-done.4.far_vecs = bf16[32,32,512]{2,1,0:T(8,128)(2,1)S(1)} async-done(((bf16[32,32,512]{2,1,0:T(8,128)(2,1)}), bf16[32,32,512]{2,1,0:T(8,128)(2,1)S(1)}, u32[]{:S(2)}, u32[]{:S(2)}) %all-to-all-start.4) | async-done | bytes 1048608 | tf_op jit(solution)/shard_map/all_to_all | solution.py:556
  269.6 4.6 %all-to-all-start.5 = ((bf16[32,32,512]{2,1,0:T(8,128)(2,1)}), bf16[32,32,512]{2,1,0:T(8,128)(2,1)}, u32[]{:S(2)}, u32[]{:S(2)}) async-start(bf16[32,32,512]{2,1,0:T(8,128)(2,1)} %far_back.1), calls=%async_computation.5 | async-start | bytes 2097152 | tf_op jit(solution)/shard_map/all_to_all | solution.py:556
  274.3 11.2 %local_apply.1.before = f32[32,12288]{1,0:T(8,128)S(1)} custom-call(s32[128]{0:T(128)S(1)} %get-tuple-element.20.table, bf16[33,512,512]{2,1,0:T(8,128)(2,1)} %get-tuple-element.31.tiles, bf16[32,12288]{1,0:T(8,128)(2,1)S(1)} %get-tuple-element.32.rounded), custom_call_target="tpu_custom_call" | custom-call | flops 4429185024 | bytes 18874368 | tf_op jit(solution)/shard_map/local_apply/pallas_call | solution.py:425
  285.5 6.5 %far_own.3.own = f32[32,12288]{1,0:T(8,128)S(1)} custom-call(s32[32]{0:T(128)S(1)} %reduce.wanted, bf16[32,512,512]{2,1,0:T(8,128)(2,1)} %get-tuple-element.24.tiles, bf16[32,32,512]{2,1,0:T(8,128)(2,1)S(1)} %all-to-all-done.4.far_vecs, f32[32,12288]{1,0:T(8,128)S(1)} %local_apply.1.before), custom_call_target="tpu_custom_call" | custom-call | flops 2147483648 | bytes 20971520 | tf_op jit(solution)/shard_map/far_own/pallas_call | solution.py:402
  292.0 6.6 %assemble.3 = (f32[32,12288]{1,0:T(8,128)S(1)}, f32[32,32]{1,0:T(8,128)S(1)}) custom-call(s32[128]{0:T(128)S(1)} %get-tuple-element.20.table, f32[32,12288]{1,0:T(8,128)S(1)} %far_own.3.own, bf16[32,32,512]{2,1,0:T(8,128)(2,1)} %all-to-all-done.5.returned), custom_call_target="tpu_custom_call" | custom-call | flops 100000000 | bytes 5242880 | tf_op jit(solution)/shard_map/assemble/pallas_call | solution.py:461
  301.5 2.3 collective-permute-start.13
  303.8 3.5 %collective-permute-start.12 = (f32[32,32]{1,0:T(8,128)S(1)}, f32[32,32]{1,0:T(8,128)S(1)}, u32[]{:S(2)}, u32[]{:S(2)}) collective-permute-start(f32[32,32]{1,0:T(8,128)S(1)} %add.70), channel_id=1, source_target_pairs={{0,4},{1,5},{2,6},{3,7},{4,0},{5,1},{6,2},{7,3},{8,12},{9,13},{10,... | collective-permute-start | bytes 12296 | tf_op jit(solution)/shard_map/ppermute | solution.py:550
  309.9 2.0 collective-permute-start.16
  313.7 2.3 collective-permute-done.15
  316.0 2.9 collective-permute-start.19
  320.1 3.0 collective-permute-done.18
  323.0 8.4 %last.1 = f32[32,12288]{1,0:T(8,128)} custom-call(f32[32,32]{1,0:T(8,128)S(1)} %add_add_fusion.gram, f32[32,12288]{1,0:T(8,128)S(1)} %get-tuple-element.34.image), custom_call_target="tpu_custom_call" | custom-call | flops 100000000 | bytes 4194304 | tf_op jit(solution)/shard_map/last/pallas_call | solution.py:536
  (45 shorter events, 22.7 us)
Async XLA Ops:
  1.3 29.9 %all-to-all-start = ((s32[32,1,1]{2,1,0:T(1,128)}), s32[32,1,1]{2,1,0:T(1,128)S(1)}, u32[]{:S(2)}, u32[]{:S(2)}) async-start(s32[32,1,1]{2,1,0:T(1,128)} %copy.10), calls=%async_computation | async-start | bytes 32768 | tf_op jit(solution)/shard_map/all_to_all | solution.py:556
  31.2 7.6 %copy-start = (f32[32,12288]{1,0:T(8,128)S(1)}, f32[32,12288]{1,0:T(8,128)}, u32[]{:S(2)}) copy-start(f32[32,12288]{1,0:T(8,128)} %start.1) | copy-start | bytes 4718596
  31.2 107.3 %all-to-all-start.1 = ((bf16[32,512,256]{2,1,0:T(8,128)(2,1)}), bf16[32,512,256]{2,1,0:T(8,128)(2,1)}, u32[]{:S(2)}, u32[]{:S(2)}) async-start(bf16[32,512,256]{2,1,0:T(8,128)(2,1)} %get-tuple-element.22), calls=%async_computation.1 | async-start | bytes 16777216 | tf_op jit(solution)/shard_map/all_to_all | solution.py:556
  138.5 27.3 %all-to-all-start.2 = ((bf16[32,32,512]{2,1,0:T(8,128)(2,1)}), bf16[32,32,512]{2,1,0:T(8,128)(2,1)S(1)}, u32[]{:S(2)}, u32[]{:S(2)}) async-start(bf16[32,32,512]{2,1,0:T(8,128)(2,1)} %get-tuple-element.25), calls=%async_computation.2 | async-start | bytes 2097152 | tf_op jit(solution)/shard_map/all_to_all | solution.py:556
  165.8 31.6 %all-to-all-start.3 = ((bf16[32,32,512]{2,1,0:T(8,128)(2,1)}), bf16[32,32,512]{2,1,0:T(8,128)(2,1)}, u32[]{:S(2)}, u32[]{:S(2)}) async-start(bf16[32,32,512]{2,1,0:T(8,128)(2,1)} %get-tuple-element.27), calls=%async_computation.3 | async-start | bytes 2097152 | tf_op jit(solution)/shard_map/all_to_all | solution.py:556
  204.1 3.0 collective-permute-start
  207.1 7.2 %collective-permute-start.3 = (f32[32,32]{1,0:T(8,128)S(1)}, f32[32,32]{1,0:T(8,128)S(1)}, u32[]{:S(2)}, u32[]{:S(2)}) collective-permute-start(f32[32,32]{1,0:T(8,128)S(1)} %add.60), channel_id=1, source_target_pairs={{0,6},{1,7},{2,4},{3,5},{4,2},{5,3},{6,0},{7,1},{8,14},{9,15},{10,... | collective-permute-start | bytes 12296 | tf_op jit(solution)/shard_map/ppermute | solution.py:550
  210.3 5.1 %collective-permute-start.2 = (f32[32,32]{1,0:T(8,128)S(1)}, f32[32,32]{1,0:T(8,128)S(1)}, u32[]{:S(2)}, u32[]{:S(2)}) collective-permute-start(f32[32,32]{1,0:T(8,128)S(1)} %add.60), channel_id=1, source_target_pairs={{0,4},{1,5},{2,6},{3,7},{4,0},{5,1},{6,2},{7,3},{8,12},{9,13},{10,... | collective-permute-start | bytes 12296 | tf_op jit(solution)/shard_map/ppermute | solution.py:550
  214.2 2.6 collective-permute-start.1
  216.8 3.8 %collective-permute-start.6 = (f32[32,32]{1,0:T(8,128)S(1)}, f32[32,32]{1,0:T(8,128)S(1)}, u32[]{:S(2)}, u32[]{:S(2)}) collective-permute-start(f32[32,32]{1,0:T(8,128)S(1)} %add_add_fusion.5), channel_id=1, source_target_pairs={{0,24},{1,25},{2,26},{3,27},{4,28},{5,29},{6,30},{7,31},{8,16},{9,... | collective-permute-start | bytes 12296 | tf_op jit(solution)/shard_map/ppermute | solution.py:550
  218.3 4.1 %collective-permute-start.5 = (f32[32,32]{1,0:T(8,128)S(1)}, f32[32,32]{1,0:T(8,128)S(1)}, u32[]{:S(2)}, u32[]{:S(2)}) collective-permute-start(f32[32,32]{1,0:T(8,128)S(1)} %add_add_fusion.5), channel_id=1, source_target_pairs={{0,16},{1,17},{2,18},{3,19},{4,20},{5,21},{6,22},{7,23},{8,24},{9,... | collective-permute-start | bytes 12296 | tf_op jit(solution)/shard_map/ppermute | solution.py:550
  219.6 2.8 collective-permute-start.4
  222.4 8.8 %collective-permute-start.9 = (f32[32,32]{1,0:T(8,128)S(1)}, f32[32,32]{1,0:T(8,128)S(1)}, u32[]{:S(2)}, u32[]{:S(2)}) collective-permute-start(f32[32,32]{1,0:T(8,128)S(1)} %add_add_fusion.4), channel_id=1, source_target_pairs={{0,96},{32,64},{64,32},{96,0},{1,97},{33,65},{65,33},{97,1},{2,98}... | collective-permute-start | bytes 12296 | tf_op jit(solution)/shard_map/ppermute | solution.py:550
  227.2 5.0 %collective-permute-start.8 = (f32[32,32]{1,0:T(8,128)S(1)}, f32[32,32]{1,0:T(8,128)S(1)}, u32[]{:S(2)}, u32[]{:S(2)}) collective-permute-start(f32[32,32]{1,0:T(8,128)S(1)} %add_add_fusion.4), channel_id=1, source_target_pairs={{0,64},{32,96},{64,0},{96,32},{1,65},{33,97},{65,1},{97,33},{2,66}... | collective-permute-start | bytes 12296 | tf_op jit(solution)/shard_map/ppermute | solution.py:550
  231.2 2.6 collective-permute-start.7
  243.1 26.6 %all-to-all-start.4 = ((bf16[32,32,512]{2,1,0:T(8,128)(2,1)}), bf16[32,32,512]{2,1,0:T(8,128)(2,1)S(1)}, u32[]{:S(2)}, u32[]{:S(2)}) async-start(bf16[32,32,512]{2,1,0:T(8,128)(2,1)} %get-tuple-element.30), calls=%async_computation.4 | async-start | bytes 2097152 | tf_op jit(solution)/shard_map/all_to_all | solution.py:556
  269.6 22.4 %all-to-all-start.5 = ((bf16[32,32,512]{2,1,0:T(8,128)(2,1)}), bf16[32,32,512]{2,1,0:T(8,128)(2,1)}, u32[]{:S(2)}, u32[]{:S(2)}) async-start(bf16[32,32,512]{2,1,0:T(8,128)(2,1)} %far_back.1), calls=%async_computation.5 | async-start | bytes 2097152 | tf_op jit(solution)/shard_map/all_to_all | solution.py:556
  298.6 2.8 collective-permute-start.10
  301.5 5.8 %collective-permute-start.13 = (f32[32,32]{1,0:T(8,128)S(1)}, f32[32,32]{1,0:T(8,128)S(1)}, u32[]{:S(2)}, u32[]{:S(2)}) collective-permute-start(f32[32,32]{1,0:T(8,128)S(1)} %add.70), channel_id=1, source_target_pairs={{0,6},{1,7},{2,4},{3,5},{4,2},{5,3},{6,0},{7,1},{8,14},{9,15},{10,... | collective-permute-start | bytes 12296 | tf_op jit(solution)/shard_map/ppermute | solution.py:550
  303.8 4.6 %collective-permute-start.12 = (f32[32,32]{1,0:T(8,128)S(1)}, f32[32,32]{1,0:T(8,128)S(1)}, u32[]{:S(2)}, u32[]{:S(2)}) collective-permute-start(f32[32,32]{1,0:T(8,128)S(1)} %add.70), channel_id=1, source_target_pairs={{0,4},{1,5},{2,6},{3,7},{4,0},{5,1},{6,2},{7,3},{8,12},{9,13},{10,... | collective-permute-start | bytes 12296 | tf_op jit(solution)/shard_map/ppermute | solution.py:550
  307.3 2.6 collective-permute-start.11
  309.9 3.8 %collective-permute-start.16 = (f32[32,32]{1,0:T(8,128)S(1)}, f32[32,32]{1,0:T(8,128)S(1)}, u32[]{:S(2)}, u32[]{:S(2)}) collective-permute-start(f32[32,32]{1,0:T(8,128)S(1)} %add_add_fusion.2), channel_id=1, source_target_pairs={{0,24},{1,25},{2,26},{3,27},{4,28},{5,29},{6,30},{7,31},{8,16},{9,... | collective-permute-start | bytes 12296 | tf_op jit(solution)/shard_map/ppermute | solution.py:550
  311.9 4.1 %collective-permute-start.15 = (f32[32,32]{1,0:T(8,128)S(1)}, f32[32,32]{1,0:T(8,128)S(1)}, u32[]{:S(2)}, u32[]{:S(2)}) collective-permute-start(f32[32,32]{1,0:T(8,128)S(1)} %add_add_fusion.2), channel_id=1, source_target_pairs={{0,16},{1,17},{2,18},{3,19},{4,20},{5,21},{6,22},{7,23},{8,24},{9,... | collective-permute-start | bytes 12296 | tf_op jit(solution)/shard_map/ppermute | solution.py:550
  312.7 3.3 collective-permute-start.14
  316.0 4.0 %collective-permute-start.19 = (f32[32,32]{1,0:T(8,128)S(1)}, f32[32,32]{1,0:T(8,128)S(1)}, u32[]{:S(2)}, u32[]{:S(2)}) collective-permute-start(f32[32,32]{1,0:T(8,128)S(1)} %add_add_fusion.1), channel_id=1, source_target_pairs={{0,96},{32,64},{64,32},{96,0},{1,97},{33,65},{65,33},{97,1},{2,98}... | collective-permute-start | bytes 12296 | tf_op jit(solution)/shard_map/ppermute | solution.py:550
  318.9 4.1 %collective-permute-start.18 = (f32[32,32]{1,0:T(8,128)S(1)}, f32[32,32]{1,0:T(8,128)S(1)}, u32[]{:S(2)}, u32[]{:S(2)}) collective-permute-start(f32[32,32]{1,0:T(8,128)S(1)} %add_add_fusion.1), channel_id=1, source_target_pairs={{0,64},{32,96},{64,0},{96,32},{1,65},{33,97},{65,1},{97,33},{2,66}... | collective-permute-start | bytes 12296 | tf_op jit(solution)/shard_map/ppermute | solution.py:550
  319.6 3.4 %collective-permute-start.17 = (f32[32,32]{1,0:T(8,128)S(1)}, f32[32,32]{1,0:T(8,128)S(1)}, u32[]{:S(2)}, u32[]{:S(2)}) collective-permute-start(f32[32,32]{1,0:T(8,128)S(1)} %add_add_fusion.1), channel_id=1, source_target_pairs={{0,32},{32,0},{64,96},{96,64},{1,33},{33,1},{65,97},{97,65},{2,34}... | collective-permute-start | bytes 12296 | tf_op jit(solution)/shard_map/ppermute | solution.py:550

commit v2 on v1

v2 whole, which is shorter than its diff:
```python
import functools

import jax
import jax.numpy as jnp
from jax import lax
from jax.experimental import pallas as pl
from jax.experimental.pallas import tpu as pltpu
from jax.sharding import PartitionSpec as P

D = 256
VECS = 32
BLK = 512
ITERS = 2
HALF = BLK // 2
EXTRA = 9

FAR_ROW = 0
LOCAL = 32
LOCAL_COUNT = 96
TABLE = 128

NT = (((1,), (1,)), ((), ()))
NN = (((1,), (0,)), ((), ()))
SMEM = pl.BlockSpec(memory_space=pltpu.SMEM)
VMEM = pl.BlockSpec(memory_space=pltpu.VMEM)
HBM = pl.BlockSpec(memory_space=pltpu.HBM)
GROUP = 4
CHUNK = 2048
VEC_ROWS = 2 * VECS
NOTE_ROWS = 16
PACK = 8
NOTE = BLK + VEC_ROWS
SENT = NOTE + NOTE_ROWS


def in_hbm(array):
    return pltpu.with_memory_space_constraint(array, pltpu.HBM)


def columns_of(block):
    return pl.ds(pl.multiple_of(block * BLK, BLK), BLK)


def params(limit_mib):
    return pltpu.CompilerParams(vmem_limit_bytes=limit_mib * 1024 * 1024)


def cost(flops, bytes_accessed):
    return pl.CostEstimate(flops=flops, bytes_accessed=bytes_accessed, transcendentals=0)


def normalized(rows):
    values = rows.astype(jnp.float32)
    scaled = values * lax.rsqrt(jnp.sum(values * values, axis=-1, keepdims=True) + 1e-06)
    return scaled.astype(jnp.bfloat16)


def note_slots(pairs, counts, table, head, following, block_count):
    def clear(i, _):
        table[FAR_ROW + i] = -1
        head[i] = -1
        return 0

    lax.fori_loop(0, following.shape[0], clear, 0)

    def note(k, local_count):
        row = pairs[0, k]
        col = pairs[1, k]
        far = col >= block_count

        @pl.when(far)
        def _():
            peer = col - block_count
            table[FAR_ROW + peer] = row
            following[peer] = head[row]
            head[row] = peer

        @pl.when(jnp.logical_not(far))
        def _():
            table[LOCAL + local_count] = row * 64 + col

        return local_count + jnp.where(far, 0, 1)

    table[LOCAL_COUNT] = lax.fori_loop(0, counts[0], note, 0)


def prepare_kernel(
    pairs, counts, requests, raw, start, send, rounded, table,
    fresh, vecs, held, notes, head, following, load_sem, vec_sem, note_sem, send_sem,
):
    block_count = held.shape[0]
    peer_count = send.shape[0]

    def load(b):
        return pltpu.make_async_copy(raw.at[pl.ds(b * BLK, BLK), :], fresh.at[b], load_sem.at[b])

    def give(peer, b):
        return pltpu.make_async_copy(held.at[b], send.at[peer, pl.ds(0, NOTE), :], send_sem.at[peer])

    load(0).start()
    vec_load = pltpu.make_async_copy(start, vecs, vec_sem)
    vec_load.start()

    def begin(b, _):
        load(b).start()
        return 0

    lax.fori_loop(1, block_count, begin, 0)
    note_slots(pairs, counts, table, head, following, block_count)

    def write_note(peer, _):
        block = requests[0, peer].astype(jnp.float32)
        notes[peer] = jnp.full((NOTE_ROWS, D), block, jnp.float32).astype(jnp.bfloat16)
        return 0

    lax.fori_loop(0, peer_count, write_note, 0)
    note = pltpu.make_async_copy(notes, send.at[:, pl.ds(NOTE, NOTE_ROWS), :], note_sem)
    note.start()
    vec_load.wait()

    def one(b, _):
        load(b).wait()
        held[b, 0:BLK, :] = normalized(fresh[b])
        w = vecs[:, columns_of(b)].astype(jnp.bfloat16)
        rounded[:, columns_of(b)] = w
        held[b, BLK : BLK + VECS, :] = w[:, :HALF]
        held[b, BLK + VECS : NOTE, :] = w[:, HALF:]

        def emit(peer):
            give(peer, b).start()
            return following[peer]

        lax.while_loop(lambda peer: peer >= 0, emit, head[b])
        return 0

    lax.fori_loop(0, block_count, one, 0)

    def given(peer, _):
        row = table[FAR_ROW + peer]

        @pl.when(row >= 0)
        def _():
            give(peer, row).wait()

        return 0

    lax.fori_loop(0, peer_count, given, 0)
    note.wait()


def prepare(embeddings, start, requests, pairs, counts):
    peer_count = requests.shape[1]
    block_count = embeddings.shape[0] // BLK
    lists = max(block_count, peer_count)
    return pl.pallas_call(
        prepare_kernel,
        in_specs=[SMEM, SMEM, SMEM, HBM, HBM],
        out_specs=[HBM, VMEM, SMEM],
        out_shape=[
            pltpu.HBM((peer_count, SENT, D), jnp.bfloat16),
            jax.ShapeDtypeStruct(start.shape, jnp.bfloat16),
            jax.ShapeDtypeStruct((TABLE,), jnp.int32),
        ],
        scratch_shapes=[
            pltpu.VMEM((block_count, BLK, D), jnp.bfloat16),
            pltpu.VMEM(start.shape, jnp.float32),
            pltpu.VMEM((block_count, NOTE, D), jnp.bfloat16),
            pltpu.VMEM((peer_count, NOTE_ROWS, D), jnp.bfloat16),
            pltpu.SMEM((lists,), jnp.int32),
            pltpu.SMEM((lists,), jnp.int32),
            pltpu.SemaphoreType.DMA((block_count,)),
            pltpu.SemaphoreType.DMA,
            pltpu.SemaphoreType.DMA,
            pltpu.SemaphoreType.DMA((peer_count,)),
        ],
        compiler_params=params(20),
        cost_estimate=cost(10**7, 24 * 2**20),
        name="prepare",
    )(pairs, counts, requests, in_hbm(embeddings), in_hbm(start))


def tile_of(left, right):
    product = lax.dot_general(left, right, NT, preferred_element_type=jnp.float32)
    return (product * product * product).astype(jnp.bfloat16)


def dot_nt(vecs, tile):
    return lax.dot_general(vecs, tile, NT, preferred_element_type=jnp.float32)


def dot_nn(vecs, tile):
    return lax.dot_general(vecs, tile, NN, preferred_element_type=jnp.float32)


def local_build_kernel(
    table, raw, rounded, all_units, total, tiles, done, fresh, units, buffer, sem, unit_sem, keep_sem
):
    block_count = units.shape[0]
    load = pltpu.make_async_copy(raw, fresh, unit_sem)
    load.start()
    count = table[LOCAL_COUNT]
    done[0] = count
    total[...] = jnp.zeros_like(total)
    load.wait()

    def normalize(b, _):
        units[b] = normalized(fresh[pl.ds(pl.multiple_of(b * BLK, BLK), BLK), :])
        return 0

    lax.fori_loop(0, block_count, normalize, 0)
    keep = pltpu.make_async_copy(units, all_units, keep_sem)
    keep.start()

    def copy(n):
        return pltpu.make_async_copy(buffer.at[n % 2], tiles.at[n], sem.at[n % 2])

    def one(n, _):
        code = table[LOCAL + n]
        row = code // 64
        col = code % 64

        @pl.when(n >= 2)
        def _():
            copy(n - 2).wait()

        tile = buffer.at[n % 2]
        tile[...] = tile_of(units[row], units[col])
        copy(n).start()
        total[:, columns_of(col)] += dot_nn(rounded[:, columns_of(row)], tile[...])

        @pl.when(row != col)
        def _():
            total[:, columns_of(row)] += dot_nt(rounded[:, columns_of(col)], tile[...])

        return 0

    lax.fori_loop(0, count, one, 0)

    @pl.when(count >= 2)
    def _():
        copy(count - 2).wait()

    @pl.when(count >= 1)
    def _():
        copy(count - 1).wait()

    keep.wait()


def local_build(table, raw, rounded):
    block_count = raw.shape[0] // BLK
    return pl.pallas_call(
        local_build_kernel,
        in_specs=[SMEM, HBM, VMEM],
        out_specs=[HBM, VMEM, HBM, SMEM],
        out_shape=[
            pltpu.HBM((block_count, BLK, D), jnp.bfloat16),
            jax.ShapeDtypeStruct(rounded.shape, jnp.float32),
            pltpu.HBM((block_count + EXTRA, BLK, BLK), jnp.bfloat16),
            jax.ShapeDtypeStruct((1,), jnp.int32),
        ],
        scratch_shapes=[
            pltpu.VMEM(raw.shape, jnp.bfloat16),
            pltpu.VMEM((block_count, BLK, D), jnp.bfloat16),
            pltpu.VMEM((2, BLK, BLK), jnp.bfloat16),
            pltpu.SemaphoreType.DMA((2,)),
            pltpu.SemaphoreType.DMA,
            pltpu.SemaphoreType.DMA,
        ],
        compiler_params=params(20),
        cost_estimate=cost(33 * 2 * BLK * BLK * (D + 8 * VECS), 32 * 2**20),
        name="local_build",
    )(table, in_hbm(raw), rounded)


def note_active(wanted, active):
    def one(peer, count):
        @pl.when(wanted[peer] >= 0)
        def _():
            active[count] = peer

        return count + jnp.where(wanted[peer] >= 0, 1, 0)

    return lax.fori_loop(0, wanted.shape[0], one, 0)


def build_groups(count, active, wanted, units, far_rows, near, far, buffer, load_sem, use, save=None):
    def loads(n):
        peer = active[n]
        return (
            pltpu.make_async_copy(far_rows.at[peer, pl.ds(0, BLK), :], far.at[n], load_sem.at[0, n]),
            pltpu.make_async_copy(units.at[wanted[peer]], near.at[n], load_sem.at[1, n]),
        )

    def begin(n):
        @pl.when(n < count)
        def _():
            for load in loads(n):
                load.start()

    def group(first, base):
        for z in range(GROUP):
            begin(first + 2 * GROUP + z)
        for z in range(GROUP):

            @pl.when(first + z < count)
            def _(n=first + z):
                for load in loads(n):
                    load.wait()

        if save:

            @pl.when(first >= 2 * GROUP)
            def _():
                for z in range(GROUP):
                    save(first - 2 * GROUP + z, base + z).wait()

        held = [jnp.minimum(first + z, count - 1) for z in range(GROUP)]
        live = [first + z < count for z in range(GROUP)]
        for z, n in enumerate(held):
            buffer[base + z] = tile_of(near[n], far[n])
        use([active[n] for n in held], live, [buffer.at[base + z] for z in range(GROUP)])
        if save:
            for z in range(GROUP):

                @pl.when(live[z])
                def _(n=first + z, z=z):
                    save(n, base + z).start()

    def two_groups(i, _):
        first = 2 * GROUP * i
        group(first, 0)

        @pl.when(first + GROUP < count)
        def _():
            group(first + GROUP, GROUP)

        return 0

    for n in range(2 * GROUP):
        begin(n)
    lax.fori_loop(0, (count + 2 * GROUP - 1) // (2 * GROUP), two_groups, 0)
    if save:
        for z in range(2 * GROUP):
            newest = z + 2 * GROUP * ((count - 1 - z) // (2 * GROUP))

            @pl.when((count > z) & (newest // GROUP * GROUP + 2 * GROUP >= count))
            def _(n=newest, z=z):
                save(n, z).wait()


def build_scratch(peer_count):
    return [
        pltpu.SMEM((peer_count,), jnp.int32),
        pltpu.VMEM((peer_count, BLK, D), jnp.bfloat16),
        pltpu.VMEM((peer_count, BLK, D), jnp.bfloat16),
        pltpu.VMEM((2 * GROUP, BLK, BLK), jnp.bfloat16),
        pltpu.SemaphoreType.DMA((2, peer_count)),
    ]


def far_build_kernel(wanted, units, far_rows, rounded, after, back, active, near, far, buffer, load_sem):
    del after
    count = note_active(wanted, active)

    def use(peers, live, group):
        for peer, tile in zip(peers, group):
            vecs = rounded[:, columns_of(wanted[peer])]
            back[peer] = dot_nn(vecs, tile[...]).astype(jnp.bfloat16)

    build_groups(count, active, wanted, units, far_rows, near, far, buffer, load_sem, use)


def far_build(wanted, units, far_rows, rounded, after):
    peer_count = far_rows.shape[0]
    return pl.pallas_call(
        far_build_kernel,
        in_specs=[SMEM, HBM, HBM, VMEM, SMEM],
        out_specs=VMEM,
        out_shape=jax.ShapeDtypeStruct((peer_count, VECS, BLK), jnp.bfloat16),
        scratch_shapes=build_scratch(peer_count),
        compiler_params=params(28),
        cost_estimate=cost(32 * 2 * BLK * BLK * (D + 4 * VECS), 18 * 2**20),
        name="far_build",
    )(wanted, in_hbm(units), in_hbm(far_rows), rounded, after)


def far_first_kernel(
    wanted, units, far_rows, before, total, tiles,
    active, near, far, buffer, load_sem, vecs, save_sem, vec_sem, before_sem,
):
    count = note_active(wanted, active)
    vec_load = pltpu.make_async_copy(far_rows.at[:, pl.ds(BLK, VEC_ROWS), :], vecs, vec_sem)
    before_load = pltpu.make_async_copy(before, total, before_sem)
    vec_load.start()
    before_load.start()

    def save(n, z):
        return pltpu.make_async_copy(buffer.at[z], tiles.at[active[n]], save_sem.at[z])

    def use(peers, live, group):
        terms = []
        for peer, alive, tile in zip(peers, live, group):
            both = vecs[peer]
            both = masked(alive, jnp.concatenate([both[:VECS], both[VECS:]], axis=1))
            terms.append(dot_nt(both, tile[...]))
        for peer, term in zip(peers, terms):
            total[:, columns_of(wanted[peer])] += term

    vec_load.wait()
    before_load.wait()
    build_groups(count, active, wanted, units, far_rows, near, far, buffer, load_sem, use, save)


def far_first(wanted, units, far_rows, before):
    peer_count = far_rows.shape[0]
    return pl.pallas_call(
        far_first_kernel,
        in_specs=[SMEM, HBM, HBM, HBM],
        out_specs=[VMEM, HBM],
        out_shape=[
            jax.ShapeDtypeStruct(before.shape, jnp.float32),
            pltpu.HBM((peer_count, BLK, BLK), jnp.bfloat16),
        ],
        scratch_shapes=[
            *build_scratch(peer_count),
            pltpu.VMEM((peer_count, VEC_ROWS, D), jnp.bfloat16),
            pltpu.SemaphoreType.DMA((2 * GROUP,)),
            pltpu.SemaphoreType.DMA,
            pltpu.SemaphoreType.DMA,
        ],
        compiler_params=params(28),
        cost_estimate=cost(32 * 2 * BLK * BLK * (D + 4 * VECS), 36 * 2**20),
        name="far_first",
    )(wanted, in_hbm(units), in_hbm(far_rows), in_hbm(before))


def stream(count, source_of, buffer, sem, use):
    slots = 2 * GROUP

    def load(n):
        return pltpu.make_async_copy(source_of(n), buffer.at[n % slots], sem.at[n % slots])

    def begin(n):
        @pl.when(n < count)
        def _():
            load(n).start()

    for n in range(GROUP):
        begin(n)

    def group(g, _):
        first = g * GROUP
        for z in range(GROUP):
            begin(first + GROUP + z)
        for z in range(GROUP):

            @pl.when(first + z < count)
            def _(n=first + z):
                load(n).wait()

        held = [jnp.minimum(first + z, count - 1) for z in range(GROUP)]
        live = [first + z < count for z in range(GROUP)]
        use(held, live, [buffer.at[n % slots] for n in held])
        return 0

    lax.fori_loop(0, (count + GROUP - 1) // GROUP, group, 0)


def tile_scratch():
    return [
        pltpu.VMEM((2 * GROUP, BLK, BLK), jnp.bfloat16),
        pltpu.SemaphoreType.DMA((2 * GROUP,)),
    ]


def masked(live, vecs):
    return jnp.where(live, vecs, jnp.zeros_like(vecs))


def far_back_kernel(wanted, tiles, rounded, back, active, buffer, sem):
    count = note_active(wanted, active)

    def use(held, live, group):
        peers = [active[n] for n in held]
        terms = [
            dot_nn(rounded[:, columns_of(wanted[peer])], tile[...]) for peer, tile in zip(peers, group)
        ]
        for peer, term in zip(peers, terms):
            back[peer] = term.astype(jnp.bfloat16)

    stream(count, lambda n: tiles.at[active[n]], buffer, sem, use)


def far_back(wanted, tiles, rounded):
    peer_count = tiles.shape[0]
    return pl.pallas_call(
        far_back_kernel,
        in_specs=[SMEM, HBM, VMEM],
        out_specs=VMEM,
        out_shape=jax.ShapeDtypeStruct((peer_count, VECS, BLK), jnp.bfloat16),
        scratch_shapes=[pltpu.SMEM((peer_count,), jnp.int32), *tile_scratch()],
        compiler_params=params(12),
        cost_estimate=cost(32 * 2 * BLK * BLK * 4 * VECS, 17 * 2**20),
        name="far_back",
    )(wanted, in_hbm(tiles), rounded)


def add_far(wanted, tiles, vecs_of, before, total, active, buffer, sem):
    count = note_active(wanted, active)
    total[...] = before[...]

    def use(held, live, group):
        peers = [active[n] for n in held]
        terms = [
            dot_nt(masked(alive, vecs_of(peer)), tile[...])
            for peer, alive, tile in zip(peers, live, group)
        ]
        for peer, term in zip(peers, terms):
            total[:, columns_of(wanted[peer])] += term

    stream(count, lambda n: tiles.at[active[n]], buffer, sem, use)


def far_next_kernel(wanted, tiles, far_vecs, before, total, active, buffer, sem):
    add_far(wanted, tiles, lambda peer: far_vecs[peer], before, total, active, buffer, sem)


def far_next(wanted, tiles, far_vecs, before):
    peer_count = tiles.shape[0]
    return pl.pallas_call(
        far_next_kernel,
        in_specs=[SMEM, HBM, VMEM, VMEM],
        out_specs=VMEM,
        out_shape=jax.ShapeDtypeStruct(before.shape, jnp.float32),
        scratch_shapes=[pltpu.SMEM((peer_count,), jnp.int32), *tile_scratch()],
        compiler_params=params(14),
        cost_estimate=cost(32 * 2 * BLK * BLK * 4 * VECS, 20 * 2**20),
        name="far_next",
    )(wanted, in_hbm(tiles), far_vecs, before)


def local_apply_kernel(table, tiles, rounded, total, buffer, sem):
    total[...] = jnp.zeros_like(total)

    def use(held, live, group):
        codes = [table[LOCAL + n] for n in held]
        terms = [
            dot_nn(masked(alive, rounded[:, columns_of(code // 64)]), tile[...])
            for code, alive, tile in zip(codes, live, group)
        ]
        for code, term in zip(codes, terms):
            total[:, columns_of(code % 64)] += term
        for code, alive, tile in zip(codes, live, group):
            row = code // 64
            col = code % 64

            @pl.when(alive & (row != col))
            def _(row=row, col=col, tile=tile):
                total[:, columns_of(row)] += dot_nt(rounded[:, columns_of(col)], tile[...])

    stream(table[LOCAL_COUNT], lambda n: tiles.at[n], buffer, sem, use)


def local_apply(table, tiles, rounded):
    return pl.pallas_call(
        local_apply_kernel,
        in_specs=[SMEM, HBM, VMEM],
        out_specs=VMEM,
        out_shape=jax.ShapeDtypeStruct(rounded.shape, jnp.float32),
        scratch_shapes=tile_scratch(),
        compiler_params=params(12),
        cost_estimate=cost(33 * 2 * BLK * BLK * 8 * VECS, 18 * 2**20),
        name="local_apply",
    )(table, in_hbm(tiles), rounded)


def three_parts(values):
    high = values.astype(jnp.bfloat16)
    rest = values - high.astype(jnp.float32)
    middle = rest.astype(jnp.bfloat16)
    low = (rest - middle.astype(jnp.float32)).astype(jnp.bfloat16)
    return high, middle, low


def factor_parts(factor):
    high, middle, low = three_parts(factor)
    return jnp.concatenate([high, high, high, middle, middle, low], axis=1)


def solved(factor, values):
    high, middle, low = three_parts(values)
    return dot_nn(factor, jnp.concatenate([high, middle, low, high, middle, high], axis=0))


def products(values):
    parts = jnp.concatenate(three_parts(values), axis=0)
    return dot_nt(parts, parts)


def assemble_kernel(table, own, returned, image, gram):
    image[...] = own[...]

    def add(peer, _):
        row = table[FAR_ROW + peer]

        @pl.when(row >= 0)
        def _():
            image[:, columns_of(row)] += returned[peer].astype(jnp.float32)

        return 0

    lax.fori_loop(0, returned.shape[0], add, 0)
    total = jnp.zeros((3 * VECS, 3 * VECS), jnp.float32)
    for c in range(0, image.shape[1], CHUNK):
        total += products(image[:, c : c + CHUNK])
    total = total[:VECS] + total[VECS : 2 * VECS] + total[2 * VECS :]
    total = total[:, :VECS] + total[:, VECS : 2 * VECS] + total[:, 2 * VECS :]
    gram[...] = jnp.concatenate([total[r : r + PACK] for r in range(0, VECS, PACK)], axis=1)


def assemble(table, own, returned):
    return pl.pallas_call(
        assemble_kernel,
        in_specs=[SMEM, VMEM, VMEM],
        out_specs=[VMEM, VMEM],
        out_shape=[
            jax.ShapeDtypeStruct(own.shape, jnp.float32),
            jax.ShapeDtypeStruct((PACK, VECS * VECS // PACK), jnp.float32),
        ],
        compiler_params=params(10),
        cost_estimate=cost(10**8, 5 * 2**20),
        name="assemble",
    )(table, own, returned)


def inverse_factor(matrix):
    both = (VECS, 2 * VECS)
    rows = lax.broadcasted_iota(jnp.int32, both, 0)
    lanes = lax.broadcasted_iota(jnp.int32, both, 1)
    work = jnp.where(
        lanes < VECS,
        jnp.concatenate([matrix, matrix], axis=1),
        jnp.where(rows + VECS == lanes, 1.0, 0.0),
    )
    for k in range(0, VECS, 2):
        first_col = jnp.broadcast_to(work[:, k : k + 1], both)
        next_col = jnp.broadcast_to(work[:, k + 1 : k + 2], both)
        scale = lax.rsqrt(first_col[k : k + 1])
        first_row = work[k : k + 1] * scale
        cross = next_col[k : k + 1] * scale
        next_scale = lax.rsqrt(next_col[k + 1 : k + 2] - cross * cross)
        next_row = (work[k + 1 : k + 2] - cross * first_row) * next_scale
        first_factor = first_col * scale
        next_factor = (next_col - first_factor * cross) * next_scale
        rest = work - (first_factor * first_row + next_factor * next_row)
        kept = jnp.where(rows == k, first_row, jnp.where(rows == k + 1, next_row, work))
        work = jnp.where(rows > k + 1, rest, kept)
    return work[:, VECS:]


def summed_inverse(rows_all, grams):
    packed = jnp.sum(grams[...], axis=0)
    gram = jnp.concatenate([packed[:, c : c + VECS] for c in range(0, packed.shape[1], VECS)], axis=0)
    return factor_parts(inverse_factor(gram * (1.0 / rows_all)))


def middle_kernel(rows_all, table, grams, image, rounded, out):
    factor = summed_inverse(rows_all, grams)
    for c in range(0, image.shape[1], CHUNK):
        rounded[:, c : c + CHUNK] = solved(factor, image[:, c : c + CHUNK]).astype(jnp.bfloat16)

    def give(peer, _):
        row = table[FAR_ROW + peer]

        @pl.when(row >= 0)
        def _():
            out[peer] = rounded[:, columns_of(row)]

        return 0

    lax.fori_loop(0, out.shape[0], give, 0)


def middle(rows_all, table, grams, image):
    return pl.pallas_call(
        functools.partial(middle_kernel, rows_all),
        in_specs=[SMEM, VMEM, VMEM],
        out_specs=[VMEM, VMEM],
        out_shape=[
            jax.ShapeDtypeStruct(image.shape, jnp.bfloat16),
            jax.ShapeDtypeStruct((grams.shape[0], VECS, BLK), jnp.bfloat16),
        ],
        compiler_params=params(10),
        cost_estimate=cost(10**8, 4 * 2**20),
        name="middle",
    )(table, grams, image)


def last_kernel(rows_all, grams, image, vectors):
    factor = summed_inverse(rows_all, grams)
    for c in range(0, image.shape[1], CHUNK):
        vectors[:, c : c + CHUNK] = solved(factor, image[:, c : c + CHUNK])


def last(rows_all, grams, image):
    return pl.pallas_call(
        functools.partial(last_kernel, rows_all),
        in_specs=[VMEM, VMEM],
        out_specs=VMEM,
        out_shape=jax.ShapeDtypeStruct(image.shape, jnp.float32),
        compiler_params=params(10),
        cost_estimate=cost(10**8, 4 * 2**20),
        name="last",
    )(grams, image)


def all_parts(gram):
    size = lax.axis_size("gx")
    arrived = [
        lax.ppermute(gram, "gx", [(i, i ^ mask) for i in range(size)]) for mask in range(1, size)
    ]
    gram = sum(arrived, gram)
    return exchange(jnp.broadcast_to(gram, (lax.axis_size("gy"), *gram.shape)))


def exchange(blocks):
    return lax.all_to_all(blocks, "gy", split_axis=0, concat_axis=0, tiled=True)


def per_device(embeddings, start, requests, pairs, counts):
    rows_all = embeddings.shape[0] * lax.axis_size("gx") * lax.axis_size("gy")
    send_rows, rounded, table = prepare(embeddings, start, requests, pairs[0].T, counts)
    far_rows = exchange(send_rows)
    units, own, local_tiles, done = local_build(table, embeddings, rounded)
    wanted = far_rows[:, NOTE, 0].astype(jnp.int32)
    returned = exchange(far_build(wanted, units, far_rows, rounded, done))
    own, far_tiles = far_first(wanted, units, far_rows, own)
    for _ in range(ITERS - 1):
        image, gram = assemble(table, own, returned)
        rounded, send_vecs = middle(rows_all, table, all_parts(gram), image)
        far_vecs = exchange(send_vecs)
        back = far_back(wanted, far_tiles, rounded)
        own = local_apply(table, local_tiles, rounded)
        returned = exchange(back)
        own = far_next(wanted, far_tiles, far_vecs, own)
    image, gram = assemble(table, own, returned)
    return last(rows_all, all_parts(gram), image)


def solution(mesh):
    return jax.shard_map(
        per_device,
        mesh=mesh,
        in_specs=(
            P(("gx", "gy"), None),
            P(None, ("gx", "gy")),
            P(("gx", "gy"), None),
            P(("gx", "gy"), None, None),
            P(("gx", "gy")),
        ),
        out_specs=P(None, ("gx", "gy")),
        check_vma=False,
    )
```

time: 335 us -> 274 us (0.82)
  starting transfers between devices: 81.8 us -> 35.3 us
  blocking collectives: 0 us -> 29.4 us
  Pallas kernels: 118 us -> 94.8 us
  waiting for transfers between devices: 128 us -> 108 us
    all_to_all x0 -> x2, blocking collectives: none -> 29.4 us  [exchange(): return lax.all_to_all(blocks, 'gy', split_axis=0, concat_axis=0, tiled=True)]
    ppermute x20 -> x6, starting transfers between devices: 35.9 us -> 8.14 us  [all_parts(): lax.ppermute(gram, 'gx', [(i, i ^ mask) for i in range(size)])]
    all_to_all x6 -> x4, starting transfers between devices: 45.9 us -> 27.2 us  [exchange(): return lax.all_to_all(blocks, 'gy', split_axis=0, concat_axis=0, tiled=True)]
    ppermute x20 -> x6, waiting for transfers between devices: 18 us -> 5.65 us  [all_parts(): lax.ppermute(gram, 'gx', [(i, i ^ mask) for i in range(size)])]
    pallas_call x2, Pallas kernels: 13.3 us -> 4.78 us  [assemble(): pl.pallas_call(assemble_kernel, in_specs=[SMEM, VMEM, VMEM], out_specs=[V...]
    all_to_all x6 -> x4, waiting for transfers between devices: 110 us -> 102 us  [exchange(): return lax.all_to_all(blocks, 'gy', split_axis=0, concat_axis=0, tiled=True)]
    pallas_call x8 -> x7, Pallas kernels: 86.8 us -> 81.7 us  [the longest x1 27.3 us: local_build(): pl.pallas_call(local_build_kernel, in_specs=[SMEM, HBM, VMEM], out_specs=...]
    pallas_call x1, Pallas kernels: 9.33 us -> 4.58 us  [middle(): pl.pallas_call(functools.partial(middle_kernel, rows_all), in_specs=[SMEM...]
  transfers between devices with their start and end apart: 26 -> 10, of which waited for: 17 -> 8; matrix products, arithmetic and copies ran while one was open for 0% -> 0% of each run, Pallas kernels for 26% -> 24%
where the time goes in v2:
time: 274 us; the launch traced here: 272 us
  waiting for transfers between devices  108 us (39%)
  Pallas kernels  94.8 us (35%)
  starting transfers between devices  35.3 us (13%)
  blocking collectives  29.4 us (11%)
    all_to_all x4, waiting for transfers between devices, exchange(): return lax.all_to_all(blocks, 'gy', split_axis=0, concat_axis=0, tiled=True)  102 us
    all_to_all x2, blocking collectives, exchange(): return lax.all_to_all(blocks, 'gy', split_axis=0, concat_axis=0, tiled=True)  29.4 us
    pallas_call x1, Pallas kernels, local_build(): pl.pallas_call(local_build_kernel, in_specs=[SMEM, HBM, VMEM], out_specs=...  27.3 us
    all_to_all x4, starting transfers between devices, exchange(): return lax.all_to_all(blocks, 'gy', split_axis=0, concat_axis=0, tiled=True)  27.2 us
    pallas_call x1, Pallas kernels, far_first(): pl.pallas_call(far_first_kernel, in_specs=[SMEM, HBM, HBM, HBM], out_spec...  11.8 us
    pallas_call x1, Pallas kernels, local_apply(): pl.pallas_call(local_apply_kernel, in_specs=[SMEM, HBM, VMEM], out_specs=...  10.4 us
    pallas_call x1, Pallas kernels, far_build(): pl.pallas_call(far_build_kernel, in_specs=[SMEM, HBM, HBM, VMEM, SMEM], o...  9.9 us
    ppermute x6, starting transfers between devices, all_parts(): lax.ppermute(gram, 'gx', [(i, i ^ mask) for i in range(size)])  8.14 us
  transfers between devices with their start and end apart: 10, of which 8 were waited for; matrix products, arithmetic and copies ran while one was open for 0% of the time, Pallas kernels for 24%

profile of v2, /device:TPU:1, one launch (start us, length us, event | category | flops | bytes accessed | tf_op | source)
XLA Modules:
  0.0 272.5 jit_solution(13065107349483906418)
XLA Ops:
  0.7 0.7 copy-done
  1.3 0.7 copy-done.1
  2.0 7.6 %prepare.1 = (bf16[32,592,256]{2,1,0:T(8,128)(2,1)}, bf16[32,12288]{1,0:T(8,128)(2,1)S(1)}, s32[128]{0:T(128)S(1)}) custom-call(s32[2,64]{1,0:T(2,128)S(1)} %bitcast.3, s32[1]{0:T(128)S(6)} %copy.6.counts, s32[1,32]{1,0:T(1,128)S(1)} %copy-done.1, bf16[12288,256]{1,0:T(8,128)(2,1)} %raw.3, f32[32,12288]{1,0:T(8,128)} %start.1), custom_call_target="tpu_custom_call" | custom-call | flops 10000000 | bytes 25165824 | tf_op jit(solution)/shard_map/prepare/pallas_call | solution.py:155
  9.6 8.5 %all-to-all-start = ((bf16[32,592,256]{2,1,0:T(8,128)(2,1)}), bf16[32,592,256]{2,1,0:T(8,128)(2,1)}, u32[]{:S(2)}, u32[]{:S(2)}) async-start(bf16[32,592,256]{2,1,0:T(8,128)(2,1)} %get-tuple-element.21), calls=%async_computation | async-start | bytes 19398656 | tf_op jit(solution)/shard_map/all_to_all | solution.py:728
  18.0 27.3 %local_build.1 = (bf16[24,512,256]{2,1,0:T(8,128)(2,1)}, f32[32,12288]{1,0:T(8,128)S(1)}, bf16[33,512,512]{2,1,0:T(8,128)(2,1)}, s32[1]{0:T(128)}) custom-call(s32[128]{0:T(128)S(1)} %get-tuple-element.20.table, bf16[12288,256]{1,0:T(8,128)(2,1)} %raw.3, bf16[32,12288]{1,0:T(8,128)(2,1)S(1)} %get-tuple-element.22.rounded), custom_call_target="tpu_custom_call" | custom-call | flops 8858370048 | bytes 33554432 | tf_op jit(solution)/shard_map/local_build/pallas_call | solution.py:252
  45.4 1.1 copy-done.2
  46.5 87.2 %all-to-all-done.far_rows = bf16[32,592,256]{2,1,0:T(8,128)(2,1)} async-done(((bf16[32,592,256]{2,1,0:T(8,128)(2,1)}), bf16[32,592,256]{2,1,0:T(8,128)(2,1)}, u32[]{:S(2)}, u32[]{:S(2)}) %all-to-all-start) | async-done | bytes 9699360 | tf_op jit(solution)/shard_map/all_to_all | solution.py:728
  133.7 1.5 fusion.wanted
  135.2 9.9 %far_build.1 = bf16[32,32,512]{2,1,0:T(8,128)(2,1)} custom-call(s32[32]{0:T(128)S(1)} %fusion.wanted, bf16[24,512,256]{2,1,0:T(8,128)(2,1)} %get-tuple-element.23.units, bf16[32,592,256]{2,1,0:T(8,128)(2,1)} %all-to-all-done.far_rows, bf16[32,12288]{1,0:T(8,128)(2,1)S(1)} %get-tuple-element.22.rounded, s32[1]{0:T(128)} %get-tuple-element.27.after), custom_call_target="tpu_custom_call" | custom-call | flops 6442450944 | bytes 18874368 | tf_op jit(solution)/shard_map/far_build/pallas_call | solution.py:376
  145.1 10.1 %all-to-all-start.1 = ((bf16[32,32,512]{2,1,0:T(8,128)(2,1)}), bf16[32,32,512]{2,1,0:T(8,128)(2,1)S(1)}, u32[]{:S(2)}, u32[]{:S(2)}) async-start(bf16[32,32,512]{2,1,0:T(8,128)(2,1)} %far_build.1), calls=%async_computation.1 | async-start | bytes 2097152 | tf_op jit(solution)/shard_map/all_to_all | solution.py:728
  155.2 11.8 %far_first.1 = (f32[32,12288]{1,0:T(8,128)S(1)}, bf16[32,512,512]{2,1,0:T(8,128)(2,1)}) custom-call(s32[32]{0:T(128)S(1)} %fusion.wanted, bf16[24,512,256]{2,1,0:T(8,128)(2,1)} %get-tuple-element.23.units, bf16[32,592,256]{2,1,0:T(8,128)(2,1)} %all-to-all-done.far_rows, f32[32,12288]{1,0:T(8,128)} %copy-done.2), custom_call_target="tpu_custom_call" | custom-call | flops 6442450944 | bytes 37748736 | tf_op jit(solution)/shard_map/far_first/pallas_call | solution.py:417
  166.9 5.5 %all-to-all-done.1.returned = bf16[32,32,512]{2,1,0:T(8,128)(2,1)S(1)} async-done(((bf16[32,32,512]{2,1,0:T(8,128)(2,1)}), bf16[32,32,512]{2,1,0:T(8,128)(2,1)S(1)}, u32[]{:S(2)}, u32[]{:S(2)}) %all-to-all-start.1) | async-done | bytes 1048608 | tf_op jit(solution)/shard_map/all_to_all | solution.py:728
  172.4 2.0 assemble.2
  174.5 4.1 %collective-permute-start.2 = (f32[8,128]{1,0:T(8,128)S(1)}, f32[8,128]{1,0:T(8,128)S(1)}, u32[]{:S(2)}, u32[]{:S(2)}) collective-permute-start(f32[8,128]{1,0:T(8,128)S(1)} %get-tuple-element.28), channel_id=1, source_target_pairs={{0,96},{32,64},{64,32},{96,0},{1,97},{33,65},{65,33},{97,1},{2,98}... | collective-permute-start | bytes 12296 | tf_op jit(solution)/shard_map/ppermute | solution.py:721
  178.6 0.7 collective-permute-start.1
  179.6 3.0 %collective-permute-done.1 = f32[8,128]{1,0:T(8,128)S(1)} collective-permute-done((f32[8,128]{1,0:T(8,128)S(1)}, f32[8,128]{1,0:T(8,128)S(1)}, u32[]{:S(2)}, u32[]{:S(2)}) %collective-permute-start.1) | collective-permute-done | bytes 4128 | tf_op jit(solution)/shard_map/ppermute | solution.py:721
  182.6 12.5 %all_to_all.30.grams = f32[32,8,128]{2,1,0:T(8,128)S(1)} all-to-all(f32[32,8,128]{2,1,0:T(8,128)S(1)} %broadcast_in_dim.6), channel_id=1, replica_groups=mesh['gx'=4,'gy'=32] {'gy'}, dimensions={0} | all-to-all | bytes 262144 | tf_op jit(solution)/shard_map/all_to_all | solution.py:728
  195.1 4.6 %middle.1 = (bf16[32,12288]{1,0:T(8,128)(2,1)S(1)}, bf16[32,32,512]{2,1,0:T(8,128)(2,1)}) custom-call(s32[128]{0:T(128)S(1)} %get-tuple-element.20.table, f32[32,8,128]{2,1,0:T(8,128)S(1)} %all_to_all.30.grams, f32[32,12288]{1,0:T(8,128)S(1)} %get-tuple-element.29.image), custom_call_target="tpu_custom_call" | custom-call | flops 100000000 | bytes 4194304 | tf_op jit(solution)/shard_map/middle/pallas_call | solution.py:686
  199.7 4.0 %all-to-all-start.3 = ((bf16[32,32,512]{2,1,0:T(8,128)(2,1)}), bf16[32,32,512]{2,1,0:T(8,128)(2,1)S(1)}, u32[]{:S(2)}, u32[]{:S(2)}) async-start(bf16[32,32,512]{2,1,0:T(8,128)(2,1)} %get-tuple-element.30), calls=%async_computation.3 | async-start | bytes 2097152 | tf_op jit(solution)/shard_map/all_to_all | solution.py:728
  203.7 7.5 %far_back.1 = bf16[32,32,512]{2,1,0:T(8,128)(2,1)} custom-call(s32[32]{0:T(128)S(1)} %fusion.wanted, bf16[32,512,512]{2,1,0:T(8,128)(2,1)} %get-tuple-element.25.tiles, bf16[32,12288]{1,0:T(8,128)(2,1)S(1)} %get-tuple-element.32.rounded), custom_call_target="tpu_custom_call" | custom-call | flops 2147483648 | bytes 17825792 | tf_op jit(solution)/shard_map/far_back/pallas_call | solution.py:497
  211.2 9.8 %all-to-all-done.3.far_vecs = bf16[32,32,512]{2,1,0:T(8,128)(2,1)S(1)} async-done(((bf16[32,32,512]{2,1,0:T(8,128)(2,1)}), bf16[32,32,512]{2,1,0:T(8,128)(2,1)S(1)}, u32[]{:S(2)}, u32[]{:S(2)}) %all-to-all-start.3) | async-done | bytes 1048608 | tf_op jit(solution)/shard_map/all_to_all | solution.py:728
  221.0 4.6 %all-to-all-start.4 = ((bf16[32,32,512]{2,1,0:T(8,128)(2,1)}), bf16[32,32,512]{2,1,0:T(8,128)(2,1)}, u32[]{:S(2)}, u32[]{:S(2)}) async-start(bf16[32,32,512]{2,1,0:T(8,128)(2,1)} %far_back.1), calls=%async_computation.4 | async-start | bytes 2097152 | tf_op jit(solution)/shard_map/all_to_all | solution.py:728
  225.6 10.4 %local_apply.1.before = f32[32,12288]{1,0:T(8,128)S(1)} custom-call(s32[128]{0:T(128)S(1)} %get-tuple-element.20.table, bf16[33,512,512]{2,1,0:T(8,128)(2,1)} %get-tuple-element.31.tiles, bf16[32,12288]{1,0:T(8,128)(2,1)S(1)} %get-tuple-element.32.rounded), custom_call_target="tpu_custom_call" | custom-call | flops 4429185024 | bytes 18874368 | tf_op jit(solution)/shard_map/local_apply/pallas_call | solution.py:566
  236.0 7.2 %far_next.1.own = f32[32,12288]{1,0:T(8,128)S(1)} custom-call(s32[32]{0:T(128)S(1)} %fusion.wanted, bf16[32,512,512]{2,1,0:T(8,128)(2,1)} %get-tuple-element.25.tiles, bf16[32,32,512]{2,1,0:T(8,128)(2,1)S(1)} %all-to-all-done.3.far_vecs, f32[32,12288]{1,0:T(8,128)S(1)} %local_apply.1.before), custom_call_target="tpu_custom_call" | custom-call | flops 2147483648 | bytes 20971520 | tf_op jit(solution)/shard_map/far_next/pallas_call | solution.py:531
  243.3 2.7 %assemble.3 = (f32[32,12288]{1,0:T(8,128)S(1)}, f32[8,128]{1,0:T(8,128)S(1)}) custom-call(s32[128]{0:T(128)S(1)} %get-tuple-element.20.table, f32[32,12288]{1,0:T(8,128)S(1)} %far_next.1.own, bf16[32,32,512]{2,1,0:T(8,128)(2,1)} %all-to-all-done.4.returned), custom_call_target="tpu_custom_call" | custom-call | flops 100000000 | bytes 5242880 | tf_op jit(solution)/shard_map/assemble/pallas_call | solution.py:623
  246.0 1.2 collective-permute-start.5
  247.2 1.7 collective-permute-start.4
  249.3 0.4 collective-permute-done.5
  249.7 1.4 collective-permute-done.4
  251.2 0.5 collective-permute-done.3
  251.7 17.0 %all_to_all.31.grams = f32[32,8,128]{2,1,0:T(8,128)S(1)} all-to-all(f32[32,8,128]{2,1,0:T(8,128)S(1)} %broadcast_in_dim.7), channel_id=1, replica_groups=mesh['gx'=4,'gy'=32] {'gy'}, dimensions={0} | all-to-all | bytes 262144 | tf_op jit(solution)/shard_map/all_to_all | solution.py:728
  268.7 3.8 %last.1 = f32[32,12288]{1,0:T(8,128)} custom-call(f32[32,8,128]{2,1,0:T(8,128)S(1)} %all_to_all.31.grams, f32[32,12288]{1,0:T(8,128)S(1)} %get-tuple-element.34.image), custom_call_target="tpu_custom_call" | custom-call | flops 100000000 | bytes 4194304 | tf_op jit(solution)/shard_map/last/pallas_call | solution.py:707
  (12 shorter events, 0.8 us)
Async XLA Ops:
  0.7 0.7 copy-start
  1.3 0.7 copy-start.1
  9.6 124.1 %all-to-all-start = ((bf16[32,592,256]{2,1,0:T(8,128)(2,1)}), bf16[32,592,256]{2,1,0:T(8,128)(2,1)}, u32[]{:S(2)}, u32[]{:S(2)}) async-start(bf16[32,592,256]{2,1,0:T(8,128)(2,1)} %get-tuple-element.21), calls=%async_computation | async-start | bytes 19398656 | tf_op jit(solution)/shard_map/all_to_all | solution.py:728
  45.4 1.1 copy-start.2
  145.1 27.4 %all-to-all-start.1 = ((bf16[32,32,512]{2,1,0:T(8,128)(2,1)}), bf16[32,32,512]{2,1,0:T(8,128)(2,1)S(1)}, u32[]{:S(2)}, u32[]{:S(2)}) async-start(bf16[32,32,512]{2,1,0:T(8,128)(2,1)} %far_build.1), calls=%async_computation.1 | async-start | bytes 2097152 | tf_op jit(solution)/shard_map/all_to_all | solution.py:728
  174.5 5.1 %collective-permute-start.2 = (f32[8,128]{1,0:T(8,128)S(1)}, f32[8,128]{1,0:T(8,128)S(1)}, u32[]{:S(2)}, u32[]{:S(2)}) collective-permute-start(f32[8,128]{1,0:T(8,128)S(1)} %get-tuple-element.28), channel_id=1, source_target_pairs={{0,96},{32,64},{64,32},{96,0},{1,97},{33,65},{65,33},{97,1},{2,98}... | collective-permute-start | bytes 12296 | tf_op jit(solution)/shard_map/ppermute | solution.py:721
  178.6 4.0 %collective-permute-start.1 = (f32[8,128]{1,0:T(8,128)S(1)}, f32[8,128]{1,0:T(8,128)S(1)}, u32[]{:S(2)}, u32[]{:S(2)}) collective-permute-start(f32[8,128]{1,0:T(8,128)S(1)} %get-tuple-element.28), channel_id=1, source_target_pairs={{0,64},{32,96},{64,0},{96,32},{1,65},{33,97},{65,1},{97,33},{2,66}... | collective-permute-start | bytes 12296 | tf_op jit(solution)/shard_map/ppermute | solution.py:721
  179.3 3.3 %collective-permute-start = (f32[8,128]{1,0:T(8,128)S(1)}, f32[8,128]{1,0:T(8,128)S(1)}, u32[]{:S(2)}, u32[]{:S(2)}) collective-permute-start(f32[8,128]{1,0:T(8,128)S(1)} %get-tuple-element.28), channel_id=1, source_target_pairs={{0,32},{32,0},{64,96},{96,64},{1,33},{33,1},{65,97},{97,65},{2,34}... | collective-permute-start | bytes 12296 | tf_op jit(solution)/shard_map/ppermute | solution.py:721
  199.7 21.3 %all-to-all-start.3 = ((bf16[32,32,512]{2,1,0:T(8,128)(2,1)}), bf16[32,32,512]{2,1,0:T(8,128)(2,1)S(1)}, u32[]{:S(2)}, u32[]{:S(2)}) async-start(bf16[32,32,512]{2,1,0:T(8,128)(2,1)} %get-tuple-element.30), calls=%async_computation.3 | async-start | bytes 2097152 | tf_op jit(solution)/shard_map/all_to_all | solution.py:728
  221.0 22.3 %all-to-all-start.4 = ((bf16[32,32,512]{2,1,0:T(8,128)(2,1)}), bf16[32,32,512]{2,1,0:T(8,128)(2,1)}, u32[]{:S(2)}, u32[]{:S(2)}) async-start(bf16[32,32,512]{2,1,0:T(8,128)(2,1)} %far_back.1), calls=%async_computation.4 | async-start | bytes 2097152 | tf_op jit(solution)/shard_map/all_to_all | solution.py:728
  246.0 3.7 %collective-permute-start.5 = (f32[8,128]{1,0:T(8,128)S(1)}, f32[8,128]{1,0:T(8,128)S(1)}, u32[]{:S(2)}, u32[]{:S(2)}) collective-permute-start(f32[8,128]{1,0:T(8,128)S(1)} %get-tuple-element.33), channel_id=1, source_target_pairs={{0,96},{32,64},{64,32},{96,0},{1,97},{33,65},{65,33},{97,1},{2,98}... | collective-permute-start | bytes 12296 | tf_op jit(solution)/shard_map/ppermute | solution.py:721
  247.2 4.0 %collective-permute-start.4 = (f32[8,128]{1,0:T(8,128)S(1)}, f32[8,128]{1,0:T(8,128)S(1)}, u32[]{:S(2)}, u32[]{:S(2)}) collective-permute-start(f32[8,128]{1,0:T(8,128)S(1)} %get-tuple-element.33), channel_id=1, source_target_pairs={{0,64},{32,96},{64,0},{96,32},{1,65},{33,97},{65,1},{97,33},{2,66}... | collective-permute-start | bytes 12296 | tf_op jit(solution)/shard_map/ppermute | solution.py:721
  248.9 2.8 %collective-permute-start.3 = (f32[8,128]{1,0:T(8,128)S(1)}, f32[8,128]{1,0:T(8,128)S(1)}, u32[]{:S(2)}, u32[]{:S(2)}) collective-permute-start(f32[8,128]{1,0:T(8,128)S(1)} %get-tuple-element.33), channel_id=1, source_target_pairs={{0,32},{32,0},{64,96},{96,64},{1,33},{33,1},{65,97},{97,65},{2,34}... | collective-permute-start | bytes 12296 | tf_op jit(solution)/shard_map/ppermute | solution.py:721

commit v3 on v2

--- a/solution.py
+++ b/solution.py
@@ -10,7 +10,6 @@
 D = 256
 VECS = 32
 BLK = 512
-ITERS = 2
 HALF = BLK // 2
 EXTRA = 9
 
@@ -30,6 +29,8 @@
 NOTE_ROWS = 16
 PACK = 8
 NOTE = BLK + VEC_ROWS
+NOTE_BLOCK = (NOTE + 8, D // 2)
+LARGEST = 1e12
 SENT = NOTE + NOTE_ROWS
 
 
@@ -47,6 +48,46 @@
 
 def cost(flops, bytes_accessed):
     return pl.CostEstimate(flops=flops, bytes_accessed=bytes_accessed, transcendentals=0)
+
+
+def three_parts(values):
+    high = values.astype(jnp.bfloat16)
+    rest = values - high.astype(jnp.float32)
+    middle = rest.astype(jnp.bfloat16)
+    low = (rest - middle.astype(jnp.float32)).astype(jnp.bfloat16)
+    return high, middle, low
+
+
+def factor_parts(factor):
+    high, middle, low = three_parts(factor)
+    return jnp.concatenate([high, high, high, middle, middle, low], axis=1)
+
+
+def solved(factor, values):
+    high, middle, low = three_parts(values)
+    return dot_nn(factor, jnp.concatenate([high, middle, low, high, middle, high], axis=0))
+
+
+def product(left, right):
+    return solved(factor_parts(left), right)
+
+
+def products(values):
+    parts = jnp.concatenate(three_parts(values), axis=0)
+    return dot_nt(parts, parts)
+
+
+def sum_of_parts(total):
+    total = total[:VECS] + total[VECS : 2 * VECS] + total[2 * VECS :]
+    return total[:, :VECS] + total[:, VECS : 2 * VECS] + total[:, 2 * VECS :]
+
+
+def packed(gram):
+    return jnp.concatenate([gram[r : r + PACK] for r in range(0, VECS, PACK)], axis=1)
+
+
+def unpacked(gram):
+    return jnp.concatenate([gram[:, c : c + VECS] for c in range(0, gram.shape[1], VECS)], axis=0)
 
 
 def normalized(rows):
@@ -67,6 +108,7 @@
         row = pairs[0, k]
         col = pairs[1, k]
         far = col >= block_count
+        crossed = jnp.logical_not(far) & (row != col)
 
         @pl.when(far)
         def _():
@@ -75,18 +117,18 @@
             following[peer] = head[row]
             head[row] = peer
 
-        @pl.when(jnp.logical_not(far))
+        @pl.when(crossed)
         def _():
             table[LOCAL + local_count] = row * 64 + col
 
-        return local_count + jnp.where(far, 0, 1)
+        return local_count + jnp.where(crossed, 1, 0)
 
     table[LOCAL_COUNT] = lax.fori_loop(0, counts[0], note, 0)
 
 
 def prepare_kernel(
-    pairs, counts, requests, raw, start, send, rounded, table,
-    fresh, vecs, held, notes, head, following, load_sem, vec_sem, note_sem, send_sem,
+    counts, all_pairs, all_requests, raw, start, send, rounded, table,
+    pairs, requests, slot_sem, fresh, vecs, held, notes, head, following, load_sem, vec_sem, note_sem, send_sem,
 ):
     block_count = held.shape[0]
     peer_count = send.shape[0]
@@ -97,40 +139,66 @@
     def give(peer, b):
         return pltpu.make_async_copy(held.at[b], send.at[peer, pl.ds(0, NOTE), :], send_sem.at[peer])
 
-    load(0).start()
+    slot_loads = (
+        pltpu.make_async_copy(all_pairs, pairs, slot_sem.at[0]),
+        pltpu.make_async_copy(all_requests, requests, slot_sem.at[1]),
+    )
+    for slot_load in slot_loads:
+        slot_load.start()
     vec_load = pltpu.make_async_copy(start, vecs, vec_sem)
     vec_load.start()
+    for slot_load in slot_loads:
+        slot_load.wait()
+    note_slots(pairs, counts, table, head, following, block_count)
 
     def begin(b, _):
-        load(b).start()
-        return 0
-
-    lax.fori_loop(1, block_count, begin, 0)
-    note_slots(pairs, counts, table, head, following, block_count)
+        @pl.when(head[b] >= 0)
+        def _():
+            load(b).start()
+
+        return 0
+
+    lax.fori_loop(0, block_count, begin, 0)
+
+    vec_load.wait()
+    gram = jnp.zeros((VECS, VECS), jnp.float32)
+    for c in range(0, vecs.shape[1], CHUNK):
+        w = vecs[:, c : c + CHUNK]
+        rounded[:, c : c + CHUNK] = w.astype(jnp.bfloat16)
+        w = jnp.clip(w, -LARGEST, LARGEST).astype(jnp.bfloat16)
+        gram += dot_nt(w, w)
+    high, middle, low = three_parts(packed(gram))
 
     def write_note(peer, _):
-        block = requests[0, peer].astype(jnp.float32)
-        notes[peer] = jnp.full((NOTE_ROWS, D), block, jnp.float32).astype(jnp.bfloat16)
+        block = jnp.full(low.shape, requests[0, peer].astype(jnp.float32), jnp.float32)
+        notes[peer] = jnp.concatenate(
+            [
+                jnp.concatenate([high, middle], axis=1),
+                jnp.concatenate([low, block.astype(jnp.bfloat16)], axis=1),
+            ],
+            axis=0,
+        )
         return 0
 
     lax.fori_loop(0, peer_count, write_note, 0)
     note = pltpu.make_async_copy(notes, send.at[:, pl.ds(NOTE, NOTE_ROWS), :], note_sem)
     note.start()
-    vec_load.wait()
 
     def one(b, _):
-        load(b).wait()
-        held[b, 0:BLK, :] = normalized(fresh[b])
-        w = vecs[:, columns_of(b)].astype(jnp.bfloat16)
-        rounded[:, columns_of(b)] = w
-        held[b, BLK : BLK + VECS, :] = w[:, :HALF]
-        held[b, BLK + VECS : NOTE, :] = w[:, HALF:]
-
-        def emit(peer):
-            give(peer, b).start()
-            return following[peer]
-
-        lax.while_loop(lambda peer: peer >= 0, emit, head[b])
+        @pl.when(head[b] >= 0)
+        def _():
+            load(b).wait()
+            held[b, 0:BLK, :] = normalized(fresh[b])
+            w = rounded[:, columns_of(b)]
+            held[b, BLK : BLK + VECS, :] = w[:, :HALF]
+            held[b, BLK + VECS : NOTE, :] = w[:, HALF:]
+
+            def emit(peer):
+                give(peer, b).start()
+                return following[peer]
+
+            lax.while_loop(lambda peer: peer >= 0, emit, head[b])
+
         return 0
 
     lax.fori_loop(0, block_count, one, 0)
@@ -154,7 +222,7 @@
     lists = max(block_count, peer_count)
     return pl.pallas_call(
         prepare_kernel,
-        in_specs=[SMEM, SMEM, SMEM, HBM, HBM],
+        in_specs=[SMEM, HBM, HBM, HBM, HBM],
         out_specs=[HBM, VMEM, SMEM],
         out_shape=[
             pltpu.HBM((peer_count, SENT, D), jnp.bfloat16),
@@ -162,6 +230,9 @@
             jax.ShapeDtypeStruct((TABLE,), jnp.int32),
         ],
         scratch_shapes=[
+            pltpu.SMEM(pairs.shape, jnp.int32),
+            pltpu.SMEM(requests.shape, jnp.int32),
+            pltpu.SemaphoreType.DMA((2,)),
             pltpu.VMEM((block_count, BLK, D), jnp.bfloat16),
             pltpu.VMEM(start.shape, jnp.float32),
             pltpu.VMEM((block_count, NOTE, D), jnp.bfloat16),
@@ -176,7 +247,7 @@
         compiler_params=params(20),
         cost_estimate=cost(10**7, 24 * 2**20),
         name="prepare",
-    )(pairs, counts, requests, in_hbm(embeddings), in_hbm(start))
+    )(counts, in_hbm(pairs), in_hbm(requests), in_hbm(embeddings), in_hbm(start))
 
 
 def tile_of(left, right):
@@ -198,7 +269,7 @@
     block_count = units.shape[0]
     load = pltpu.make_async_copy(raw, fresh, unit_sem)
     load.start()
-    count = table[LOCAL_COUNT]
+    count = block_count + table[LOCAL_COUNT]
     done[0] = count
     total[...] = jnp.zeros_like(total)
     load.wait()
@@ -215,9 +286,9 @@
         return pltpu.make_async_copy(buffer.at[n % 2], tiles.at[n], sem.at[n % 2])
 
     def one(n, _):
-        code = table[LOCAL + n]
-        row = code // 64
-        col = code % 64
+        code = table[LOCAL + jnp.maximum(n - block_count, 0)]
+        row = jnp.where(n < block_count, n, code // 64)
+        col = jnp.where(n < block_count, n, code % 64)
 
         @pl.when(n >= 2)
         def _():
@@ -284,7 +355,9 @@
     return lax.fori_loop(0, wanted.shape[0], one, 0)
 
 
-def build_groups(count, active, wanted, units, far_rows, near, far, buffer, load_sem, use, save=None):
+def build_groups(
+    count, active, wanted, units, far_rows, near, far, buffer, load_sem, use, save=None, after_first=()
+):
     def loads(n):
         peer = active[n]
         return (
@@ -339,6 +412,9 @@
 
     for n in range(2 * GROUP):
         begin(n)
+        if n == GROUP - 1:
+            for load in after_first:
+                load.start()
     lax.fori_loop(0, (count + 2 * GROUP - 1) // (2 * GROUP), two_groups, 0)
     if save:
         for z in range(2 * GROUP):
@@ -359,8 +435,11 @@
     ]
 
 
-def far_build_kernel(wanted, units, far_rows, rounded, after, back, active, near, far, buffer, load_sem):
+def far_build_kernel(
+    wanted, units, far_rows, rounded, after, back, gram, active, near, far, buffer, load_sem, notes, note_sem
+):
     del after
+    load = pltpu.make_async_copy(far_rows.at[:, pl.ds(NOTE, NOTE_ROWS), :], notes, note_sem)
     count = note_active(wanted, active)
 
     def use(peers, live, group):
@@ -368,7 +447,11 @@
             vecs = rounded[:, columns_of(wanted[peer])]
             back[peer] = dot_nn(vecs, tile[...]).astype(jnp.bfloat16)
 
-    build_groups(count, active, wanted, units, far_rows, near, far, buffer, load_sem, use)
+    build_groups(count, active, wanted, units, far_rows, near, far, buffer, load_sem, use, after_first=[load])
+    load.wait()
+    total = jnp.sum(notes[...].astype(jnp.float32), axis=0)
+    half = D // 2
+    gram[...] = total[:PACK, :half] + total[:PACK, half:] + total[PACK:, :half]
 
 
 def far_build(wanted, units, far_rows, rounded, after):
@@ -376,9 +459,16 @@
     return pl.pallas_call(
         far_build_kernel,
         in_specs=[SMEM, HBM, HBM, VMEM, SMEM],
-        out_specs=VMEM,
-        out_shape=jax.ShapeDtypeStruct((peer_count, VECS, BLK), jnp.bfloat16),
-        scratch_shapes=build_scratch(peer_count),
+        out_specs=[VMEM, VMEM],
+        out_shape=[
+            jax.ShapeDtypeStruct((peer_count, VECS, BLK), jnp.bfloat16),
+            jax.ShapeDtypeStruct((PACK, VECS * VECS // PACK), jnp.float32),
+        ],
+        scratch_shapes=[
+            *build_scratch(peer_count),
+            pltpu.VMEM((peer_count, NOTE_ROWS, D), jnp.bfloat16),
+            pltpu.SemaphoreType.DMA,
+        ],
         compiler_params=params(28),
         cost_estimate=cost(32 * 2 * BLK * BLK * (D + 4 * VECS), 18 * 2**20),
         name="far_build",
@@ -478,7 +568,36 @@
     return jnp.where(live, vecs, jnp.zeros_like(vecs))
 
 
-def far_back_kernel(wanted, tiles, rounded, back, active, buffer, sem):
+def own_apply_kernel(tiles, rounded, total, done, buffer, sem):
+    count = rounded.shape[1] // BLK
+    done[0] = count
+
+    def use(held, live, group):
+        terms = [dot_nn(rounded[:, columns_of(n)], tile[...]) for n, tile in zip(held, group)]
+        for n, term in zip(held, terms):
+            total[:, columns_of(n)] = term
+
+    stream(count, lambda n: tiles.at[n], buffer, sem, use)
+
+
+def own_apply(tiles, rounded):
+    return pl.pallas_call(
+        own_apply_kernel,
+        in_specs=[HBM, VMEM],
+        out_specs=[VMEM, SMEM],
+        out_shape=[
+            jax.ShapeDtypeStruct(rounded.shape, jnp.float32),
+            jax.ShapeDtypeStruct((1,), jnp.int32),
+        ],
+        scratch_shapes=tile_scratch(),
+        compiler_params=params(10),
+        cost_estimate=cost(24 * 2 * BLK * BLK * 4 * VECS, 13 * 2**20),
+        name="own_apply",
+    )(in_hbm(tiles), rounded)
+
+
+def far_back_kernel(wanted, tiles, rounded, after, back, active, buffer, sem):
+    del after
     count = note_active(wanted, active)
 
     def use(held, live, group):
@@ -492,113 +611,64 @@
     stream(count, lambda n: tiles.at[active[n]], buffer, sem, use)
 
 
-def far_back(wanted, tiles, rounded):
+def far_back(wanted, tiles, rounded, after):
     peer_count = tiles.shape[0]
     return pl.pallas_call(
         far_back_kernel,
-        in_specs=[SMEM, HBM, VMEM],
+        in_specs=[SMEM, HBM, VMEM, SMEM],
         out_specs=VMEM,
         out_shape=jax.ShapeDtypeStruct((peer_count, VECS, BLK), jnp.bfloat16),
         scratch_shapes=[pltpu.SMEM((peer_count,), jnp.int32), *tile_scratch()],
         compiler_params=params(12),
         cost_estimate=cost(32 * 2 * BLK * BLK * 4 * VECS, 17 * 2**20),
         name="far_back",
-    )(wanted, in_hbm(tiles), rounded)
-
-
-def add_far(wanted, tiles, vecs_of, before, total, active, buffer, sem):
+    )(wanted, in_hbm(tiles), rounded, after)
+
+
+def rest_apply_kernel(
+    table, wanted, local_tiles, far_tiles, rounded, far_vecs, before, total, active, buffer, sem
+):
+    block_count = rounded.shape[1] // BLK
     count = note_active(wanted, active)
     total[...] = before[...]
 
-    def use(held, live, group):
+    def use_crossed(held, live, group):
+        codes = [table[LOCAL + n] for n in held]
+        pairs = [(code // 64, code % 64) for code in codes]
+        vecs = [[masked(alive, rounded[:, columns_of(b)]) for b in pair] for pair, alive in zip(pairs, live)]
+        to_col = [dot_nn(row_vecs, tile[...]) for (row_vecs, _), tile in zip(vecs, group)]
+        to_row = [dot_nt(col_vecs, tile[...]) for (_, col_vecs), tile in zip(vecs, group)]
+        for (row, col), row_term, col_term in zip(pairs, to_row, to_col):
+            total[:, columns_of(col)] += col_term
+            total[:, columns_of(row)] += row_term
+
+    def use_far(held, live, group):
         peers = [active[n] for n in held]
         terms = [
-            dot_nt(masked(alive, vecs_of(peer)), tile[...])
+            dot_nt(masked(alive, far_vecs[peer]), tile[...])
             for peer, alive, tile in zip(peers, live, group)
         ]
         for peer, term in zip(peers, terms):
             total[:, columns_of(wanted[peer])] += term
 
-    stream(count, lambda n: tiles.at[active[n]], buffer, sem, use)
-
-
-def far_next_kernel(wanted, tiles, far_vecs, before, total, active, buffer, sem):
-    add_far(wanted, tiles, lambda peer: far_vecs[peer], before, total, active, buffer, sem)
-
-
-def far_next(wanted, tiles, far_vecs, before):
-    peer_count = tiles.shape[0]
-    return pl.pallas_call(
-        far_next_kernel,
-        in_specs=[SMEM, HBM, VMEM, VMEM],
+    stream(table[LOCAL_COUNT], lambda n: local_tiles.at[block_count + n], buffer, sem, use_crossed)
+    stream(count, lambda n: far_tiles.at[active[n]], buffer, sem, use_far)
+
+
+def rest_apply(table, wanted, local_tiles, far_tiles, rounded, far_vecs, before):
+    return pl.pallas_call(
+        rest_apply_kernel,
+        in_specs=[SMEM, SMEM, HBM, HBM, VMEM, VMEM, VMEM],
         out_specs=VMEM,
         out_shape=jax.ShapeDtypeStruct(before.shape, jnp.float32),
-        scratch_shapes=[pltpu.SMEM((peer_count,), jnp.int32), *tile_scratch()],
-        compiler_params=params(14),
-        cost_estimate=cost(32 * 2 * BLK * BLK * 4 * VECS, 20 * 2**20),
-        name="far_next",
-    )(wanted, in_hbm(tiles), far_vecs, before)
-
-
-def local_apply_kernel(table, tiles, rounded, total, buffer, sem):
-    total[...] = jnp.zeros_like(total)
-
-    def use(held, live, group):
-        codes = [table[LOCAL + n] for n in held]
-        terms = [
-            dot_nn(masked(alive, rounded[:, columns_of(code // 64)]), tile[...])
-            for code, alive, tile in zip(codes, live, group)
-        ]
-        for code, term in zip(codes, terms):
-            total[:, columns_of(code % 64)] += term
-        for code, alive, tile in zip(codes, live, group):
-            row = code // 64
-            col = code % 64
-
-            @pl.when(alive & (row != col))
-            def _(row=row, col=col, tile=tile):
-                total[:, columns_of(row)] += dot_nt(rounded[:, columns_of(col)], tile[...])
-
-    stream(table[LOCAL_COUNT], lambda n: tiles.at[n], buffer, sem, use)
-
-
-def local_apply(table, tiles, rounded):
-    return pl.pallas_call(
-        local_apply_kernel,
-        in_specs=[SMEM, HBM, VMEM],
-        out_specs=VMEM,
-        out_shape=jax.ShapeDtypeStruct(rounded.shape, jnp.float32),
-        scratch_shapes=tile_scratch(),
+        scratch_shapes=[pltpu.SMEM(wanted.shape, jnp.int32), *tile_scratch()],
         compiler_params=params(12),
-        cost_estimate=cost(33 * 2 * BLK * BLK * 8 * VECS, 18 * 2**20),
-        name="local_apply",
-    )(table, in_hbm(tiles), rounded)
-
-
-def three_parts(values):
-    high = values.astype(jnp.bfloat16)
-    rest = values - high.astype(jnp.float32)
-    middle = rest.astype(jnp.bfloat16)
-    low = (rest - middle.astype(jnp.float32)).astype(jnp.bfloat16)
-    return high, middle, low
-
-
-def factor_parts(factor):
-    high, middle, low = three_parts(factor)
-    return jnp.concatenate([high, high, high, middle, middle, low], axis=1)
-
-
-def solved(factor, values):
-    high, middle, low = three_parts(values)
-    return dot_nn(factor, jnp.concatenate([high, middle, low, high, middle, high], axis=0))
-
-
-def products(values):
-    parts = jnp.concatenate(three_parts(values), axis=0)
-    return dot_nt(parts, parts)
-
-
-def assemble_kernel(table, own, returned, image, gram):
+        cost_estimate=cost(40 * 2 * BLK * BLK * 4 * VECS, 24 * 2**20),
+        name="rest_apply",
+    )(table, wanted, in_hbm(local_tiles), in_hbm(far_tiles), rounded, far_vecs, before)
+
+
+def add_returned(table, own, returned, image):
     image[...] = own[...]
 
     def add(peer, _):
@@ -611,12 +681,63 @@
         return 0
 
     lax.fori_loop(0, returned.shape[0], add, 0)
+
+
+def gram_kernel(image, gram):
     total = jnp.zeros((3 * VECS, 3 * VECS), jnp.float32)
     for c in range(0, image.shape[1], CHUNK):
         total += products(image[:, c : c + CHUNK])
-    total = total[:VECS] + total[VECS : 2 * VECS] + total[2 * VECS :]
-    total = total[:, :VECS] + total[:, VECS : 2 * VECS] + total[:, 2 * VECS :]
-    gram[...] = jnp.concatenate([total[r : r + PACK] for r in range(0, VECS, PACK)], axis=1)
+    gram[...] = packed(sum_of_parts(total))
+
+
+def forward_kernel(table, own, returned, inverse, rounded, gram, send, image, out, sem):
+    factor = factor_parts(inverse[...])
+    add_returned(table, own, returned, image)
+    for c in range(0, image.shape[1], CHUNK):
+        based = solved(factor, image[:, c : c + CHUNK])
+        image[:, c : c + CHUNK] = based
+        rounded[:, c : c + CHUNK] = based.astype(jnp.bfloat16)
+
+    def give(peer, _):
+        row = table[FAR_ROW + peer]
+
+        @pl.when(row >= 0)
+        def _():
+            out[peer] = rounded[:, columns_of(row)]
+
+        return 0
+
+    lax.fori_loop(0, out.shape[0], give, 0)
+    save = pltpu.make_async_copy(out, send, sem)
+    save.start()
+    gram_kernel(image, gram)
+    save.wait()
+
+
+def forward(table, own, returned, inverse):
+    return pl.pallas_call(
+        forward_kernel,
+        in_specs=[SMEM, VMEM, VMEM, VMEM],
+        out_specs=[VMEM, VMEM, HBM],
+        out_shape=[
+            jax.ShapeDtypeStruct(own.shape, jnp.bfloat16),
+            jax.ShapeDtypeStruct((PACK, VECS * VECS // PACK), jnp.float32),
+            pltpu.HBM(returned.shape, jnp.bfloat16),
+        ],
+        scratch_shapes=[
+            pltpu.VMEM(own.shape, jnp.float32),
+            pltpu.VMEM(returned.shape, jnp.bfloat16),
+            pltpu.SemaphoreType.DMA,
+        ],
+        compiler_params=params(12),
+        cost_estimate=cost(10**8, 5 * 2**20),
+        name="forward",
+    )(table, own, returned, inverse)
+
+
+def assemble_kernel(table, own, returned, image, gram):
+    add_returned(table, own, returned, image)
+    gram_kernel(image, gram)
 
 
 def assemble(table, own, returned):
@@ -659,46 +780,43 @@
     return work[:, VECS:]
 
 
-def summed_inverse(rows_all, grams):
-    packed = jnp.sum(grams[...], axis=0)
-    gram = jnp.concatenate([packed[:, c : c + VECS] for c in range(0, packed.shape[1], VECS)], axis=0)
-    return factor_parts(inverse_factor(gram * (1.0 / rows_all)))
-
-
-def middle_kernel(rows_all, table, grams, image, rounded, out):
-    factor = summed_inverse(rows_all, grams)
-    for c in range(0, image.shape[1], CHUNK):
-        rounded[:, c : c + CHUNK] = solved(factor, image[:, c : c + CHUNK]).astype(jnp.bfloat16)
-
-    def give(peer, _):
-        row = table[FAR_ROW + peer]
-
-        @pl.when(row >= 0)
-        def _():
-            out[peer] = rounded[:, columns_of(row)]
-
-        return 0
-
-    lax.fori_loop(0, out.shape[0], give, 0)
-
-
-def middle(rows_all, table, grams, image):
-    return pl.pallas_call(
-        functools.partial(middle_kernel, rows_all),
-        in_specs=[SMEM, VMEM, VMEM],
-        out_specs=[VMEM, VMEM],
-        out_shape=[
-            jax.ShapeDtypeStruct(image.shape, jnp.bfloat16),
-            jax.ShapeDtypeStruct((grams.shape[0], VECS, BLK), jnp.bfloat16),
-        ],
-        compiler_params=params(10),
-        cost_estimate=cost(10**8, 4 * 2**20),
-        name="middle",
-    )(table, grams, image)
+def identity():
+    rows = lax.broadcasted_iota(jnp.int32, (VECS, VECS), 0)
+    lanes = lax.broadcasted_iota(jnp.int32, (VECS, VECS), 1)
+    return jnp.where(rows == lanes, 1.0, 0.0).astype(jnp.float32)
+
+
+def basis_kernel(rows_all, gram, inverse):
+    eye = identity()
+    matrix = unpacked(gram[...]) * (1.0 / rows_all)
+    factor = inverse_factor(matrix * (1.0 + 1e-3 * eye))
+    usable = jnp.sum(jnp.abs(factor)) < 1e30
+    inverse[...] = jnp.where(usable, factor, eye)
+
+
+def basis(rows_all, gram):
+    return pl.pallas_call(
+        functools.partial(basis_kernel, rows_all),
+        in_specs=[VMEM],
+        out_specs=VMEM,
+        out_shape=jax.ShapeDtypeStruct((VECS, VECS), jnp.float32),
+        compiler_params=params(4),
+        cost_estimate=cost(10**6, 10**4),
+        name="basis",
+    )(gram)
 
 
 def last_kernel(rows_all, grams, image, vectors):
-    factor = summed_inverse(rows_all, grams)
+    both = jnp.sum(grams[...], axis=0) * (1.0 / rows_all)
+    first = inverse_factor(unpacked(both[:PACK]))
+    turned = lax.dot_general(
+        product(first, unpacked(both[PACK:])),
+        first,
+        NT,
+        precision=lax.Precision.HIGHEST,
+        preferred_element_type=jnp.float32,
+    )
+    factor = factor_parts(product(inverse_factor(turned), first))
     for c in range(0, image.shape[1], CHUNK):
         vectors[:, c : c + CHUNK] = solved(factor, image[:, c : c + CHUNK])
 
@@ -715,12 +833,16 @@
     )(grams, image)
 
 
-def all_parts(gram):
+def sum_over_gx(gram):
     size = lax.axis_size("gx")
     arrived = [
         lax.ppermute(gram, "gx", [(i, i ^ mask) for i in range(size)]) for mask in range(1, size)
     ]
-    gram = sum(arrived, gram)
+    return sum(arrived, gram)
+
+
+def all_parts(gram):
+    gram = sum_over_gx(gram)
     return exchange(jnp.broadcast_to(gram, (lax.axis_size("gy"), *gram.shape)))
 
 
@@ -733,19 +855,19 @@
     send_rows, rounded, table = prepare(embeddings, start, requests, pairs[0].T, counts)
     far_rows = exchange(send_rows)
     units, own, local_tiles, done = local_build(table, embeddings, rounded)
-    wanted = far_rows[:, NOTE, 0].astype(jnp.int32)
-    returned = exchange(far_build(wanted, units, far_rows, rounded, done))
+    wanted = far_rows[:, NOTE_BLOCK[0], NOTE_BLOCK[1]].astype(jnp.int32)
+    back, start_gram = far_build(wanted, units, far_rows, rounded, done)
+    returned = exchange(back)
+    inverse = basis(rows_all, sum_over_gx(start_gram))
     own, far_tiles = far_first(wanted, units, far_rows, own)
-    for _ in range(ITERS - 1):
-        image, gram = assemble(table, own, returned)
-        rounded, send_vecs = middle(rows_all, table, all_parts(gram), image)
-        far_vecs = exchange(send_vecs)
-        back = far_back(wanted, far_tiles, rounded)
-        own = local_apply(table, local_tiles, rounded)
-        returned = exchange(back)
-        own = far_next(wanted, far_tiles, far_vecs, own)
-    image, gram = assemble(table, own, returned)
-    return last(rows_all, all_parts(gram), image)
+    rounded, first_gram, send_vecs = forward(table, own, returned, inverse)
+    far_vecs = exchange(send_vecs)
+    own, done = own_apply(local_tiles, rounded)
+    returned = exchange(far_back(wanted, far_tiles, rounded, done))
+    own = rest_apply(table, wanted, local_tiles, far_tiles, rounded, far_vecs, own)
+    image, next_gram = assemble(table, own, returned)
+    grams = all_parts(jnp.concatenate([first_gram, next_gram], axis=0))
+    return last(rows_all, grams, image)
 
 
 def solution(mesh):

time: 274 us -> 257 us (0.938)
  blocking collectives: 29.4 us -> 14.9 us
  starting transfers between devices: 35.3 us -> 44.9 us
  waiting for transfers between devices: 108 us -> 99.9 us
    all_to_all x2 -> x1, blocking collectives: 29.4 us -> 14.9 us  [exchange(): return lax.all_to_all(blocks, 'gy', split_axis=0, concat_axis=0, tiled=True)]
    all_to_all x4, starting transfers between devices: 27.2 us -> 34.9 us  [exchange(): return lax.all_to_all(blocks, 'gy', split_axis=0, concat_axis=0, tiled=True)]
    all_to_all x4, waiting for transfers between devices: 102 us -> 96.6 us  [exchange(): return lax.all_to_all(blocks, 'gy', split_axis=0, concat_axis=0, tiled=True)]
    pallas_call x5 -> x6, Pallas kernels: 37.3 us -> 36.9 us  [the longest x1 9.82 us: rest_apply(): pl.pallas_call(rest_apply_kernel, in_specs=[SMEM, SMEM, HBM, HBM, VMEM, V...]
  transfers between devices with their start and end apart: 10 -> 10, of which waited for: 8 -> 5; matrix products, arithmetic and copies ran while one was open for 0% -> 0% of each run, Pallas kernels for 24% -> 25%
where the time goes in v3:
time: 257 us; the launch traced here: 258 us
  waiting for transfers between devices  99.9 us (39%)
  Pallas kernels  93 us (36%)
  starting transfers between devices  44.9 us (17%)
  blocking collectives  14.9 us (6%)
  local copies, waits for them, and re-layouts  2.57 us (1%)
    all_to_all x4, waiting for transfers between devices, exchange(): return lax.all_to_all(blocks, 'gy', split_axis=0, concat_axis=0, tiled=True)  96.6 us
    all_to_all x4, starting transfers between devices, exchange(): return lax.all_to_all(blocks, 'gy', split_axis=0, concat_axis=0, tiled=True)  34.9 us
    pallas_call x1, Pallas kernels, local_build(): pl.pallas_call(local_build_kernel, in_specs=[SMEM, HBM, VMEM], out_specs=...  26.8 us
    all_to_all x1, blocking collectives, exchange(): return lax.all_to_all(blocks, 'gy', split_axis=0, concat_axis=0, tiled=True)  14.9 us
    pallas_call x1, Pallas kernels, far_first(): pl.pallas_call(far_first_kernel, in_specs=[SMEM, HBM, HBM, HBM], out_spec...  11.4 us
    ppermute x6, starting transfers between devices, sum_over_gx(): lax.ppermute(gram, 'gx', [(i, i ^ mask) for i in range(size)])  9.98 us
    pallas_call x1, Pallas kernels, rest_apply(): pl.pallas_call(rest_apply_kernel, in_specs=[SMEM, SMEM, HBM, HBM, VMEM, V...  9.82 us
    pallas_call x1, Pallas kernels, far_build(): pl.pallas_call(far_build_kernel, in_specs=[SMEM, HBM, HBM, VMEM, SMEM], o...  9.29 us
  transfers between devices with their start and end apart: 10, of which 5 were waited for; matrix products, arithmetic and copies ran while one was open for 0% of the time, Pallas kernels for 25%

profile of v3, /device:TPU:1, one launch (start us, length us, event | category | flops | bytes accessed | tf_op | source)
XLA Modules:
  0.0 257.7 jit_solution(1480822197766546357)
XLA Ops:
  0.7 6.5 %prepare.1 = (bf16[32,592,256]{2,1,0:T(8,128)(2,1)}, bf16[32,12288]{1,0:T(8,128)(2,1)S(1)}, s32[128]{0:T(128)S(1)}) custom-call(s32[1]{0:T(128)S(6)} %copy.7.counts, s32[2,64]{1,0:T(2,128)} %bitcast.3, s32[1,32]{1,0:T(1,128)} %all_requests.1, bf16[12288,256]{1,0:T(8,128)(2,1)} %raw.3, f32[32,12288]{1,0:T(8,128)} %start.1), custom_call_target="tpu_custom_call" | custom-call | flops 10000000 | bytes 25165824 | tf_op jit(solution)/shard_map/prepare/pallas_call | solution.py:223
  7.2 9.3 %all-to-all-start = ((bf16[32,592,256]{2,1,0:T(8,128)(2,1)}), bf16[32,592,256]{2,1,0:T(8,128)(2,1)}, u32[]{:S(2)}, u32[]{:S(2)}) async-start(bf16[32,592,256]{2,1,0:T(8,128)(2,1)} %get-tuple-element.24), calls=%async_computation | async-start | bytes 19398656 | tf_op jit(solution)/shard_map/all_to_all | solution.py:850
  16.4 26.8 %local_build.1 = (bf16[24,512,256]{2,1,0:T(8,128)(2,1)}, f32[32,12288]{1,0:T(8,128)S(1)}, bf16[33,512,512]{2,1,0:T(8,128)(2,1)}, s32[1]{0:T(128)}) custom-call(s32[128]{0:T(128)S(1)} %get-tuple-element.23.table, bf16[12288,256]{1,0:T(8,128)(2,1)} %raw.3, bf16[32,12288]{1,0:T(8,128)(2,1)S(1)} %get-tuple-element.25.rounded), custom_call_target="tpu_custom_call" | custom-call | flops 8858370048 | bytes 33554432 | tf_op jit(solution)/shard_map/local_build/pallas_call | solution.py:323
  43.3 0.0 copy-start.2
  43.3 1.1 copy-done.2
  44.4 87.6 %all-to-all-done.far_rows = bf16[32,592,256]{2,1,0:T(8,128)(2,1)} async-done(((bf16[32,592,256]{2,1,0:T(8,128)(2,1)}), bf16[32,592,256]{2,1,0:T(8,128)(2,1)}, u32[]{:S(2)}, u32[]{:S(2)}) %all-to-all-start) | async-done | bytes 9699360 | tf_op jit(solution)/shard_map/all_to_all | solution.py:850
  132.1 1.5 fusion.wanted
  133.6 9.3 %far_build.1 = (bf16[32,32,512]{2,1,0:T(8,128)(2,1)}, f32[8,128]{1,0:T(8,128)S(1)}) custom-call(s32[32]{0:T(128)S(1)} %fusion.wanted, bf16[24,512,256]{2,1,0:T(8,128)(2,1)} %get-tuple-element.26.units, bf16[32,592,256]{2,1,0:T(8,128)(2,1)} %all-to-all-done.far_rows, bf16[32,12288]{1,0:T(8,128)(2,1)S(1)} %get-tuple-element.25.rounded, s32[1]{0:T(128)} %get-tuple-element.29.after), custom_call_target="tpu_custom_call" | custom-call | flops 6442450944 | bytes 18874368 | tf_op jit(solution)/shard_map/far_build/pallas_call | solution.py:459
  142.8 11.9 %all-to-all-start.1 = ((bf16[32,32,512]{2,1,0:T(8,128)(2,1)}), bf16[32,32,512]{2,1,0:T(8,128)(2,1)S(1)}, u32[]{:S(2)}, u32[]{:S(2)}) async-start(bf16[32,32,512]{2,1,0:T(8,128)(2,1)} %get-tuple-element.30), calls=%async_computation.1 | async-start | bytes 2097152 | tf_op jit(solution)/shard_map/all_to_all | solution.py:850
  154.7 2.1 collective-permute-start.2
  156.8 2.3 collective-permute-start.1
  159.1 11.4 %far_first.1 = (f32[32,12288]{1,0:T(8,128)S(1)}, bf16[32,512,512]{2,1,0:T(8,128)(2,1)}) custom-call(s32[32]{0:T(128)S(1)} %fusion.wanted, bf16[24,512,256]{2,1,0:T(8,128)(2,1)} %get-tuple-element.26.units, bf16[32,592,256]{2,1,0:T(8,128)(2,1)} %all-to-all-done.far_rows, f32[32,12288]{1,0:T(8,128)} %copy-done.2), custom_call_target="tpu_custom_call" | custom-call | flops 6442450944 | bytes 37748736 | tf_op jit(solution)/shard_map/far_first/pallas_call | solution.py:507
  170.5 0.0 collective-permute-done.1
  170.5 1.8 basis.1.inverse
  172.4 4.6 %forward.1 = (bf16[32,12288]{1,0:T(8,128)(2,1)S(1)}, f32[8,128]{1,0:T(8,128)S(1)}, bf16[32,32,512]{2,1,0:T(8,128)(2,1)}) custom-call(s32[128]{0:T(128)S(1)} %get-tuple-element.23.table, f32[32,12288]{1,0:T(8,128)S(1)} %get-tuple-element.28.own, bf16[32,32,512]{2,1,0:T(8,128)(2,1)S(1)} %all-to-all-done.1.returned, f32[32,32]{1,0:T(8,128)S(1)} %basis.1.inverse), custom_call_target="tpu_custom_call" | custom-call | flops 100000000 | bytes 5242880 | tf_op jit(solution)/shard_map/forward/pallas_call | solution.py:718
  177.0 8.5 %all-to-all-start.2 = ((bf16[32,32,512]{2,1,0:T(8,128)(2,1)}), bf16[32,32,512]{2,1,0:T(8,128)(2,1)S(1)}, u32[]{:S(2)}, u32[]{:S(2)}) async-start(bf16[32,32,512]{2,1,0:T(8,128)(2,1)} %get-tuple-element.36), calls=%async_computation.2 | async-start | bytes 2097152 | tf_op jit(solution)/shard_map/all_to_all | solution.py:850
  185.5 7.0 %own_apply.1 = (f32[32,12288]{1,0:T(8,128)S(1)}, s32[1]{0:T(128)}) custom-call(bf16[33,512,512]{2,1,0:T(8,128)(2,1)} %get-tuple-element.33.tiles.local_tiles, bf16[32,12288]{1,0:T(8,128)(2,1)S(1)} %get-tuple-element.35.rounded), custom_call_target="tpu_custom_call" | custom-call | flops 1610612736 | bytes 13631488 | tf_op jit(solution)/shard_map/own_apply/pallas_call | solution.py:584
  192.5 0.0 copy-start
  192.5 7.1 %far_back.1 = bf16[32,32,512]{2,1,0:T(8,128)(2,1)} custom-call(s32[32]{0:T(128)S(1)} %fusion.wanted, bf16[32,512,512]{2,1,0:T(8,128)(2,1)} %get-tuple-element.34.far_tiles.tiles, bf16[32,12288]{1,0:T(8,128)(2,1)S(1)} %get-tuple-element.35.rounded, s32[1]{0:T(128)} %get-tuple-element.38.after), custom_call_target="tpu_custom_call" | custom-call | flops 2147483648 | bytes 17825792 | tf_op jit(solution)/shard_map/far_back/pallas_call | solution.py:616
  199.6 3.0 %all-to-all-done.2.far_vecs = bf16[32,32,512]{2,1,0:T(8,128)(2,1)S(1)} async-done(((bf16[32,32,512]{2,1,0:T(8,128)(2,1)}), bf16[32,32,512]{2,1,0:T(8,128)(2,1)S(1)}, u32[]{:S(2)}, u32[]{:S(2)}) %all-to-all-start.2) | async-done | bytes 1048608 | tf_op jit(solution)/shard_map/all_to_all | solution.py:850
  202.6 5.3 %all-to-all-start.3 = ((bf16[32,32,512]{2,1,0:T(8,128)(2,1)}), bf16[32,32,512]{2,1,0:T(8,128)(2,1)}, u32[]{:S(2)}, u32[]{:S(2)}) async-start(bf16[32,32,512]{2,1,0:T(8,128)(2,1)} %far_back.1), calls=%async_computation.3 | async-start | bytes 2097152 | tf_op jit(solution)/shard_map/all_to_all | solution.py:850
  208.0 0.0 copy-start.1
  208.0 1.4 copy-done.1
  209.4 9.8 %rest_apply.1.own = f32[32,12288]{1,0:T(8,128)S(1)} custom-call(s32[128]{0:T(128)S(1)} %get-tuple-element.23.table, s32[32]{0:T(128)S(1)} %fusion.wanted, bf16[33,512,512]{2,1,0:T(8,128)(2,1)} %get-tuple-element.33.tiles.local_tiles, bf16[32,512,512]{2,1,0:T(8,128)(2,1)} %get-tuple-element.34.far_tiles.tiles, ...), custom_call_target="tpu_custom_call" | custom-call | flops 2684354560 | bytes 25165824 | tf_op jit(solution)/shard_map/rest_apply/pallas_call | solution.py:659
  219.2 6.0 %all-to-all-done.3.returned = bf16[32,32,512]{2,1,0:T(8,128)(2,1)} async-done(((bf16[32,32,512]{2,1,0:T(8,128)(2,1)}), bf16[32,32,512]{2,1,0:T(8,128)(2,1)}, u32[]{:S(2)}, u32[]{:S(2)}) %all-to-all-start.3) | async-done | bytes 1048608 | tf_op jit(solution)/shard_map/all_to_all | solution.py:850
  225.2 2.7 %assemble.1 = (f32[32,12288]{1,0:T(8,128)S(1)}, f32[8,128]{1,0:T(8,128)S(1)}) custom-call(s32[128]{0:T(128)S(1)} %get-tuple-element.23.table, f32[32,12288]{1,0:T(8,128)S(1)} %rest_apply.1.own, bf16[32,32,512]{2,1,0:T(8,128)(2,1)} %all-to-all-done.3.returned), custom_call_target="tpu_custom_call" | custom-call | flops 100000000 | bytes 5242880 | tf_op jit(solution)/shard_map/assemble/pallas_call | solution.py:744
  228.0 4.9 %collective-permute-start.5 = (f32[16,128]{1,0:T(8,128)S(1)}, f32[16,128]{1,0:T(8,128)S(1)}, u32[]{:S(2)}, u32[]{:S(2)}) collective-permute-start(f32[16,128]{1,0:T(8,128)S(1)} %constant_dynamic-update-slice_fusion), channel_id=1, source_target_pairs={{0,96},{32,64},{64,32},{96,0},{1,97},{33,65},{65,33},{97,1},{2,98}... | collective-permute-start | bytes 24584 | tf_op jit(solution)/shard_map/ppermute | solution.py:839
  232.9 0.7 collective-permute-start.3
  233.5 0.4 collective-permute-done.5
  233.9 3.0 %collective-permute-done.4 = f32[16,128]{1,0:T(8,128)S(1)} collective-permute-done((f32[16,128]{1,0:T(8,128)S(1)}, f32[16,128]{1,0:T(8,128)S(1)}, u32[]{:S(2)}, u32[]{:S(2)}) %collective-permute-start.4) | collective-permute-done | bytes 8224 | tf_op jit(solution)/shard_map/ppermute | solution.py:839
  236.9 14.9 %all_to_all.25.grams = f32[32,16,128]{2,1,0:T(8,128)S(1)} all-to-all(f32[32,16,128]{2,1,0:T(8,128)S(1)} %broadcast_in_dim.3), channel_id=1, replica_groups=mesh['gx'=4,'gy'=32] {'gy'}, dimensions={0} | all-to-all | bytes 524288 | tf_op jit(solution)/shard_map/all_to_all | solution.py:850
  251.8 5.9 %last.1 = f32[32,12288]{1,0:T(8,128)} custom-call(f32[32,16,128]{2,1,0:T(8,128)S(1)} %all_to_all.25.grams, f32[32,12288]{1,0:T(8,128)S(1)} %get-tuple-element.40.image), custom_call_target="tpu_custom_call" | custom-call | flops 100000000 | bytes 4194304 | tf_op jit(solution)/shard_map/last/pallas_call | solution.py:825
  (12 shorter events, 0.1 us)
Async XLA Ops:
  7.2 124.9 %all-to-all-start = ((bf16[32,592,256]{2,1,0:T(8,128)(2,1)}), bf16[32,592,256]{2,1,0:T(8,128)(2,1)}, u32[]{:S(2)}, u32[]{:S(2)}) async-start(bf16[32,592,256]{2,1,0:T(8,128)(2,1)} %get-tuple-element.24), calls=%async_computation | async-start | bytes 19398656 | tf_op jit(solution)/shard_map/all_to_all | solution.py:850
  43.3 1.1 copy-start.2
  142.8 29.5 %all-to-all-start.1 = ((bf16[32,32,512]{2,1,0:T(8,128)(2,1)}), bf16[32,32,512]{2,1,0:T(8,128)(2,1)S(1)}, u32[]{:S(2)}, u32[]{:S(2)}) async-start(bf16[32,32,512]{2,1,0:T(8,128)(2,1)} %get-tuple-element.30), calls=%async_computation.1 | async-start | bytes 2097152 | tf_op jit(solution)/shard_map/all_to_all | solution.py:850
  154.7 15.8 %collective-permute-start.2 = (f32[8,128]{1,0:T(8,128)S(1)}, f32[8,128]{1,0:T(8,128)S(1)}, u32[]{:S(2)}, u32[]{:S(2)}) collective-permute-start(f32[8,128]{1,0:T(8,128)S(1)} %get-tuple-element.31), channel_id=1, source_target_pairs={{0,96},{32,64},{64,32},{96,0},{1,97},{33,65},{65,33},{97,1},{2,98}... | collective-permute-start | bytes 12296 | tf_op jit(solution)/shard_map/ppermute | solution.py:839
  156.8 13.7 %collective-permute-start.1 = (f32[8,128]{1,0:T(8,128)S(1)}, f32[8,128]{1,0:T(8,128)S(1)}, u32[]{:S(2)}, u32[]{:S(2)}) collective-permute-start(f32[8,128]{1,0:T(8,128)S(1)} %get-tuple-element.31), channel_id=1, source_target_pairs={{0,64},{32,96},{64,0},{96,32},{1,65},{33,97},{65,1},{97,33},{2,66}... | collective-permute-start | bytes 12296 | tf_op jit(solution)/shard_map/ppermute | solution.py:839
  159.1 11.4 %collective-permute-start = (f32[8,128]{1,0:T(8,128)S(1)}, f32[8,128]{1,0:T(8,128)S(1)}, u32[]{:S(2)}, u32[]{:S(2)}) collective-permute-start(f32[8,128]{1,0:T(8,128)S(1)} %get-tuple-element.31), channel_id=1, source_target_pairs={{0,32},{32,0},{64,96},{96,64},{1,33},{33,1},{65,97},{97,65},{2,34}... | collective-permute-start | bytes 12296 | tf_op jit(solution)/shard_map/ppermute | solution.py:839
  177.0 25.7 %all-to-all-start.2 = ((bf16[32,32,512]{2,1,0:T(8,128)(2,1)}), bf16[32,32,512]{2,1,0:T(8,128)(2,1)S(1)}, u32[]{:S(2)}, u32[]{:S(2)}) async-start(bf16[32,32,512]{2,1,0:T(8,128)(2,1)} %get-tuple-element.36), calls=%async_computation.2 | async-start | bytes 2097152 | tf_op jit(solution)/shard_map/all_to_all | solution.py:850
  192.5 7.1 %copy-start = (f32[32,12288]{1,0:T(8,128)}, f32[32,12288]{1,0:T(8,128)S(1)}, u32[]{:S(2)}) copy-start(f32[32,12288]{1,0:T(8,128)S(1)} %get-tuple-element.37.before) | copy-start | bytes 4718596
  202.6 22.6 %all-to-all-start.3 = ((bf16[32,32,512]{2,1,0:T(8,128)(2,1)}), bf16[32,32,512]{2,1,0:T(8,128)(2,1)}, u32[]{:S(2)}, u32[]{:S(2)}) async-start(bf16[32,32,512]{2,1,0:T(8,128)(2,1)} %far_back.1), calls=%async_computation.3 | async-start | bytes 2097152 | tf_op jit(solution)/shard_map/all_to_all | solution.py:850
  208.0 1.4 copy-start.1
  228.0 6.0 %collective-permute-start.5 = (f32[16,128]{1,0:T(8,128)S(1)}, f32[16,128]{1,0:T(8,128)S(1)}, u32[]{:S(2)}, u32[]{:S(2)}) collective-permute-start(f32[16,128]{1,0:T(8,128)S(1)} %constant_dynamic-update-slice_fusion), channel_id=1, source_target_pairs={{0,96},{32,64},{64,32},{96,0},{1,97},{33,65},{65,33},{97,1},{2,98}... | collective-permute-start | bytes 24584 | tf_op jit(solution)/shard_map/ppermute | solution.py:839
  232.9 4.0 %collective-permute-start.4 = (f32[16,128]{1,0:T(8,128)S(1)}, f32[16,128]{1,0:T(8,128)S(1)}, u32[]{:S(2)}, u32[]{:S(2)}) collective-permute-start(f32[16,128]{1,0:T(8,128)S(1)} %constant_dynamic-update-slice_fusion), channel_id=1, source_target_pairs={{0,64},{32,96},{64,0},{96,32},{1,65},{33,97},{65,1},{97,33},{2,66}... | collective-permute-start | bytes 24584 | tf_op jit(solution)/shard_map/ppermute | solution.py:839
  232.9 4.0 %collective-permute-start.3 = (f32[16,128]{1,0:T(8,128)S(1)}, f32[16,128]{1,0:T(8,128)S(1)}, u32[]{:S(2)}, u32[]{:S(2)}) collective-permute-start(f32[16,128]{1,0:T(8,128)S(1)} %constant_dynamic-update-slice_fusion), channel_id=1, source_target_pairs={{0,32},{32,0},{64,96},{96,64},{1,33},{33,1},{65,97},{97,65},{2,34}... | collective-permute-start | bytes 24584 | tf_op jit(solution)/shard_map/ppermute | solution.py:839

commit v4 on v3

--- a/solution.py
+++ b/solution.py
@@ -10,7 +10,6 @@
 D = 256
 VECS = 32
 BLK = 512
-HALF = BLK // 2
 EXTRA = 9
 
 FAR_ROW = 0
@@ -24,11 +23,11 @@
 VMEM = pl.BlockSpec(memory_space=pltpu.VMEM)
 HBM = pl.BlockSpec(memory_space=pltpu.HBM)
 GROUP = 4
+BUFFERS = 16
 CHUNK = 2048
-VEC_ROWS = 2 * VECS
 NOTE_ROWS = 16
 PACK = 8
-NOTE = BLK + VEC_ROWS
+NOTE = BLK
 NOTE_BLOCK = (NOTE + 8, D // 2)
 LARGEST = 1e12
 SENT = NOTE + NOTE_ROWS
@@ -188,10 +187,7 @@
         @pl.when(head[b] >= 0)
         def _():
             load(b).wait()
-            held[b, 0:BLK, :] = normalized(fresh[b])
-            w = rounded[:, columns_of(b)]
-            held[b, BLK : BLK + VECS, :] = w[:, :HALF]
-            held[b, BLK + VECS : NOTE, :] = w[:, HALF:]
+            held[b] = normalized(fresh[b])
 
             def emit(peer):
                 give(peer, b).start()
@@ -264,7 +260,8 @@
 
 
 def local_build_kernel(
-    table, raw, rounded, all_units, total, tiles, done, fresh, units, buffer, sem, unit_sem, keep_sem
+    table, raw, rounded, all_units, out, tiles, send, done,
+    fresh, units, total, given, buffer, sem, unit_sem, keep_sem, save_sem, send_sem,
 ):
     block_count = units.shape[0]
     load = pltpu.make_async_copy(raw, fresh, unit_sem)
@@ -272,6 +269,9 @@
     count = block_count + table[LOCAL_COUNT]
     done[0] = count
     total[...] = jnp.zeros_like(total)
+    spread(table, rounded, given)
+    give = pltpu.make_async_copy(given, send, send_sem)
+    give.start()
     load.wait()
 
     def normalize(b, _):
@@ -315,26 +315,36 @@
     def _():
         copy(count - 1).wait()
 
+    save = pltpu.make_async_copy(total, out, save_sem)
+    save.start()
+    save.wait()
     keep.wait()
-
-
-def local_build(table, raw, rounded):
+    give.wait()
+
+
+def local_build(table, raw, rounded, peer_count):
     block_count = raw.shape[0] // BLK
+    given = (peer_count, VECS, BLK)
     return pl.pallas_call(
         local_build_kernel,
         in_specs=[SMEM, HBM, VMEM],
-        out_specs=[HBM, VMEM, HBM, SMEM],
+        out_specs=[HBM, HBM, HBM, HBM, SMEM],
         out_shape=[
             pltpu.HBM((block_count, BLK, D), jnp.bfloat16),
-            jax.ShapeDtypeStruct(rounded.shape, jnp.float32),
+            pltpu.HBM(rounded.shape, jnp.float32),
             pltpu.HBM((block_count + EXTRA, BLK, BLK), jnp.bfloat16),
+            pltpu.HBM(given, jnp.bfloat16),
             jax.ShapeDtypeStruct((1,), jnp.int32),
         ],
         scratch_shapes=[
             pltpu.VMEM(raw.shape, jnp.bfloat16),
             pltpu.VMEM((block_count, BLK, D), jnp.bfloat16),
+            pltpu.VMEM(rounded.shape, jnp.float32),
+            pltpu.VMEM(given, jnp.bfloat16),
             pltpu.VMEM((2, BLK, BLK), jnp.bfloat16),
             pltpu.SemaphoreType.DMA((2,)),
+            pltpu.SemaphoreType.DMA,
+            pltpu.SemaphoreType.DMA,
             pltpu.SemaphoreType.DMA,
             pltpu.SemaphoreType.DMA,
         ],
@@ -344,6 +354,19 @@
     )(table, in_hbm(raw), rounded)
 
 
+def spread(table, source, out):
+    def give(peer, _):
+        row = table[FAR_ROW + peer]
+
+        @pl.when(row >= 0)
+        def _():
+            out[peer] = source[:, columns_of(row)]
+
+        return 0
+
+    lax.fori_loop(0, out.shape[0], give, 0)
+
+
 def note_active(wanted, active):
     def one(peer, count):
         @pl.when(wanted[peer] >= 0)
@@ -355,15 +378,25 @@
     return lax.fori_loop(0, wanted.shape[0], one, 0)
 
 
-def build_groups(
-    count, active, wanted, units, far_rows, near, far, buffer, load_sem, use, save=None, after_first=()
+def tile_loads(wanted, active, units, far_rows, near, far, load_sem, n):
+    peer = active[n]
+    return (
+        pltpu.make_async_copy(far_rows.at[peer, pl.ds(0, BLK), :], far.at[n], load_sem.at[0, n]),
+        pltpu.make_async_copy(units.at[wanted[peer]], near.at[n], load_sem.at[1, n]),
+    )
+
+
+def far_build_kernel(
+    wanted, units, far_rows, rounded, after, back, gram, tiles,
+    active, near, far, buffer, load_sem, save_sem, notes, note_sem,
 ):
-    def loads(n):
-        peer = active[n]
-        return (
-            pltpu.make_async_copy(far_rows.at[peer, pl.ds(0, BLK), :], far.at[n], load_sem.at[0, n]),
-            pltpu.make_async_copy(units.at[wanted[peer]], near.at[n], load_sem.at[1, n]),
-        )
+    del after
+    note_load = pltpu.make_async_copy(far_rows.at[:, pl.ds(NOTE, NOTE_ROWS), :], notes, note_sem)
+    count = note_active(wanted, active)
+    loads = functools.partial(tile_loads, wanted, active, units, far_rows, near, far, load_sem)
+
+    def save(n, z):
+        return pltpu.make_async_copy(buffer.at[z], tiles.at[active[n]], save_sem.at[z])
 
     def begin(n):
         @pl.when(n < count)
@@ -381,24 +414,23 @@
                 for load in loads(n):
                     load.wait()
 
-        if save:
-
-            @pl.when(first >= 2 * GROUP)
-            def _():
-                for z in range(GROUP):
-                    save(first - 2 * GROUP + z, base + z).wait()
+        @pl.when(first >= 2 * GROUP)
+        def _():
+            for z in range(GROUP):
+                save(first - 2 * GROUP + z, base + z).wait()
 
         held = [jnp.minimum(first + z, count - 1) for z in range(GROUP)]
-        live = [first + z < count for z in range(GROUP)]
+        peers = [active[n] for n in held]
         for z, n in enumerate(held):
             buffer[base + z] = tile_of(near[n], far[n])
-        use([active[n] for n in held], live, [buffer.at[base + z] for z in range(GROUP)])
-        if save:
-            for z in range(GROUP):
-
-                @pl.when(live[z])
-                def _(n=first + z, z=z):
-                    save(n, base + z).start()
+        for z, peer in enumerate(peers):
+            vecs = rounded[:, columns_of(wanted[peer])]
+            back[peer] = dot_nn(vecs, buffer[base + z]).astype(jnp.bfloat16)
+        for z in range(GROUP):
+
+            @pl.when(first + z < count)
+            def _(n=first + z, z=z):
+                save(n, base + z).start()
 
     def two_groups(i, _):
         first = 2 * GROUP * i
@@ -413,45 +445,18 @@
     for n in range(2 * GROUP):
         begin(n)
         if n == GROUP - 1:
-            for load in after_first:
-                load.start()
+            note_load.start()
     lax.fori_loop(0, (count + 2 * GROUP - 1) // (2 * GROUP), two_groups, 0)
-    if save:
-        for z in range(2 * GROUP):
-            newest = z + 2 * GROUP * ((count - 1 - z) // (2 * GROUP))
-
-            @pl.when((count > z) & (newest // GROUP * GROUP + 2 * GROUP >= count))
-            def _(n=newest, z=z):
-                save(n, z).wait()
-
-
-def build_scratch(peer_count):
-    return [
-        pltpu.SMEM((peer_count,), jnp.int32),
-        pltpu.VMEM((peer_count, BLK, D), jnp.bfloat16),
-        pltpu.VMEM((peer_count, BLK, D), jnp.bfloat16),
-        pltpu.VMEM((2 * GROUP, BLK, BLK), jnp.bfloat16),
-        pltpu.SemaphoreType.DMA((2, peer_count)),
-    ]
-
-
-def far_build_kernel(
-    wanted, units, far_rows, rounded, after, back, gram, active, near, far, buffer, load_sem, notes, note_sem
-):
-    del after
-    load = pltpu.make_async_copy(far_rows.at[:, pl.ds(NOTE, NOTE_ROWS), :], notes, note_sem)
-    count = note_active(wanted, active)
-
-    def use(peers, live, group):
-        for peer, tile in zip(peers, group):
-            vecs = rounded[:, columns_of(wanted[peer])]
-            back[peer] = dot_nn(vecs, tile[...]).astype(jnp.bfloat16)
-
-    build_groups(count, active, wanted, units, far_rows, near, far, buffer, load_sem, use, after_first=[load])
-    load.wait()
+    note_load.wait()
     total = jnp.sum(notes[...].astype(jnp.float32), axis=0)
     half = D // 2
     gram[...] = total[:PACK, :half] + total[:PACK, half:] + total[PACK:, :half]
+    for z in range(2 * GROUP):
+        newest = z + 2 * GROUP * ((count - 1 - z) // (2 * GROUP))
+
+        @pl.when((count > z) & (newest // GROUP * GROUP + 2 * GROUP >= count))
+        def _(n=newest, z=z):
+            save(n, z).wait()
 
 
 def far_build(wanted, units, far_rows, rounded, after):
@@ -459,90 +464,44 @@
     return pl.pallas_call(
         far_build_kernel,
         in_specs=[SMEM, HBM, HBM, VMEM, SMEM],
-        out_specs=[VMEM, VMEM],
+        out_specs=[VMEM, VMEM, HBM],
         out_shape=[
             jax.ShapeDtypeStruct((peer_count, VECS, BLK), jnp.bfloat16),
             jax.ShapeDtypeStruct((PACK, VECS * VECS // PACK), jnp.float32),
+            pltpu.HBM((peer_count, BLK, BLK), jnp.bfloat16),
         ],
         scratch_shapes=[
-            *build_scratch(peer_count),
+            pltpu.SMEM((peer_count,), jnp.int32),
+            pltpu.VMEM((peer_count, BLK, D), jnp.bfloat16),
+            pltpu.VMEM((peer_count, BLK, D), jnp.bfloat16),
+            pltpu.VMEM((2 * GROUP, BLK, BLK), jnp.bfloat16),
+            pltpu.SemaphoreType.DMA((2, peer_count)),
+            pltpu.SemaphoreType.DMA((2 * GROUP,)),
             pltpu.VMEM((peer_count, NOTE_ROWS, D), jnp.bfloat16),
             pltpu.SemaphoreType.DMA,
         ],
         compiler_params=params(28),
-        cost_estimate=cost(32 * 2 * BLK * BLK * (D + 4 * VECS), 18 * 2**20),
+        cost_estimate=cost(32 * 2 * BLK * BLK * (D + 4 * VECS), 34 * 2**20),
         name="far_build",
     )(wanted, in_hbm(units), in_hbm(far_rows), rounded, after)
 
 
-def far_first_kernel(
-    wanted, units, far_rows, before, total, tiles,
-    active, near, far, buffer, load_sem, vecs, save_sem, vec_sem, before_sem,
-):
-    count = note_active(wanted, active)
-    vec_load = pltpu.make_async_copy(far_rows.at[:, pl.ds(BLK, VEC_ROWS), :], vecs, vec_sem)
-    before_load = pltpu.make_async_copy(before, total, before_sem)
-    vec_load.start()
-    before_load.start()
-
-    def save(n, z):
-        return pltpu.make_async_copy(buffer.at[z], tiles.at[active[n]], save_sem.at[z])
-
-    def use(peers, live, group):
-        terms = []
-        for peer, alive, tile in zip(peers, live, group):
-            both = vecs[peer]
-            both = masked(alive, jnp.concatenate([both[:VECS], both[VECS:]], axis=1))
-            terms.append(dot_nt(both, tile[...]))
-        for peer, term in zip(peers, terms):
-            total[:, columns_of(wanted[peer])] += term
-
-    vec_load.wait()
-    before_load.wait()
-    build_groups(count, active, wanted, units, far_rows, near, far, buffer, load_sem, use, save)
-
-
-def far_first(wanted, units, far_rows, before):
-    peer_count = far_rows.shape[0]
-    return pl.pallas_call(
-        far_first_kernel,
-        in_specs=[SMEM, HBM, HBM, HBM],
-        out_specs=[VMEM, HBM],
-        out_shape=[
-            jax.ShapeDtypeStruct(before.shape, jnp.float32),
-            pltpu.HBM((peer_count, BLK, BLK), jnp.bfloat16),
-        ],
-        scratch_shapes=[
-            *build_scratch(peer_count),
-            pltpu.VMEM((peer_count, VEC_ROWS, D), jnp.bfloat16),
-            pltpu.SemaphoreType.DMA((2 * GROUP,)),
-            pltpu.SemaphoreType.DMA,
-            pltpu.SemaphoreType.DMA,
-        ],
-        compiler_params=params(28),
-        cost_estimate=cost(32 * 2 * BLK * BLK * (D + 4 * VECS), 36 * 2**20),
-        name="far_first",
-    )(wanted, in_hbm(units), in_hbm(far_rows), in_hbm(before))
-
-
 def stream(count, source_of, buffer, sem, use):
-    slots = 2 * GROUP
-
     def load(n):
-        return pltpu.make_async_copy(source_of(n), buffer.at[n % slots], sem.at[n % slots])
+        return pltpu.make_async_copy(source_of(n), buffer.at[n % BUFFERS], sem.at[n % BUFFERS])
 
     def begin(n):
         @pl.when(n < count)
         def _():
             load(n).start()
 
-    for n in range(GROUP):
+    for n in range(BUFFERS - GROUP):
         begin(n)
 
     def group(g, _):
         first = g * GROUP
         for z in range(GROUP):
-            begin(first + GROUP + z)
+            begin(first + BUFFERS - GROUP + z)
         for z in range(GROUP):
 
             @pl.when(first + z < count)
@@ -551,7 +510,7 @@
 
         held = [jnp.minimum(first + z, count - 1) for z in range(GROUP)]
         live = [first + z < count for z in range(GROUP)]
-        use(held, live, [buffer.at[n % slots] for n in held])
+        use(held, live, [buffer.at[n % BUFFERS] for n in held])
         return 0
 
     lax.fori_loop(0, (count + GROUP - 1) // GROUP, group, 0)
@@ -559,8 +518,8 @@
 
 def tile_scratch():
     return [
-        pltpu.VMEM((2 * GROUP, BLK, BLK), jnp.bfloat16),
-        pltpu.SemaphoreType.DMA((2 * GROUP,)),
+        pltpu.VMEM((BUFFERS, BLK, BLK), jnp.bfloat16),
+        pltpu.SemaphoreType.DMA((BUFFERS,)),
     ]
 
 
@@ -568,7 +527,7 @@
     return jnp.where(live, vecs, jnp.zeros_like(vecs))
 
 
-def own_apply_kernel(tiles, rounded, total, done, buffer, sem):
+def own_apply_kernel(tiles, rounded, out, done, total, buffer, sem, save_sem):
     count = rounded.shape[1] // BLK
     done[0] = count
 
@@ -578,19 +537,26 @@
             total[:, columns_of(n)] = term
 
     stream(count, lambda n: tiles.at[n], buffer, sem, use)
+    save = pltpu.make_async_copy(total, out, save_sem)
+    save.start()
+    save.wait()
 
 
 def own_apply(tiles, rounded):
     return pl.pallas_call(
         own_apply_kernel,
         in_specs=[HBM, VMEM],
-        out_specs=[VMEM, SMEM],
+        out_specs=[HBM, SMEM],
         out_shape=[
-            jax.ShapeDtypeStruct(rounded.shape, jnp.float32),
+            pltpu.HBM(rounded.shape, jnp.float32),
             jax.ShapeDtypeStruct((1,), jnp.int32),
         ],
-        scratch_shapes=tile_scratch(),
-        compiler_params=params(10),
+        scratch_shapes=[
+            pltpu.VMEM(rounded.shape, jnp.float32),
+            *tile_scratch(),
+            pltpu.SemaphoreType.DMA,
+        ],
+        compiler_params=params(16),
         cost_estimate=cost(24 * 2 * BLK * BLK * 4 * VECS, 13 * 2**20),
         name="own_apply",
     )(in_hbm(tiles), rounded)
@@ -619,18 +585,58 @@
         out_specs=VMEM,
         out_shape=jax.ShapeDtypeStruct((peer_count, VECS, BLK), jnp.bfloat16),
         scratch_shapes=[pltpu.SMEM((peer_count,), jnp.int32), *tile_scratch()],
-        compiler_params=params(12),
+        compiler_params=params(16),
         cost_estimate=cost(32 * 2 * BLK * BLK * 4 * VECS, 17 * 2**20),
         name="far_back",
     )(wanted, in_hbm(tiles), rounded, after)
 
 
+def add_far(wanted, tiles, far_vecs, total, active, buffer, sem):
+    count = note_active(wanted, active)
+
+    def use(held, live, group):
+        peers = [active[n] for n in held]
+        terms = [
+            dot_nt(masked(alive, far_vecs[peer]), tile[...])
+            for peer, alive, tile in zip(peers, live, group)
+        ]
+        for peer, term in zip(peers, terms):
+            total[:, columns_of(wanted[peer])] += term
+
+    stream(count, lambda n: tiles.at[active[n]], buffer, sem, use)
+
+
+def far_first_kernel(wanted, tiles, far_vecs, before, total, active, buffer, sem, before_sem):
+    before_load = pltpu.make_async_copy(before, total, before_sem)
+    before_load.start()
+    before_load.wait()
+    add_far(wanted, tiles, far_vecs, total, active, buffer, sem)
+
+
+def far_first(wanted, tiles, far_vecs, before):
+    return pl.pallas_call(
+        far_first_kernel,
+        in_specs=[SMEM, HBM, VMEM, HBM],
+        out_specs=VMEM,
+        out_shape=jax.ShapeDtypeStruct(before.shape, jnp.float32),
+        scratch_shapes=[
+            pltpu.SMEM(wanted.shape, jnp.int32),
+            *tile_scratch(),
+            pltpu.SemaphoreType.DMA,
+        ],
+        compiler_params=params(16),
+        cost_estimate=cost(32 * 2 * BLK * BLK * 4 * VECS, 20 * 2**20),
+        name="far_first",
+    )(wanted, in_hbm(tiles), far_vecs, in_hbm(before))
+
+
 def rest_apply_kernel(
-    table, wanted, local_tiles, far_tiles, rounded, far_vecs, before, total, active, buffer, sem
+    table, wanted, local_tiles, far_tiles, rounded, far_vecs, before, total, active, buffer, sem, before_sem
 ):
     block_count = rounded.shape[1] // BLK
-    count = note_active(wanted, active)
-    total[...] = before[...]
+    before_load = pltpu.make_async_copy(before, total, before_sem)
+    before_load.start()
+    before_load.wait()
 
     def use_crossed(held, live, group):
         codes = [table[LOCAL + n] for n in held]
@@ -642,30 +648,21 @@
             total[:, columns_of(col)] += col_term
             total[:, columns_of(row)] += row_term
 
-    def use_far(held, live, group):
-        peers = [active[n] for n in held]
-        terms = [
-            dot_nt(masked(alive, far_vecs[peer]), tile[...])
-            for peer, alive, tile in zip(peers, live, group)
-        ]
-        for peer, term in zip(peers, terms):
-            total[:, columns_of(wanted[peer])] += term
-
     stream(table[LOCAL_COUNT], lambda n: local_tiles.at[block_count + n], buffer, sem, use_crossed)
-    stream(count, lambda n: far_tiles.at[active[n]], buffer, sem, use_far)
+    add_far(wanted, far_tiles, far_vecs, total, active, buffer, sem)
 
 
 def rest_apply(table, wanted, local_tiles, far_tiles, rounded, far_vecs, before):
     return pl.pallas_call(
         rest_apply_kernel,
-        in_specs=[SMEM, SMEM, HBM, HBM, VMEM, VMEM, VMEM],
+        in_specs=[SMEM, SMEM, HBM, HBM, VMEM, VMEM, HBM],
         out_specs=VMEM,
         out_shape=jax.ShapeDtypeStruct(before.shape, jnp.float32),
-        scratch_shapes=[pltpu.SMEM(wanted.shape, jnp.int32), *tile_scratch()],
-        compiler_params=params(12),
+        scratch_shapes=[pltpu.SMEM(wanted.shape, jnp.int32), *tile_scratch(), pltpu.SemaphoreType.DMA],
+        compiler_params=params(16),
         cost_estimate=cost(40 * 2 * BLK * BLK * 4 * VECS, 24 * 2**20),
         name="rest_apply",
-    )(table, wanted, in_hbm(local_tiles), in_hbm(far_tiles), rounded, far_vecs, before)
+    )(table, wanted, in_hbm(local_tiles), in_hbm(far_tiles), rounded, far_vecs, in_hbm(before))
 
 
 def add_returned(table, own, returned, image):
@@ -698,16 +695,7 @@
         image[:, c : c + CHUNK] = based
         rounded[:, c : c + CHUNK] = based.astype(jnp.bfloat16)
 
-    def give(peer, _):
-        row = table[FAR_ROW + peer]
-
-        @pl.when(row >= 0)
-        def _():
-            out[peer] = rounded[:, columns_of(row)]
-
-        return 0
-
-    lax.fori_loop(0, out.shape[0], give, 0)
+    spread(table, rounded, out)
     save = pltpu.make_async_copy(out, send, sem)
     save.start()
     gram_kernel(image, gram)
@@ -854,12 +842,13 @@
     rows_all = embeddings.shape[0] * lax.axis_size("gx") * lax.axis_size("gy")
     send_rows, rounded, table = prepare(embeddings, start, requests, pairs[0].T, counts)
     far_rows = exchange(send_rows)
-    units, own, local_tiles, done = local_build(table, embeddings, rounded)
+    units, own, local_tiles, send_vecs, done = local_build(table, embeddings, rounded, requests.shape[1])
+    far_vecs = exchange(send_vecs)
     wanted = far_rows[:, NOTE_BLOCK[0], NOTE_BLOCK[1]].astype(jnp.int32)
-    back, start_gram = far_build(wanted, units, far_rows, rounded, done)
+    back, start_gram, far_tiles = far_build(wanted, units, far_rows, rounded, done)
     returned = exchange(back)
     inverse = basis(rows_all, sum_over_gx(start_gram))
-    own, far_tiles = far_first(wanted, units, far_rows, own)
+    own = far_first(wanted, far_tiles, far_vecs, own)
     rounded, first_gram, send_vecs = forward(table, own, returned, inverse)
     far_vecs = exchange(send_vecs)
     own, done = own_apply(local_tiles, rounded)

time: 257 us -> 248 us (0.965)
  waiting for transfers between devices: 99.9 us -> 91.6 us
  Pallas kernels: 93 us -> 98.6 us
  starting transfers between devices: 44.9 us -> 40.9 us
    all_to_all x4 -> x5, waiting for transfers between devices: 96.6 us -> 88.2 us  [exchange(): return lax.all_to_all(blocks, 'gy', split_axis=0, concat_axis=0, tiled=True)]
    pallas_call x1, Pallas kernels: 9.29 us -> 12.7 us  [far_build(): pl.pallas_call(far_build_kernel, in_specs=[SMEM, HBM, HBM, VMEM, SMEM], o...]
    pallas_call x2, Pallas kernels: 18.4 us -> 15.1 us  [the longest x1 8.04 us: far_first(): pl.pallas_call(far_first_kernel, in_specs=[SMEM, HBM, VMEM, HBM], out_spe...]
    all_to_all x4 -> x5, starting transfers between devices: 34.9 us -> 33.2 us  [exchange(): return lax.all_to_all(blocks, 'gy', split_axis=0, concat_axis=0, tiled=True)]
  transfers between devices with their start and end apart: 10 -> 11, of which waited for: 5 -> 7; matrix products, arithmetic and copies ran while one was open for 0% -> 1% of each run, Pallas kernels for 25% -> 32%
where the time goes in v4:
time: 248 us; the launch traced here: 247 us
  Pallas kernels  98.6 us (40%)
  waiting for transfers between devices  91.6 us (37%)
  starting transfers between devices  40.9 us (16%)
  blocking collectives  13.7 us (6%)
    all_to_all x5, waiting for transfers between devices, exchange(): return lax.all_to_all(blocks, 'gy', split_axis=0, concat_axis=0, tiled=True)  88.2 us
    all_to_all x5, starting transfers between devices, exchange(): return lax.all_to_all(blocks, 'gy', split_axis=0, concat_axis=0, tiled=True)  33.2 us
    pallas_call x1, Pallas kernels, local_build(): pl.pallas_call(local_build_kernel, in_specs=[SMEM, HBM, VMEM], out_specs=...  29.2 us
    all_to_all x1, blocking collectives, exchange(): return lax.all_to_all(blocks, 'gy', split_axis=0, concat_axis=0, tiled=True)  13.7 us
    pallas_call x1, Pallas kernels, far_build(): pl.pallas_call(far_build_kernel, in_specs=[SMEM, HBM, HBM, VMEM, SMEM], o...  12.7 us
    pallas_call x1, Pallas kernels, rest_apply(): pl.pallas_call(rest_apply_kernel, in_specs=[SMEM, SMEM, HBM, HBM, VMEM, V...  12 us
    pallas_call x1, Pallas kernels, far_first(): pl.pallas_call(far_first_kernel, in_specs=[SMEM, HBM, VMEM, HBM], out_spe...  8.04 us
    ppermute x6, starting transfers between devices, sum_over_gx(): lax.ppermute(gram, 'gx', [(i, i ^ mask) for i in range(size)])  7.71 us
  transfers between devices with their start and end apart: 11, of which 7 were waited for; matrix products, arithmetic and copies ran while one was open for 1% of the time, Pallas kernels for 32%

profile of v4, /device:TPU:1, one launch (start us, length us, event | category | flops | bytes accessed | tf_op | source)
XLA Modules:
  0.0 247.2 jit_solution(3470814500151851023)
XLA Ops:
  0.7 6.3 %prepare.1 = (bf16[32,528,256]{2,1,0:T(8,128)(2,1)}, bf16[32,12288]{1,0:T(8,128)(2,1)S(1)}, s32[128]{0:T(128)S(1)}) custom-call(s32[1]{0:T(128)S(6)} %copy.7.counts, s32[2,64]{1,0:T(2,128)} %bitcast.3, s32[1,32]{1,0:T(1,128)} %all_requests.1, bf16[12288,256]{1,0:T(8,128)(2,1)} %raw.3, f32[32,12288]{1,0:T(8,128)} %start.1), custom_call_target="tpu_custom_call" | custom-call | flops 10000000 | bytes 25165824 | tf_op jit(solution)/shard_map/prepare/pallas_call | solution.py:219
  6.9 9.7 %all-to-all-start = ((bf16[32,528,256]{2,1,0:T(8,128)(2,1)}), bf16[32,528,256]{2,1,0:T(8,128)(2,1)}, u32[]{:S(2)}, u32[]{:S(2)}) async-start(bf16[32,528,256]{2,1,0:T(8,128)(2,1)} %get-tuple-element.24), calls=%async_computation | async-start | bytes 17301504 | tf_op jit(solution)/shard_map/all_to_all | solution.py:838
  16.6 29.2 %local_build.1 = (bf16[24,512,256]{2,1,0:T(8,128)(2,1)}, f32[32,12288]{1,0:T(8,128)}, bf16[33,512,512]{2,1,0:T(8,128)(2,1)}, bf16[32,32,512]{2,1,0:T(8,128)(2,1)}, s32[1]{0:T(128)}) custom-call(s32[128]{0:T(128)S(1)} %get-tuple-element.23.table, bf16[12288,256]{1,0:T(8,128)(2,1)} %raw.3, bf16[32,12288]{1,0:T(8,128)(2,1)S(1)} %get-tuple-element.25.rounded), custom_call_target="tpu_custom_call" | custom-call | flops 8858370048 | bytes 33554432 | tf_op jit(solution)/shard_map/local_build/pallas_call | solution.py:328
  45.8 73.7 %all-to-all-done.far_rows = bf16[32,528,256]{2,1,0:T(8,128)(2,1)} async-done(((bf16[32,528,256]{2,1,0:T(8,128)(2,1)}), bf16[32,528,256]{2,1,0:T(8,128)(2,1)}, u32[]{:S(2)}, u32[]{:S(2)}) %all-to-all-start) | async-done | bytes 8650784 | tf_op jit(solution)/shard_map/all_to_all | solution.py:838
  119.5 10.3 %all-to-all-start.1 = ((bf16[32,32,512]{2,1,0:T(8,128)(2,1)}), bf16[32,32,512]{2,1,0:T(8,128)(2,1)S(1)}, u32[]{:S(2)}, u32[]{:S(2)}) async-start(bf16[32,32,512]{2,1,0:T(8,128)(2,1)} %get-tuple-element.29), calls=%async_computation.1 | async-start | bytes 2097152 | tf_op jit(solution)/shard_map/all_to_all | solution.py:838
  129.8 1.5 fusion.wanted
  131.3 12.7 %far_build.1 = (bf16[32,32,512]{2,1,0:T(8,128)(2,1)}, f32[8,128]{1,0:T(8,128)S(1)}, bf16[32,512,512]{2,1,0:T(8,128)(2,1)}) custom-call(s32[32]{0:T(128)S(1)} %fusion.wanted, bf16[24,512,256]{2,1,0:T(8,128)(2,1)} %get-tuple-element.26.units, bf16[32,528,256]{2,1,0:T(8,128)(2,1)} %all-to-all-done.far_rows, bf16[32,12288]{1,0:T(8,128)(2,1)S(1)} %get-tuple-element.25.rounded, ...), custom_call_target="tpu_custom_call" | custom-call | flops 6442450944 | bytes 35651584 | tf_op jit(solution)/shard_map/far_build/pallas_call | solution.py:464
  144.0 3.1 %all-to-all-done.1.far_vecs = bf16[32,32,512]{2,1,0:T(8,128)(2,1)S(1)} async-done(((bf16[32,32,512]{2,1,0:T(8,128)(2,1)}), bf16[32,32,512]{2,1,0:T(8,128)(2,1)S(1)}, u32[]{:S(2)}, u32[]{:S(2)}) %all-to-all-start.1) | async-done | bytes 1048608 | tf_op jit(solution)/shard_map/all_to_all | solution.py:838
  147.1 4.6 %all-to-all-start.2 = ((bf16[32,32,512]{2,1,0:T(8,128)(2,1)}), bf16[32,32,512]{2,1,0:T(8,128)(2,1)}, u32[]{:S(2)}, u32[]{:S(2)}) async-start(bf16[32,32,512]{2,1,0:T(8,128)(2,1)} %get-tuple-element.31), calls=%async_computation.2 | async-start | bytes 2097152 | tf_op jit(solution)/shard_map/all_to_all | solution.py:838
  151.7 3.2 %collective-permute-start.2 = (f32[8,128]{1,0:T(8,128)S(1)}, f32[8,128]{1,0:T(8,128)S(1)}, u32[]{:S(2)}, u32[]{:S(2)}) collective-permute-start(f32[8,128]{1,0:T(8,128)S(1)} %get-tuple-element.32), channel_id=1, source_target_pairs={{0,96},{32,64},{64,32},{96,0},{1,97},{33,65},{65,33},{97,1},{2,98}... | collective-permute-start | bytes 12296 | tf_op jit(solution)/shard_map/ppermute | solution.py:827
  154.9 0.2 collective-permute-start.1
  155.1 0.5 collective-permute-start
  155.6 8.0 %far_first.1.own = f32[32,12288]{1,0:T(8,128)S(1)} custom-call(s32[32]{0:T(128)S(1)} %fusion.wanted, bf16[32,512,512]{2,1,0:T(8,128)(2,1)} %get-tuple-element.28.tiles.far_tiles, bf16[32,32,512]{2,1,0:T(8,128)(2,1)S(1)} %all-to-all-done.1.far_vecs, f32[32,12288]{1,0:T(8,128)} %get-tuple-element.30.before), custom_call_target="tpu_custom_call" | custom-call | flops 2147483648 | bytes 20971520 | tf_op jit(solution)/shard_map/far_first/pallas_call | solution.py:617
  163.6 0.0 collective-permute-done.2
  163.7 1.8 basis.1.inverse
  165.5 3.6 %all-to-all-done.2.returned = bf16[32,32,512]{2,1,0:T(8,128)(2,1)} async-done(((bf16[32,32,512]{2,1,0:T(8,128)(2,1)}), bf16[32,32,512]{2,1,0:T(8,128)(2,1)}, u32[]{:S(2)}, u32[]{:S(2)}) %all-to-all-start.2) | async-done | bytes 1048608 | tf_op jit(solution)/shard_map/all_to_all | solution.py:838
  169.1 5.2 %forward.1 = (bf16[32,12288]{1,0:T(8,128)(2,1)S(1)}, f32[8,128]{1,0:T(8,128)S(1)}, bf16[32,32,512]{2,1,0:T(8,128)(2,1)}) custom-call(s32[128]{0:T(128)S(1)} %get-tuple-element.23.table, f32[32,12288]{1,0:T(8,128)S(1)} %far_first.1.own, bf16[32,32,512]{2,1,0:T(8,128)(2,1)} %all-to-all-done.2.returned, f32[32,32]{1,0:T(8,128)S(1)} %basis.1.inverse), custom_call_target="tpu_custom_call" | custom-call | flops 100000000 | bytes 5242880 | tf_op jit(solution)/shard_map/forward/pallas_call | solution.py:706
  174.3 4.0 %all-to-all-start.3 = ((bf16[32,32,512]{2,1,0:T(8,128)(2,1)}), bf16[32,32,512]{2,1,0:T(8,128)(2,1)S(1)}, u32[]{:S(2)}, u32[]{:S(2)}) async-start(bf16[32,32,512]{2,1,0:T(8,128)(2,1)} %get-tuple-element.36), calls=%async_computation.3 | async-start | bytes 2097152 | tf_op jit(solution)/shard_map/all_to_all | solution.py:838
  178.3 7.0 %own_apply.1 = (f32[32,12288]{1,0:T(8,128)}, s32[1]{0:T(128)}) custom-call(bf16[33,512,512]{2,1,0:T(8,128)(2,1)} %get-tuple-element.34.tiles.local_tiles, bf16[32,12288]{1,0:T(8,128)(2,1)S(1)} %get-tuple-element.35.rounded), custom_call_target="tpu_custom_call" | custom-call | flops 1610612736 | bytes 13631488 | tf_op jit(solution)/shard_map/own_apply/pallas_call | solution.py:546
  185.4 7.7 %far_back.1 = bf16[32,32,512]{2,1,0:T(8,128)(2,1)} custom-call(s32[32]{0:T(128)S(1)} %fusion.wanted, bf16[32,512,512]{2,1,0:T(8,128)(2,1)} %get-tuple-element.28.tiles.far_tiles, bf16[32,12288]{1,0:T(8,128)(2,1)S(1)} %get-tuple-element.35.rounded, s32[1]{0:T(128)} %get-tuple-element.38.after), custom_call_target="tpu_custom_call" | custom-call | flops 2147483648 | bytes 17825792 | tf_op jit(solution)/shard_map/far_back/pallas_call | solution.py:582
  193.1 2.6 %all-to-all-done.3.far_vecs = bf16[32,32,512]{2,1,0:T(8,128)(2,1)S(1)} async-done(((bf16[32,32,512]{2,1,0:T(8,128)(2,1)}), bf16[32,32,512]{2,1,0:T(8,128)(2,1)S(1)}, u32[]{:S(2)}, u32[]{:S(2)}) %all-to-all-start.3) | async-done | bytes 1048608 | tf_op jit(solution)/shard_map/all_to_all | solution.py:838
  195.6 4.6 %all-to-all-start.4 = ((bf16[32,32,512]{2,1,0:T(8,128)(2,1)}), bf16[32,32,512]{2,1,0:T(8,128)(2,1)}, u32[]{:S(2)}, u32[]{:S(2)}) async-start(bf16[32,32,512]{2,1,0:T(8,128)(2,1)} %far_back.1), calls=%async_computation.4 | async-start | bytes 2097152 | tf_op jit(solution)/shard_map/all_to_all | solution.py:838
  200.3 12.0 %rest_apply.1.own = f32[32,12288]{1,0:T(8,128)S(1)} custom-call(s32[128]{0:T(128)S(1)} %get-tuple-element.23.table, s32[32]{0:T(128)S(1)} %fusion.wanted, bf16[33,512,512]{2,1,0:T(8,128)(2,1)} %get-tuple-element.34.tiles.local_tiles, bf16[32,512,512]{2,1,0:T(8,128)(2,1)} %get-tuple-element.28.tiles.far_tiles, ...), custom_call_target="tpu_custom_call" | custom-call | flops 2684354560 | bytes 25165824 | tf_op jit(solution)/shard_map/rest_apply/pallas_call | solution.py:656
  212.3 5.3 %all-to-all-done.4.returned = bf16[32,32,512]{2,1,0:T(8,128)(2,1)} async-done(((bf16[32,32,512]{2,1,0:T(8,128)(2,1)}), bf16[32,32,512]{2,1,0:T(8,128)(2,1)}, u32[]{:S(2)}, u32[]{:S(2)}) %all-to-all-start.4) | async-done | bytes 1048608 | tf_op jit(solution)/shard_map/all_to_all | solution.py:838
  217.6 2.7 %assemble.1 = (f32[32,12288]{1,0:T(8,128)S(1)}, f32[8,128]{1,0:T(8,128)S(1)}) custom-call(s32[128]{0:T(128)S(1)} %get-tuple-element.23.table, f32[32,12288]{1,0:T(8,128)S(1)} %rest_apply.1.own, bf16[32,32,512]{2,1,0:T(8,128)(2,1)} %all-to-all-done.4.returned), custom_call_target="tpu_custom_call" | custom-call | flops 100000000 | bytes 5242880 | tf_op jit(solution)/shard_map/assemble/pallas_call | solution.py:732
  220.4 3.2 %collective-permute-start.5 = (f32[16,128]{1,0:T(8,128)S(1)}, f32[16,128]{1,0:T(8,128)S(1)}, u32[]{:S(2)}, u32[]{:S(2)}) collective-permute-start(f32[16,128]{1,0:T(8,128)S(1)} %constant_dynamic-update-slice_fusion), channel_id=1, source_target_pairs={{0,96},{32,64},{64,32},{96,0},{1,97},{33,65},{65,33},{97,1},{2,98}... | collective-permute-start | bytes 24584 | tf_op jit(solution)/shard_map/ppermute | solution.py:827
  223.6 0.1 collective-permute-start.4
  223.7 0.6 collective-permute-start.3
  224.2 0.4 collective-permute-done.5
  224.6 3.0 %collective-permute-done.4 = f32[16,128]{1,0:T(8,128)S(1)} collective-permute-done((f32[16,128]{1,0:T(8,128)S(1)}, f32[16,128]{1,0:T(8,128)S(1)}, u32[]{:S(2)}, u32[]{:S(2)}) %collective-permute-start.4) | collective-permute-done | bytes 8224 | tf_op jit(solution)/shard_map/ppermute | solution.py:827
  227.6 13.7 %all_to_all.30.grams = f32[32,16,128]{2,1,0:T(8,128)S(1)} all-to-all(f32[32,16,128]{2,1,0:T(8,128)S(1)} %broadcast_in_dim.3), channel_id=1, replica_groups=mesh['gx'=4,'gy'=32] {'gy'}, dimensions={0} | all-to-all | bytes 524288 | tf_op jit(solution)/shard_map/all_to_all | solution.py:838
  241.3 5.9 %last.1 = f32[32,12288]{1,0:T(8,128)} custom-call(f32[32,16,128]{2,1,0:T(8,128)S(1)} %all_to_all.30.grams, f32[32,12288]{1,0:T(8,128)S(1)} %get-tuple-element.40.image), custom_call_target="tpu_custom_call" | custom-call | flops 100000000 | bytes 4194304 | tf_op jit(solution)/shard_map/last/pallas_call | solution.py:813
  (8 shorter events, 0.0 us)
Async XLA Ops:
  6.9 112.6 %all-to-all-start = ((bf16[32,528,256]{2,1,0:T(8,128)(2,1)}), bf16[32,528,256]{2,1,0:T(8,128)(2,1)}, u32[]{:S(2)}, u32[]{:S(2)}) async-start(bf16[32,528,256]{2,1,0:T(8,128)(2,1)} %get-tuple-element.24), calls=%async_computation | async-start | bytes 17301504 | tf_op jit(solution)/shard_map/all_to_all | solution.py:838
  119.5 27.6 %all-to-all-start.1 = ((bf16[32,32,512]{2,1,0:T(8,128)(2,1)}), bf16[32,32,512]{2,1,0:T(8,128)(2,1)S(1)}, u32[]{:S(2)}, u32[]{:S(2)}) async-start(bf16[32,32,512]{2,1,0:T(8,128)(2,1)} %get-tuple-element.29), calls=%async_computation.1 | async-start | bytes 2097152 | tf_op jit(solution)/shard_map/all_to_all | solution.py:838
  147.1 22.0 %all-to-all-start.2 = ((bf16[32,32,512]{2,1,0:T(8,128)(2,1)}), bf16[32,32,512]{2,1,0:T(8,128)(2,1)}, u32[]{:S(2)}, u32[]{:S(2)}) async-start(bf16[32,32,512]{2,1,0:T(8,128)(2,1)} %get-tuple-element.31), calls=%async_computation.2 | async-start | bytes 2097152 | tf_op jit(solution)/shard_map/all_to_all | solution.py:838
  151.7 11.9 %collective-permute-start.2 = (f32[8,128]{1,0:T(8,128)S(1)}, f32[8,128]{1,0:T(8,128)S(1)}, u32[]{:S(2)}, u32[]{:S(2)}) collective-permute-start(f32[8,128]{1,0:T(8,128)S(1)} %get-tuple-element.32), channel_id=1, source_target_pairs={{0,96},{32,64},{64,32},{96,0},{1,97},{33,65},{65,33},{97,1},{2,98}... | collective-permute-start | bytes 12296 | tf_op jit(solution)/shard_map/ppermute | solution.py:827
  154.9 8.7 %collective-permute-start.1 = (f32[8,128]{1,0:T(8,128)S(1)}, f32[8,128]{1,0:T(8,128)S(1)}, u32[]{:S(2)}, u32[]{:S(2)}) collective-permute-start(f32[8,128]{1,0:T(8,128)S(1)} %get-tuple-element.32), channel_id=1, source_target_pairs={{0,64},{32,96},{64,0},{96,32},{1,65},{33,97},{65,1},{97,33},{2,66}... | collective-permute-start | bytes 12296 | tf_op jit(solution)/shard_map/ppermute | solution.py:827
  155.1 8.6 %collective-permute-start = (f32[8,128]{1,0:T(8,128)S(1)}, f32[8,128]{1,0:T(8,128)S(1)}, u32[]{:S(2)}, u32[]{:S(2)}) collective-permute-start(f32[8,128]{1,0:T(8,128)S(1)} %get-tuple-element.32), channel_id=1, source_target_pairs={{0,32},{32,0},{64,96},{96,64},{1,33},{33,1},{65,97},{97,65},{2,34}... | collective-permute-start | bytes 12296 | tf_op jit(solution)/shard_map/ppermute | solution.py:827
  174.3 21.3 %all-to-all-start.3 = ((bf16[32,32,512]{2,1,0:T(8,128)(2,1)}), bf16[32,32,512]{2,1,0:T(8,128)(2,1)S(1)}, u32[]{:S(2)}, u32[]{:S(2)}) async-start(bf16[32,32,512]{2,1,0:T(8,128)(2,1)} %get-tuple-element.36), calls=%async_computation.3 | async-start | bytes 2097152 | tf_op jit(solution)/shard_map/all_to_all | solution.py:838
  195.6 22.0 %all-to-all-start.4 = ((bf16[32,32,512]{2,1,0:T(8,128)(2,1)}), bf16[32,32,512]{2,1,0:T(8,128)(2,1)}, u32[]{:S(2)}, u32[]{:S(2)}) async-start(bf16[32,32,512]{2,1,0:T(8,128)(2,1)} %far_back.1), calls=%async_computation.4 | async-start | bytes 2097152 | tf_op jit(solution)/shard_map/all_to_all | solution.py:838
  220.4 4.2 %collective-permute-start.5 = (f32[16,128]{1,0:T(8,128)S(1)}, f32[16,128]{1,0:T(8,128)S(1)}, u32[]{:S(2)}, u32[]{:S(2)}) collective-permute-start(f32[16,128]{1,0:T(8,128)S(1)} %constant_dynamic-update-slice_fusion), channel_id=1, source_target_pairs={{0,96},{32,64},{64,32},{96,0},{1,97},{33,65},{65,33},{97,1},{2,98}... | collective-permute-start | bytes 24584 | tf_op jit(solution)/shard_map/ppermute | solution.py:827
  223.6 4.0 %collective-permute-start.4 = (f32[16,128]{1,0:T(8,128)S(1)}, f32[16,128]{1,0:T(8,128)S(1)}, u32[]{:S(2)}, u32[]{:S(2)}) collective-permute-start(f32[16,128]{1,0:T(8,128)S(1)} %constant_dynamic-update-slice_fusion), channel_id=1, source_target_pairs={{0,64},{32,96},{64,0},{96,32},{1,65},{33,97},{65,1},{97,33},{2,66}... | collective-permute-start | bytes 24584 | tf_op jit(solution)/shard_map/ppermute | solution.py:827
  223.7 3.9 %collective-permute-start.3 = (f32[16,128]{1,0:T(8,128)S(1)}, f32[16,128]{1,0:T(8,128)S(1)}, u32[]{:S(2)}, u32[]{:S(2)}) collective-permute-start(f32[16,128]{1,0:T(8,128)S(1)} %constant_dynamic-update-slice_fusion), channel_id=1, source_target_pairs={{0,32},{32,0},{64,96},{96,64},{1,33},{33,1},{65,97},{97,65},{2,34}... | collective-permute-start | bytes 24584 | tf_op jit(solution)/shard_map/ppermute | solution.py:827

commit v5 on v4

--- a/solution.py
+++ b/solution.py
@@ -15,7 +15,9 @@
 FAR_ROW = 0
 LOCAL = 32
 LOCAL_COUNT = 96
-TABLE = 128
+FIRST_PEER = 128
+NEXT_PEER = 160
+TABLE = 192
 
 NT = (((1,), (1,)), ((), ()))
 NN = (((1,), (0,)), ((), ()))
@@ -23,7 +25,6 @@
 VMEM = pl.BlockSpec(memory_space=pltpu.VMEM)
 HBM = pl.BlockSpec(memory_space=pltpu.HBM)
 GROUP = 4
-BUFFERS = 16
 CHUNK = 2048
 NOTE_ROWS = 16
 PACK = 8
@@ -95,13 +96,13 @@
     return scaled.astype(jnp.bfloat16)
 
 
-def note_slots(pairs, counts, table, head, following, block_count):
+def note_slots(pairs, counts, table, block_count, peer_count):
     def clear(i, _):
         table[FAR_ROW + i] = -1
-        head[i] = -1
-        return 0
-
-    lax.fori_loop(0, following.shape[0], clear, 0)
+        table[FIRST_PEER + i] = -1
+        return 0
+
+    lax.fori_loop(0, peer_count, clear, 0)
 
     def note(k, local_count):
         row = pairs[0, k]
@@ -113,8 +114,8 @@
         def _():
             peer = col - block_count
             table[FAR_ROW + peer] = row
-            following[peer] = head[row]
-            head[row] = peer
+            table[NEXT_PEER + peer] = table[FIRST_PEER + row]
+            table[FIRST_PEER + row] = peer
 
         @pl.when(crossed)
         def _():
@@ -123,11 +124,19 @@
         return local_count + jnp.where(crossed, 1, 0)
 
     table[LOCAL_COUNT] = lax.fori_loop(0, counts[0], note, 0)
+
+
+def each_peer_of(table, block, act):
+    def one(peer):
+        act(peer)
+        return table[NEXT_PEER + peer]
+
+    lax.while_loop(lambda peer: peer >= 0, one, table[FIRST_PEER + block])
 
 
 def prepare_kernel(
     counts, all_pairs, all_requests, raw, start, send, rounded, table,
-    pairs, requests, slot_sem, fresh, vecs, held, notes, head, following, load_sem, vec_sem, note_sem, send_sem,
+    pairs, requests, slot_sem, fresh, vecs, held, notes, load_sem, vec_sem, note_sem, send_sem,
 ):
     block_count = held.shape[0]
     peer_count = send.shape[0]
@@ -148,10 +157,10 @@
     vec_load.start()
     for slot_load in slot_loads:
         slot_load.wait()
-    note_slots(pairs, counts, table, head, following, block_count)
+    note_slots(pairs, counts, table, block_count, peer_count)
 
     def begin(b, _):
-        @pl.when(head[b] >= 0)
+        @pl.when(table[FIRST_PEER + b] >= 0)
         def _():
             load(b).start()
 
@@ -184,16 +193,12 @@
     note.start()
 
     def one(b, _):
-        @pl.when(head[b] >= 0)
+        @pl.when(table[FIRST_PEER + b] >= 0)
         def _():
             load(b).wait()
             held[b] = normalized(fresh[b])
 
-            def emit(peer):
-                give(peer, b).start()
-                return following[peer]
-
-            lax.while_loop(lambda peer: peer >= 0, emit, head[b])
+            each_peer_of(table, b, lambda peer: give(peer, b).start())
 
         return 0
 
@@ -215,7 +220,6 @@
 def prepare(embeddings, start, requests, pairs, counts):
     peer_count = requests.shape[1]
     block_count = embeddings.shape[0] // BLK
-    lists = max(block_count, peer_count)
     return pl.pallas_call(
         prepare_kernel,
         in_specs=[SMEM, HBM, HBM, HBM, HBM],
@@ -233,8 +237,6 @@
             pltpu.VMEM(start.shape, jnp.float32),
             pltpu.VMEM((block_count, NOTE, D), jnp.bfloat16),
             pltpu.VMEM((peer_count, NOTE_ROWS, D), jnp.bfloat16),
-            pltpu.SMEM((lists,), jnp.int32),
-            pltpu.SMEM((lists,), jnp.int32),
             pltpu.SemaphoreType.DMA((block_count,)),
             pltpu.SemaphoreType.DMA,
             pltpu.SemaphoreType.DMA,
@@ -398,15 +400,12 @@
     def save(n, z):
         return pltpu.make_async_copy(buffer.at[z], tiles.at[active[n]], save_sem.at[z])
 
-    def begin(n):
-        @pl.when(n < count)
-        def _():
-            for load in loads(n):
-                load.start()
+    def begin(n, _):
+        for load in loads(n):
+            load.start()
+        return 0
 
     def group(first, base):
-        for z in range(GROUP):
-            begin(first + 2 * GROUP + z)
         for z in range(GROUP):
 
             @pl.when(first + z < count)
@@ -442,10 +441,8 @@
 
         return 0
 
-    for n in range(2 * GROUP):
-        begin(n)
-        if n == GROUP - 1:
-            note_load.start()
+    lax.fori_loop(0, count, begin, 0)
+    note_load.start()
     lax.fori_loop(0, (count + 2 * GROUP - 1) // (2 * GROUP), two_groups, 0)
     note_load.wait()
     total = jnp.sum(notes[...].astype(jnp.float32), axis=0)
@@ -486,40 +483,39 @@
     )(wanted, in_hbm(units), in_hbm(far_rows), rounded, after)
 
 
-def stream(count, source_of, buffer, sem, use):
+def stream(count, source_of, buffer, sem, base=0):
     def load(n):
-        return pltpu.make_async_copy(source_of(n), buffer.at[n % BUFFERS], sem.at[n % BUFFERS])
-
-    def begin(n):
-        @pl.when(n < count)
-        def _():
-            load(n).start()
-
-    for n in range(BUFFERS - GROUP):
-        begin(n)
-
-    def group(g, _):
-        first = g * GROUP
-        for z in range(GROUP):
-            begin(first + BUFFERS - GROUP + z)
-        for z in range(GROUP):
-
-            @pl.when(first + z < count)
-            def _(n=first + z):
-                load(n).wait()
-
-        held = [jnp.minimum(first + z, count - 1) for z in range(GROUP)]
-        live = [first + z < count for z in range(GROUP)]
-        use(held, live, [buffer.at[n % BUFFERS] for n in held])
-        return 0
-
-    lax.fori_loop(0, (count + GROUP - 1) // GROUP, group, 0)
-
-
-def tile_scratch():
+        return pltpu.make_async_copy(source_of(n), buffer.at[base + n], sem.at[base + n])
+
+    def begin(n, _):
+        load(n).start()
+        return 0
+
+    lax.fori_loop(0, count, begin, 0)
+
+    def work(use):
+        def group(g, _):
+            first = g * GROUP
+            for z in range(GROUP):
+
+                @pl.when(first + z < count)
+                def _(n=first + z):
+                    load(n).wait()
+
+            held = [jnp.minimum(first + z, count - 1) for z in range(GROUP)]
+            live = [first + z < count for z in range(GROUP)]
+            use(held, live, [buffer.at[base + n] for n in held])
+            return 0
+
+        lax.fori_loop(0, (count + GROUP - 1) // GROUP, group, 0)
+
+    return work
+
+
+def tile_scratch(tiles):
     return [
-        pltpu.VMEM((BUFFERS, BLK, BLK), jnp.bfloat16),
-        pltpu.SemaphoreType.DMA((BUFFERS,)),
+        pltpu.VMEM((tiles, BLK, BLK), jnp.bfloat16),
+        pltpu.SemaphoreType.DMA((tiles,)),
     ]
 
 
@@ -530,13 +526,14 @@
 def own_apply_kernel(tiles, rounded, out, done, total, buffer, sem, save_sem):
     count = rounded.shape[1] // BLK
     done[0] = count
+    work = stream(count, lambda n: tiles.at[n], buffer, sem)
 
     def use(held, live, group):
         terms = [dot_nn(rounded[:, columns_of(n)], tile[...]) for n, tile in zip(held, group)]
         for n, term in zip(held, terms):
             total[:, columns_of(n)] = term
 
-    stream(count, lambda n: tiles.at[n], buffer, sem, use)
+    work(use)
     save = pltpu.make_async_copy(total, out, save_sem)
     save.start()
     save.wait()
@@ -553,10 +550,10 @@
         ],
         scratch_shapes=[
             pltpu.VMEM(rounded.shape, jnp.float32),
-            *tile_scratch(),
-            pltpu.SemaphoreType.DMA,
-        ],
-        compiler_params=params(16),
+            *tile_scratch(rounded.shape[1] // BLK),
+            pltpu.SemaphoreType.DMA,
+        ],
+        compiler_params=params(20),
         cost_estimate=cost(24 * 2 * BLK * BLK * 4 * VECS, 13 * 2**20),
         name="own_apply",
     )(in_hbm(tiles), rounded)
@@ -565,6 +562,7 @@
 def far_back_kernel(wanted, tiles, rounded, after, back, active, buffer, sem):
     del after
     count = note_active(wanted, active)
+    work = stream(count, lambda n: tiles.at[active[n]], buffer, sem)
 
     def use(held, live, group):
         peers = [active[n] for n in held]
@@ -574,7 +572,7 @@
         for peer, term in zip(peers, terms):
             back[peer] = term.astype(jnp.bfloat16)
 
-    stream(count, lambda n: tiles.at[active[n]], buffer, sem, use)
+    work(use)
 
 
 def far_back(wanted, tiles, rounded, after):
@@ -584,16 +582,14 @@
         in_specs=[SMEM, HBM, VMEM, SMEM],
         out_specs=VMEM,
         out_shape=jax.ShapeDtypeStruct((peer_count, VECS, BLK), jnp.bfloat16),
-        scratch_shapes=[pltpu.SMEM((peer_count,), jnp.int32), *tile_scratch()],
-        compiler_params=params(16),
+        scratch_shapes=[pltpu.SMEM((peer_count,), jnp.int32), *tile_scratch(peer_count)],
+        compiler_params=params(24),
         cost_estimate=cost(32 * 2 * BLK * BLK * 4 * VECS, 17 * 2**20),
         name="far_back",
     )(wanted, in_hbm(tiles), rounded, after)
 
 
-def add_far(wanted, tiles, far_vecs, total, active, buffer, sem):
-    count = note_active(wanted, active)
-
+def add_far(wanted, far_vecs, total, active, work):
     def use(held, live, group):
         peers = [active[n] for n in held]
         terms = [
@@ -603,14 +599,16 @@
         for peer, term in zip(peers, terms):
             total[:, columns_of(wanted[peer])] += term
 
-    stream(count, lambda n: tiles.at[active[n]], buffer, sem, use)
+    work(use)
 
 
 def far_first_kernel(wanted, tiles, far_vecs, before, total, active, buffer, sem, before_sem):
     before_load = pltpu.make_async_copy(before, total, before_sem)
     before_load.start()
+    count = note_active(wanted, active)
+    work = stream(count, lambda n: tiles.at[active[n]], buffer, sem)
     before_load.wait()
-    add_far(wanted, tiles, far_vecs, total, active, buffer, sem)
+    add_far(wanted, far_vecs, total, active, work)
 
 
 def far_first(wanted, tiles, far_vecs, before):
@@ -621,10 +619,10 @@
         out_shape=jax.ShapeDtypeStruct(before.shape, jnp.float32),
         scratch_shapes=[
             pltpu.SMEM(wanted.shape, jnp.int32),
-            *tile_scratch(),
-            pltpu.SemaphoreType.DMA,
-        ],
-        compiler_params=params(16),
+            *tile_scratch(wanted.shape[0]),
+            pltpu.SemaphoreType.DMA,
+        ],
+        compiler_params=params(28),
         cost_estimate=cost(32 * 2 * BLK * BLK * 4 * VECS, 20 * 2**20),
         name="far_first",
     )(wanted, in_hbm(tiles), far_vecs, in_hbm(before))
@@ -636,6 +634,9 @@
     block_count = rounded.shape[1] // BLK
     before_load = pltpu.make_async_copy(before, total, before_sem)
     before_load.start()
+    crossed_work = stream(table[LOCAL_COUNT], lambda n: local_tiles.at[block_count + n], buffer, sem)
+    count = note_active(wanted, active)
+    far_work = stream(count, lambda n: far_tiles.at[active[n]], buffer, sem, EXTRA)
     before_load.wait()
 
     def use_crossed(held, live, group):
@@ -648,8 +649,8 @@
             total[:, columns_of(col)] += col_term
             total[:, columns_of(row)] += row_term
 
-    stream(table[LOCAL_COUNT], lambda n: local_tiles.at[block_count + n], buffer, sem, use_crossed)
-    add_far(wanted, far_tiles, far_vecs, total, active, buffer, sem)
+    crossed_work(use_crossed)
+    add_far(wanted, far_vecs, total, active, far_work)
 
 
 def rest_apply(table, wanted, local_tiles, far_tiles, rounded, far_vecs, before):
@@ -658,8 +659,12 @@
         in_specs=[SMEM, SMEM, HBM, HBM, VMEM, VMEM, HBM],
         out_specs=VMEM,
         out_shape=jax.ShapeDtypeStruct(before.shape, jnp.float32),
-        scratch_shapes=[pltpu.SMEM(wanted.shape, jnp.int32), *tile_scratch(), pltpu.SemaphoreType.DMA],
-        compiler_params=params(16),
+        scratch_shapes=[
+            pltpu.SMEM(wanted.shape, jnp.int32),
+            *tile_scratch(EXTRA + wanted.shape[0]),
+            pltpu.SemaphoreType.DMA,
+        ],
+        compiler_params=params(30),
         cost_estimate=cost(40 * 2 * BLK * BLK * 4 * VECS, 24 * 2**20),
         name="rest_apply",
     )(table, wanted, in_hbm(local_tiles), in_hbm(far_tiles), rounded, far_vecs, in_hbm(before))
@@ -687,19 +692,31 @@
     gram[...] = packed(sum_of_parts(total))
 
 
-def forward_kernel(table, own, returned, inverse, rounded, gram, send, image, out, sem):
+def forward_kernel(table, own, returned, inverse, rounded, gram, send, image, sem):
     factor = factor_parts(inverse[...])
     add_returned(table, own, returned, image)
+
+    def copy(peer, row):
+        return pltpu.make_async_copy(rounded.at[:, columns_of(row)], send.at[peer], sem.at[peer])
+
     for c in range(0, image.shape[1], CHUNK):
         based = solved(factor, image[:, c : c + CHUNK])
         image[:, c : c + CHUNK] = based
         rounded[:, c : c + CHUNK] = based.astype(jnp.bfloat16)
-
-    spread(table, rounded, out)
-    save = pltpu.make_async_copy(out, send, sem)
-    save.start()
+        for block in range(c // BLK, (c + CHUNK) // BLK):
+            each_peer_of(table, block, lambda peer, block=block: copy(peer, block).start())
     gram_kernel(image, gram)
-    save.wait()
+
+    def finish(peer, _):
+        row = table[FAR_ROW + peer]
+
+        @pl.when(row >= 0)
+        def _():
+            copy(peer, row).wait()
+
+        return 0
+
+    lax.fori_loop(0, send.shape[0], finish, 0)
 
 
 def forward(table, own, returned, inverse):
@@ -714,8 +731,7 @@
         ],
         scratch_shapes=[
             pltpu.VMEM(own.shape, jnp.float32),
-            pltpu.VMEM(returned.shape, jnp.bfloat16),
-            pltpu.SemaphoreType.DMA,
+            pltpu.SemaphoreType.DMA((returned.shape[0],)),
         ],
         compiler_params=params(12),
         cost_estimate=cost(10**8, 5 * 2**20),
@@ -794,27 +810,35 @@
     )(gram)
 
 
-def last_kernel(rows_all, grams, image, vectors):
+def last_kernel(rows_all, grams, image, out, vectors, sem):
     both = jnp.sum(grams[...], axis=0) * (1.0 / rows_all)
     first = inverse_factor(unpacked(both[:PACK]))
-    turned = lax.dot_general(
-        product(first, unpacked(both[PACK:])),
-        first,
-        NT,
-        precision=lax.Precision.HIGHEST,
-        preferred_element_type=jnp.float32,
+    high, middle, low = three_parts(first)
+    turned = dot_nt(
+        factor_parts(product(first, unpacked(both[PACK:]))),
+        jnp.concatenate([high, middle, low, high, middle, high], axis=1),
     )
     factor = factor_parts(product(inverse_factor(turned), first))
+    copies = []
     for c in range(0, image.shape[1], CHUNK):
-        vectors[:, c : c + CHUNK] = solved(factor, image[:, c : c + CHUNK])
+        columns = pl.ds(c, CHUNK)
+        vectors[:, columns] = solved(factor, image[:, columns])
+        copies.append(pltpu.make_async_copy(vectors.at[:, columns], out.at[:, columns], sem.at[c // CHUNK]))
+        copies[-1].start()
+    for copy in copies:
+        copy.wait()
 
 
 def last(rows_all, grams, image):
     return pl.pallas_call(
         functools.partial(last_kernel, rows_all),
         in_specs=[VMEM, VMEM],
-        out_specs=VMEM,
+        out_specs=HBM,
         out_shape=jax.ShapeDtypeStruct(image.shape, jnp.float32),
+        scratch_shapes=[
+            pltpu.VMEM(image.shape, jnp.float32),
+            pltpu.SemaphoreType.DMA((image.shape[1] // CHUNK,)),
+        ],
         compiler_params=params(10),
         cost_estimate=cost(10**8, 4 * 2**20),
         name="last",

time: 248 us -> 247 us (level)
  Pallas kernels: 98.6 us -> 93.5 us
    pallas_call x1, Pallas kernels: 12 us -> 8.76 us  [rest_apply(): pl.pallas_call(rest_apply_kernel, in_specs=[SMEM, SMEM, HBM, HBM, VMEM, V...]
    all_to_all x5, waiting for transfers between devices: 88.2 us -> 91 us  [exchange(): return lax.all_to_all(blocks, 'gy', split_axis=0, concat_axis=0, tiled=True)]
  transfers between devices with their start and end apart: 11 -> 11, of which waited for: 7 -> 6; matrix products, arithmetic and copies ran while one was open for 1% -> 1% of each run, Pallas kernels for 32% -> 30%
where the time goes in v5:
time: 247 us; the launch traced here: 246 us
  Pallas kernels  93.5 us (38%)
  waiting for transfers between devices  93.5 us (38%)
  starting transfers between devices  41.5 us (17%)
  blocking collectives  14 us (6%)
    all_to_all x5, waiting for transfers between devices, exchange(): return lax.all_to_all(blocks, 'gy', split_axis=0, concat_axis=0, tiled=True)  91 us
    all_to_all x5, starting transfers between devices, exchange(): return lax.all_to_all(blocks, 'gy', split_axis=0, concat_axis=0, tiled=True)  32.6 us
    pallas_call x1, Pallas kernels, local_build(): pl.pallas_call(local_build_kernel, in_specs=[SMEM, HBM, VMEM], out_specs=...  30.6 us
    all_to_all x1, blocking collectives, exchange(): return lax.all_to_all(blocks, 'gy', split_axis=0, concat_axis=0, tiled=True)  14 us
    pallas_call x1, Pallas kernels, far_build(): pl.pallas_call(far_build_kernel, in_specs=[SMEM, HBM, HBM, VMEM, SMEM], o...  11.7 us
    ppermute x6, starting transfers between devices, sum_over_gx(): lax.ppermute(gram, 'gx', [(i, i ^ mask) for i in range(size)])  8.86 us
    pallas_call x1, Pallas kernels, rest_apply(): pl.pallas_call(rest_apply_kernel, in_specs=[SMEM, SMEM, HBM, HBM, VMEM, V...  8.76 us
    pallas_call x1, Pallas kernels, far_back(): pl.pallas_call(far_back_kernel, in_specs=[SMEM, HBM, VMEM, SMEM], out_spe...  7.06 us
  transfers between devices with their start and end apart: 11, of which 6 were waited for; matrix products, arithmetic and copies ran while one was open for 1% of the time, Pallas kernels for 30%

profile of v5, /device:TPU:1, one launch (start us, length us, event | category | flops | bytes accessed | tf_op | source)
XLA Modules:
  0.0 246.3 jit_solution(4921668564142960755)
XLA Ops:
  0.7 6.6 %prepare.1 = (bf16[32,528,256]{2,1,0:T(8,128)(2,1)}, bf16[32,12288]{1,0:T(8,128)(2,1)S(1)}, s32[192]{0:T(256)S(1)}) custom-call(s32[1]{0:T(128)S(6)} %copy.7.counts, s32[2,64]{1,0:T(2,128)} %bitcast.3, s32[1,32]{1,0:T(1,128)} %all_requests.1, bf16[12288,256]{1,0:T(8,128)(2,1)} %raw.3, f32[32,12288]{1,0:T(8,128)} %start.1), custom_call_target="tpu_custom_call" | custom-call | flops 10000000 | bytes 25165824 | tf_op jit(solution)/shard_map/prepare/pallas_call | solution.py:223
  7.3 9.0 %all-to-all-start = ((bf16[32,528,256]{2,1,0:T(8,128)(2,1)}), bf16[32,528,256]{2,1,0:T(8,128)(2,1)}, u32[]{:S(2)}, u32[]{:S(2)}) async-start(bf16[32,528,256]{2,1,0:T(8,128)(2,1)} %get-tuple-element.24), calls=%async_computation | async-start | bytes 17301504 | tf_op jit(solution)/shard_map/all_to_all | solution.py:862
  16.2 30.6 %local_build.1 = (bf16[24,512,256]{2,1,0:T(8,128)(2,1)}, f32[32,12288]{1,0:T(8,128)}, bf16[33,512,512]{2,1,0:T(8,128)(2,1)}, bf16[32,32,512]{2,1,0:T(8,128)(2,1)}, s32[1]{0:T(128)}) custom-call(s32[192]{0:T(256)S(1)} %get-tuple-element.23.table, bf16[12288,256]{1,0:T(8,128)(2,1)} %raw.3, bf16[32,12288]{1,0:T(8,128)(2,1)S(1)} %get-tuple-element.25.rounded), custom_call_target="tpu_custom_call" | custom-call | flops 8858370048 | bytes 33554432 | tf_op jit(solution)/shard_map/local_build/pallas_call | solution.py:330
  46.8 72.3 %all-to-all-done.far_rows = bf16[32,528,256]{2,1,0:T(8,128)(2,1)} async-done(((bf16[32,528,256]{2,1,0:T(8,128)(2,1)}), bf16[32,528,256]{2,1,0:T(8,128)(2,1)}, u32[]{:S(2)}, u32[]{:S(2)}) %all-to-all-start) | async-done | bytes 8650784 | tf_op jit(solution)/shard_map/all_to_all | solution.py:862
  119.2 10.3 %all-to-all-start.1 = ((bf16[32,32,512]{2,1,0:T(8,128)(2,1)}), bf16[32,32,512]{2,1,0:T(8,128)(2,1)S(1)}, u32[]{:S(2)}, u32[]{:S(2)}) async-start(bf16[32,32,512]{2,1,0:T(8,128)(2,1)} %get-tuple-element.29), calls=%async_computation.1 | async-start | bytes 2097152 | tf_op jit(solution)/shard_map/all_to_all | solution.py:862
  129.5 1.5 fusion.wanted
  131.0 11.7 %far_build.1 = (bf16[32,32,512]{2,1,0:T(8,128)(2,1)}, f32[8,128]{1,0:T(8,128)S(1)}, bf16[32,512,512]{2,1,0:T(8,128)(2,1)}) custom-call(s32[32]{0:T(128)S(1)} %fusion.wanted, bf16[24,512,256]{2,1,0:T(8,128)(2,1)} %get-tuple-element.26.units, bf16[32,528,256]{2,1,0:T(8,128)(2,1)} %all-to-all-done.far_rows, bf16[32,12288]{1,0:T(8,128)(2,1)S(1)} %get-tuple-element.25.rounded, ...), custom_call_target="tpu_custom_call" | custom-call | flops 6442450944 | bytes 35651584 | tf_op jit(solution)/shard_map/far_build/pallas_call | solution.py:461
  142.6 4.1 %all-to-all-done.1.far_vecs = bf16[32,32,512]{2,1,0:T(8,128)(2,1)S(1)} async-done(((bf16[32,32,512]{2,1,0:T(8,128)(2,1)}), bf16[32,32,512]{2,1,0:T(8,128)(2,1)S(1)}, u32[]{:S(2)}, u32[]{:S(2)}) %all-to-all-start.1) | async-done | bytes 1048608 | tf_op jit(solution)/shard_map/all_to_all | solution.py:862
  146.8 4.0 %all-to-all-start.2 = ((bf16[32,32,512]{2,1,0:T(8,128)(2,1)}), bf16[32,32,512]{2,1,0:T(8,128)(2,1)S(1)}, u32[]{:S(2)}, u32[]{:S(2)}) async-start(bf16[32,32,512]{2,1,0:T(8,128)(2,1)} %get-tuple-element.31), calls=%async_computation.2 | async-start | bytes 2097152 | tf_op jit(solution)/shard_map/all_to_all | solution.py:862
  150.7 3.4 %collective-permute-start.2 = (f32[8,128]{1,0:T(8,128)S(1)}, f32[8,128]{1,0:T(8,128)S(1)}, u32[]{:S(2)}, u32[]{:S(2)}) collective-permute-start(f32[8,128]{1,0:T(8,128)S(1)} %get-tuple-element.32), channel_id=1, source_target_pairs={{0,96},{32,64},{64,32},{96,0},{1,97},{33,65},{65,33},{97,1},{2,98}... | collective-permute-start | bytes 12296 | tf_op jit(solution)/shard_map/ppermute | solution.py:851
  154.1 1.4 collective-permute-start.1
  155.5 0.0 collective-permute-start
  155.5 1.2 copy-done.1
  156.8 6.5 %far_first.1.own = f32[32,12288]{1,0:T(8,128)S(1)} custom-call(s32[32]{0:T(128)S(1)} %fusion.wanted, bf16[32,512,512]{2,1,0:T(8,128)(2,1)} %get-tuple-element.28.tiles.far_tiles, bf16[32,32,512]{2,1,0:T(8,128)(2,1)S(1)} %copy-done.1, f32[32,12288]{1,0:T(8,128)} %get-tuple-element.30.before), custom_call_target="tpu_custom_call" | custom-call | flops 2147483648 | bytes 20971520 | tf_op jit(solution)/shard_map/far_first/pallas_call | solution.py:615
  163.3 0.0 collective-permute-done.2
  163.3 0.0 collective-permute-done.1
  163.3 1.8 basis.1.inverse
  165.2 2.8 %all-to-all-done.2.returned = bf16[32,32,512]{2,1,0:T(8,128)(2,1)S(1)} async-done(((bf16[32,32,512]{2,1,0:T(8,128)(2,1)}), bf16[32,32,512]{2,1,0:T(8,128)(2,1)S(1)}, u32[]{:S(2)}, u32[]{:S(2)}) %all-to-all-start.2) | async-done | bytes 1048608 | tf_op jit(solution)/shard_map/all_to_all | solution.py:862
  168.0 5.4 %forward.1 = (bf16[32,12288]{1,0:T(8,128)(2,1)S(1)}, f32[8,128]{1,0:T(8,128)S(1)}, bf16[32,32,512]{2,1,0:T(8,128)(2,1)}) custom-call(s32[192]{0:T(256)S(1)} %get-tuple-element.23.table, f32[32,12288]{1,0:T(8,128)S(1)} %far_first.1.own, bf16[32,32,512]{2,1,0:T(8,128)(2,1)S(1)} %all-to-all-done.2.returned, f32[32,32]{1,0:T(8,128)S(1)} %basis.1.inverse), custom_call_target="tpu_custom_call" | custom-call | flops 100000000 | bytes 5242880 | tf_op jit(solution)/shard_map/forward/pallas_call | solution.py:723
  173.5 4.7 %all-to-all-start.3 = ((bf16[32,32,512]{2,1,0:T(8,128)(2,1)}), bf16[32,32,512]{2,1,0:T(8,128)(2,1)S(1)}, u32[]{:S(2)}, u32[]{:S(2)}) async-start(bf16[32,32,512]{2,1,0:T(8,128)(2,1)} %get-tuple-element.36), calls=%async_computation.3 | async-start | bytes 2097152 | tf_op jit(solution)/shard_map/all_to_all | solution.py:862
  178.2 7.0 %own_apply.1 = (f32[32,12288]{1,0:T(8,128)}, s32[1]{0:T(128)}) custom-call(bf16[33,512,512]{2,1,0:T(8,128)(2,1)} %get-tuple-element.34.tiles.local_tiles, bf16[32,12288]{1,0:T(8,128)(2,1)S(1)} %get-tuple-element.35.rounded), custom_call_target="tpu_custom_call" | custom-call | flops 1610612736 | bytes 13631488 | tf_op jit(solution)/shard_map/own_apply/pallas_call | solution.py:543
  185.1 7.1 %far_back.1 = bf16[32,32,512]{2,1,0:T(8,128)(2,1)} custom-call(s32[32]{0:T(128)S(1)} %fusion.wanted, bf16[32,512,512]{2,1,0:T(8,128)(2,1)} %get-tuple-element.28.tiles.far_tiles, bf16[32,12288]{1,0:T(8,128)(2,1)S(1)} %get-tuple-element.35.rounded, s32[1]{0:T(128)} %get-tuple-element.38.after), custom_call_target="tpu_custom_call" | custom-call | flops 2147483648 | bytes 17825792 | tf_op jit(solution)/shard_map/far_back/pallas_call | solution.py:580
  192.2 3.1 %all-to-all-done.3.far_vecs = bf16[32,32,512]{2,1,0:T(8,128)(2,1)S(1)} async-done(((bf16[32,32,512]{2,1,0:T(8,128)(2,1)}), bf16[32,32,512]{2,1,0:T(8,128)(2,1)S(1)}, u32[]{:S(2)}, u32[]{:S(2)}) %all-to-all-start.3) | async-done | bytes 1048608 | tf_op jit(solution)/shard_map/all_to_all | solution.py:862
  195.4 4.6 %all-to-all-start.4 = ((bf16[32,32,512]{2,1,0:T(8,128)(2,1)}), bf16[32,32,512]{2,1,0:T(8,128)(2,1)}, u32[]{:S(2)}, u32[]{:S(2)}) async-start(bf16[32,32,512]{2,1,0:T(8,128)(2,1)} %far_back.1), calls=%async_computation.4 | async-start | bytes 2097152 | tf_op jit(solution)/shard_map/all_to_all | solution.py:862
  200.0 8.8 %rest_apply.1.own = f32[32,12288]{1,0:T(8,128)S(1)} custom-call(s32[192]{0:T(256)S(1)} %get-tuple-element.23.table, s32[32]{0:T(128)S(1)} %fusion.wanted, bf16[33,512,512]{2,1,0:T(8,128)(2,1)} %get-tuple-element.34.tiles.local_tiles, bf16[32,512,512]{2,1,0:T(8,128)(2,1)} %get-tuple-element.28.tiles.far_tiles, ...), custom_call_target="tpu_custom_call" | custom-call | flops 2684354560 | bytes 25165824 | tf_op jit(solution)/shard_map/rest_apply/pallas_call | solution.py:657
  208.8 8.6 %all-to-all-done.4.returned = bf16[32,32,512]{2,1,0:T(8,128)(2,1)} async-done(((bf16[32,32,512]{2,1,0:T(8,128)(2,1)}), bf16[32,32,512]{2,1,0:T(8,128)(2,1)}, u32[]{:S(2)}, u32[]{:S(2)}) %all-to-all-start.4) | async-done | bytes 1048608 | tf_op jit(solution)/shard_map/all_to_all | solution.py:862
  217.3 2.8 %assemble.1 = (f32[32,12288]{1,0:T(8,128)S(1)}, f32[8,128]{1,0:T(8,128)S(1)}) custom-call(s32[192]{0:T(256)S(1)} %get-tuple-element.23.table, f32[32,12288]{1,0:T(8,128)S(1)} %rest_apply.1.own, bf16[32,32,512]{2,1,0:T(8,128)(2,1)} %all-to-all-done.4.returned), custom_call_target="tpu_custom_call" | custom-call | flops 100000000 | bytes 5242880 | tf_op jit(solution)/shard_map/assemble/pallas_call | solution.py:748
  220.1 2.6 %collective-permute-start.5 = (f32[16,128]{1,0:T(8,128)S(1)}, f32[16,128]{1,0:T(8,128)S(1)}, u32[]{:S(2)}, u32[]{:S(2)}) collective-permute-start(f32[16,128]{1,0:T(8,128)S(1)} %constant_dynamic-update-slice_fusion), channel_id=1, source_target_pairs={{0,96},{32,64},{64,32},{96,0},{1,97},{33,65},{65,33},{97,1},{2,98}... | collective-permute-start | bytes 24584 | tf_op jit(solution)/shard_map/ppermute | solution.py:851
  222.7 1.5 collective-permute-start.4
  224.2 2.5 %collective-permute-done.4 = f32[16,128]{1,0:T(8,128)S(1)} collective-permute-done((f32[16,128]{1,0:T(8,128)S(1)}, f32[16,128]{1,0:T(8,128)S(1)}, u32[]{:S(2)}, u32[]{:S(2)}) %collective-permute-start.4) | collective-permute-done | bytes 8224 | tf_op jit(solution)/shard_map/ppermute | solution.py:851
  226.8 14.0 %all_to_all.30.grams = f32[32,16,128]{2,1,0:T(8,128)S(1)} all-to-all(f32[32,16,128]{2,1,0:T(8,128)S(1)} %broadcast_in_dim.3), channel_id=1, replica_groups=mesh['gx'=4,'gy'=32] {'gy'}, dimensions={0} | all-to-all | bytes 524288 | tf_op jit(solution)/shard_map/all_to_all | solution.py:862
  240.7 5.4 %last.1 = f32[32,12288]{1,0:T(8,128)} custom-call(f32[32,16,128]{2,1,0:T(8,128)S(1)} %all_to_all.30.grams, f32[32,12288]{1,0:T(8,128)S(1)} %get-tuple-element.40.image), custom_call_target="tpu_custom_call" | custom-call | flops 100000000 | bytes 4194304 | tf_op jit(solution)/shard_map/last/pallas_call | solution.py:833
  (12 shorter events, 0.1 us)
Async XLA Ops:
  7.3 111.9 %all-to-all-start = ((bf16[32,528,256]{2,1,0:T(8,128)(2,1)}), bf16[32,528,256]{2,1,0:T(8,128)(2,1)}, u32[]{:S(2)}, u32[]{:S(2)}) async-start(bf16[32,528,256]{2,1,0:T(8,128)(2,1)} %get-tuple-element.24), calls=%async_computation | async-start | bytes 17301504 | tf_op jit(solution)/shard_map/all_to_all | solution.py:862
  119.2 27.6 %all-to-all-start.1 = ((bf16[32,32,512]{2,1,0:T(8,128)(2,1)}), bf16[32,32,512]{2,1,0:T(8,128)(2,1)S(1)}, u32[]{:S(2)}, u32[]{:S(2)}) async-start(bf16[32,32,512]{2,1,0:T(8,128)(2,1)} %get-tuple-element.29), calls=%async_computation.1 | async-start | bytes 2097152 | tf_op jit(solution)/shard_map/all_to_all | solution.py:862
  146.8 8.8 %copy-start = (bf16[32,32,512]{2,1,0:T(8,128)(2,1)}, bf16[32,32,512]{2,1,0:T(8,128)(2,1)S(1)}, u32[]{:S(2)}) copy-start(bf16[32,32,512]{2,1,0:T(8,128)(2,1)S(1)} %all-to-all-done.1.far_vecs) | copy-start | bytes 3145732
  146.8 21.3 %all-to-all-start.2 = ((bf16[32,32,512]{2,1,0:T(8,128)(2,1)}), bf16[32,32,512]{2,1,0:T(8,128)(2,1)S(1)}, u32[]{:S(2)}, u32[]{:S(2)}) async-start(bf16[32,32,512]{2,1,0:T(8,128)(2,1)} %get-tuple-element.31), calls=%async_computation.2 | async-start | bytes 2097152 | tf_op jit(solution)/shard_map/all_to_all | solution.py:862
  150.7 12.6 %collective-permute-start.2 = (f32[8,128]{1,0:T(8,128)S(1)}, f32[8,128]{1,0:T(8,128)S(1)}, u32[]{:S(2)}, u32[]{:S(2)}) collective-permute-start(f32[8,128]{1,0:T(8,128)S(1)} %get-tuple-element.32), channel_id=1, source_target_pairs={{0,96},{32,64},{64,32},{96,0},{1,97},{33,65},{65,33},{97,1},{2,98}... | collective-permute-start | bytes 12296 | tf_op jit(solution)/shard_map/ppermute | solution.py:851
  154.1 9.2 %collective-permute-start.1 = (f32[8,128]{1,0:T(8,128)S(1)}, f32[8,128]{1,0:T(8,128)S(1)}, u32[]{:S(2)}, u32[]{:S(2)}) collective-permute-start(f32[8,128]{1,0:T(8,128)S(1)} %get-tuple-element.32), channel_id=1, source_target_pairs={{0,64},{32,96},{64,0},{96,32},{1,65},{33,97},{65,1},{97,33},{2,66}... | collective-permute-start | bytes 12296 | tf_op jit(solution)/shard_map/ppermute | solution.py:851
  155.5 7.8 %collective-permute-start = (f32[8,128]{1,0:T(8,128)S(1)}, f32[8,128]{1,0:T(8,128)S(1)}, u32[]{:S(2)}, u32[]{:S(2)}) collective-permute-start(f32[8,128]{1,0:T(8,128)S(1)} %get-tuple-element.32), channel_id=1, source_target_pairs={{0,32},{32,0},{64,96},{96,64},{1,33},{33,1},{65,97},{97,65},{2,34}... | collective-permute-start | bytes 12296 | tf_op jit(solution)/shard_map/ppermute | solution.py:851
  155.5 1.2 copy-start.1
  173.5 21.9 %all-to-all-start.3 = ((bf16[32,32,512]{2,1,0:T(8,128)(2,1)}), bf16[32,32,512]{2,1,0:T(8,128)(2,1)S(1)}, u32[]{:S(2)}, u32[]{:S(2)}) async-start(bf16[32,32,512]{2,1,0:T(8,128)(2,1)} %get-tuple-element.36), calls=%async_computation.3 | async-start | bytes 2097152 | tf_op jit(solution)/shard_map/all_to_all | solution.py:862
  195.4 22.0 %all-to-all-start.4 = ((bf16[32,32,512]{2,1,0:T(8,128)(2,1)}), bf16[32,32,512]{2,1,0:T(8,128)(2,1)}, u32[]{:S(2)}, u32[]{:S(2)}) async-start(bf16[32,32,512]{2,1,0:T(8,128)(2,1)} %far_back.1), calls=%async_computation.4 | async-start | bytes 2097152 | tf_op jit(solution)/shard_map/all_to_all | solution.py:862
  220.1 4.1 %collective-permute-start.5 = (f32[16,128]{1,0:T(8,128)S(1)}, f32[16,128]{1,0:T(8,128)S(1)}, u32[]{:S(2)}, u32[]{:S(2)}) collective-permute-start(f32[16,128]{1,0:T(8,128)S(1)} %constant_dynamic-update-slice_fusion), channel_id=1, source_target_pairs={{0,96},{32,64},{64,32},{96,0},{1,97},{33,65},{65,33},{97,1},{2,98}... | collective-permute-start | bytes 24584 | tf_op jit(solution)/shard_map/ppermute | solution.py:851
  222.7 4.0 %collective-permute-start.4 = (f32[16,128]{1,0:T(8,128)S(1)}, f32[16,128]{1,0:T(8,128)S(1)}, u32[]{:S(2)}, u32[]{:S(2)}) collective-permute-start(f32[16,128]{1,0:T(8,128)S(1)} %constant_dynamic-update-slice_fusion), channel_id=1, source_target_pairs={{0,64},{32,96},{64,0},{96,32},{1,65},{33,97},{65,1},{97,33},{2,66}... | collective-permute-start | bytes 24584 | tf_op jit(solution)/shard_map/ppermute | solution.py:851
  224.2 2.5 %collective-permute-start.3 = (f32[16,128]{1,0:T(8,128)S(1)}, f32[16,128]{1,0:T(8,128)S(1)}, u32[]{:S(2)}, u32[]{:S(2)}) collective-permute-start(f32[16,128]{1,0:T(8,128)S(1)} %constant_dynamic-update-slice_fusion), channel_id=1, source_target_pairs={{0,32},{32,0},{64,96},{96,64},{1,33},{33,1},{65,97},{97,65},{2,34}... | collective-permute-start | bytes 24584 | tf_op jit(solution)/shard_map/ppermute | solution.py:851

commit v6 on v5

--- a/solution.py
+++ b/solution.py
@@ -11,6 +11,7 @@
 VECS = 32
 BLK = 512
 EXTRA = 9
+LATE = 8
 
 FAR_ROW = 0
 LOCAL = 32
@@ -524,8 +525,9 @@
 
 
 def own_apply_kernel(tiles, rounded, out, done, total, buffer, sem, save_sem):
-    count = rounded.shape[1] // BLK
+    count = rounded.shape[1] // BLK - LATE
     done[0] = count
+    total[:, count * BLK :] = jnp.zeros((VECS, LATE * BLK), jnp.float32)
     work = stream(count, lambda n: tiles.at[n], buffer, sem)
 
     def use(held, live, group):
@@ -635,6 +637,8 @@
     before_load = pltpu.make_async_copy(before, total, before_sem)
     before_load.start()
     crossed_work = stream(table[LOCAL_COUNT], lambda n: local_tiles.at[block_count + n], buffer, sem)
+    early = block_count - LATE
+    late_work = stream(LATE, lambda n: local_tiles.at[early + n], buffer, sem, EXTRA + wanted.shape[0])
     count = note_active(wanted, active)
     far_work = stream(count, lambda n: far_tiles.at[active[n]], buffer, sem, EXTRA)
     before_load.wait()
@@ -649,6 +653,12 @@
             total[:, columns_of(col)] += col_term
             total[:, columns_of(row)] += row_term
 
+    def use_late(held, live, group):
+        terms = [dot_nn(rounded[:, columns_of(early + n)], tile[...]) for n, tile in zip(held, group)]
+        for n, term in zip(held, terms):
+            total[:, columns_of(early + n)] += term
+
+    late_work(use_late)
     crossed_work(use_crossed)
     add_far(wanted, far_vecs, total, active, far_work)
 
@@ -661,10 +671,10 @@
         out_shape=jax.ShapeDtypeStruct(before.shape, jnp.float32),
         scratch_shapes=[
             pltpu.SMEM(wanted.shape, jnp.int32),
-            *tile_scratch(EXTRA + wanted.shape[0]),
+            *tile_scratch(EXTRA + wanted.shape[0] + LATE),
             pltpu.SemaphoreType.DMA,
         ],
-        compiler_params=params(30),
+        compiler_params=params(36),
         cost_estimate=cost(40 * 2 * BLK * BLK * 4 * VECS, 24 * 2**20),
         name="rest_apply",
     )(table, wanted, in_hbm(local_tiles), in_hbm(far_tiles), rounded, far_vecs, in_hbm(before))

time: 247 us -> 248 us (level)
  waiting for transfers between devices: 93.5 us -> 101 us
  Pallas kernels: 93.5 us -> 86.1 us
    all_to_all x5, waiting for transfers between devices: 91 us -> 97.7 us  [exchange(): return lax.all_to_all(blocks, 'gy', split_axis=0, concat_axis=0, tiled=True)]
    pallas_call x1, Pallas kernels: 30.6 us -> 27.8 us  [local_build(): pl.pallas_call(local_build_kernel, in_specs=[SMEM, HBM, VMEM], out_specs=...]
  transfers between devices with their start and end apart: 11 -> 11, of which waited for: 6 -> 7; matrix products, arithmetic and copies ran while one was open for 1% -> 1% of each run, Pallas kernels for 30% -> 27%
where the time goes in v6:
time: 248 us; the launch traced here: 247 us
  waiting for transfers between devices  101 us (41%)
  Pallas kernels  86.1 us (35%)
  starting transfers between devices  41.9 us (17%)
  blocking collectives  13.8 us (6%)
    all_to_all x5, waiting for transfers between devices, exchange(): return lax.all_to_all(blocks, 'gy', split_axis=0, concat_axis=0, tiled=True)  97.7 us
    all_to_all x5, starting transfers between devices, exchange(): return lax.all_to_all(blocks, 'gy', split_axis=0, concat_axis=0, tiled=True)  33.6 us
    pallas_call x1, Pallas kernels, local_build(): pl.pallas_call(local_build_kernel, in_specs=[SMEM, HBM, VMEM], out_specs=...  27.8 us
    all_to_all x1, blocking collectives, exchange(): return lax.all_to_all(blocks, 'gy', split_axis=0, concat_axis=0, tiled=True)  13.8 us
    pallas_call x1, Pallas kernels, far_build(): pl.pallas_call(far_build_kernel, in_specs=[SMEM, HBM, HBM, VMEM, SMEM], o...  10.3 us
    pallas_call x1, Pallas kernels, rest_apply(): pl.pallas_call(rest_apply_kernel, in_specs=[SMEM, SMEM, HBM, HBM, VMEM, V...  8.75 us
    ppermute x6, starting transfers between devices, sum_over_gx(): lax.ppermute(gram, 'gx', [(i, i ^ mask) for i in range(size)])  8.34 us
    pallas_call x1, Pallas kernels, far_back(): pl.pallas_call(far_back_kernel, in_specs=[SMEM, HBM, VMEM, SMEM], out_spe...  6.46 us
  transfers between devices with their start and end apart: 11, of which 7 were waited for; matrix products, arithmetic and copies ran while one was open for 1% of the time, Pallas kernels for 27%

profile of v6, /device:TPU:1, one launch (start us, length us, event | category | flops | bytes accessed | tf_op | source)
XLA Modules:
  0.0 246.6 jit_solution(14292826390866803986)
XLA Ops:
  0.7 6.0 %prepare.1 = (bf16[32,528,256]{2,1,0:T(8,128)(2,1)}, bf16[32,12288]{1,0:T(8,128)(2,1)S(1)}, s32[192]{0:T(256)S(1)}) custom-call(s32[1]{0:T(128)S(6)} %copy.7.counts, s32[2,64]{1,0:T(2,128)} %bitcast.3, s32[1,32]{1,0:T(1,128)} %all_requests.1, bf16[12288,256]{1,0:T(8,128)(2,1)} %raw.3, f32[32,12288]{1,0:T(8,128)} %start.1), custom_call_target="tpu_custom_call" | custom-call | flops 10000000 | bytes 25165824 | tf_op jit(solution)/shard_map/prepare/pallas_call | solution.py:224
  6.7 9.1 %all-to-all-start = ((bf16[32,528,256]{2,1,0:T(8,128)(2,1)}), bf16[32,528,256]{2,1,0:T(8,128)(2,1)}, u32[]{:S(2)}, u32[]{:S(2)}) async-start(bf16[32,528,256]{2,1,0:T(8,128)(2,1)} %get-tuple-element.24), calls=%async_computation | async-start | bytes 17301504 | tf_op jit(solution)/shard_map/all_to_all | solution.py:872
  15.8 27.8 %local_build.1 = (bf16[24,512,256]{2,1,0:T(8,128)(2,1)}, f32[32,12288]{1,0:T(8,128)}, bf16[33,512,512]{2,1,0:T(8,128)(2,1)}, bf16[32,32,512]{2,1,0:T(8,128)(2,1)}, s32[1]{0:T(128)}) custom-call(s32[192]{0:T(256)S(1)} %get-tuple-element.23.table, bf16[12288,256]{1,0:T(8,128)(2,1)} %raw.3, bf16[32,12288]{1,0:T(8,128)(2,1)S(1)} %get-tuple-element.25.rounded), custom_call_target="tpu_custom_call" | custom-call | flops 8858370048 | bytes 33554432 | tf_op jit(solution)/shard_map/local_build/pallas_call | solution.py:331
  43.5 75.1 %all-to-all-done.far_rows = bf16[32,528,256]{2,1,0:T(8,128)(2,1)} async-done(((bf16[32,528,256]{2,1,0:T(8,128)(2,1)}), bf16[32,528,256]{2,1,0:T(8,128)(2,1)}, u32[]{:S(2)}, u32[]{:S(2)}) %all-to-all-start) | async-done | bytes 8650784 | tf_op jit(solution)/shard_map/all_to_all | solution.py:872
  118.7 10.3 %all-to-all-start.1 = ((bf16[32,32,512]{2,1,0:T(8,128)(2,1)}), bf16[32,32,512]{2,1,0:T(8,128)(2,1)S(1)}, u32[]{:S(2)}, u32[]{:S(2)}) async-start(bf16[32,32,512]{2,1,0:T(8,128)(2,1)} %get-tuple-element.29), calls=%async_computation.1 | async-start | bytes 2097152 | tf_op jit(solution)/shard_map/all_to_all | solution.py:872
  129.0 1.5 fusion.wanted
  130.5 10.3 %far_build.1 = (bf16[32,32,512]{2,1,0:T(8,128)(2,1)}, f32[8,128]{1,0:T(8,128)S(1)}, bf16[32,512,512]{2,1,0:T(8,128)(2,1)}) custom-call(s32[32]{0:T(128)S(1)} %fusion.wanted, bf16[24,512,256]{2,1,0:T(8,128)(2,1)} %get-tuple-element.26.units, bf16[32,528,256]{2,1,0:T(8,128)(2,1)} %all-to-all-done.far_rows, bf16[32,12288]{1,0:T(8,128)(2,1)S(1)} %get-tuple-element.25.rounded, ...), custom_call_target="tpu_custom_call" | custom-call | flops 6442450944 | bytes 35651584 | tf_op jit(solution)/shard_map/far_build/pallas_call | solution.py:462
  140.8 5.5 %all-to-all-done.1.far_vecs = bf16[32,32,512]{2,1,0:T(8,128)(2,1)S(1)} async-done(((bf16[32,32,512]{2,1,0:T(8,128)(2,1)}), bf16[32,32,512]{2,1,0:T(8,128)(2,1)S(1)}, u32[]{:S(2)}, u32[]{:S(2)}) %all-to-all-start.1) | async-done | bytes 1048608 | tf_op jit(solution)/shard_map/all_to_all | solution.py:872
  146.3 4.3 %all-to-all-start.2 = ((bf16[32,32,512]{2,1,0:T(8,128)(2,1)}), bf16[32,32,512]{2,1,0:T(8,128)(2,1)S(1)}, u32[]{:S(2)}, u32[]{:S(2)}) async-start(bf16[32,32,512]{2,1,0:T(8,128)(2,1)} %get-tuple-element.31), calls=%async_computation.2 | async-start | bytes 2097152 | tf_op jit(solution)/shard_map/all_to_all | solution.py:872
  150.6 4.0 %collective-permute-start.2 = (f32[8,128]{1,0:T(8,128)S(1)}, f32[8,128]{1,0:T(8,128)S(1)}, u32[]{:S(2)}, u32[]{:S(2)}) collective-permute-start(f32[8,128]{1,0:T(8,128)S(1)} %get-tuple-element.32), channel_id=1, source_target_pairs={{0,96},{32,64},{64,32},{96,0},{1,97},{33,65},{65,33},{97,1},{2,98}... | collective-permute-start | bytes 12296 | tf_op jit(solution)/shard_map/ppermute | solution.py:861
  154.6 0.0 collective-permute-start.1
  154.6 0.7 collective-permute-start
  155.3 1.2 copy-done.1
  156.5 5.8 %far_first.1.own = f32[32,12288]{1,0:T(8,128)S(1)} custom-call(s32[32]{0:T(128)S(1)} %fusion.wanted, bf16[32,512,512]{2,1,0:T(8,128)(2,1)} %get-tuple-element.28.tiles.far_tiles, bf16[32,32,512]{2,1,0:T(8,128)(2,1)S(1)} %copy-done.1, f32[32,12288]{1,0:T(8,128)} %get-tuple-element.30.before), custom_call_target="tpu_custom_call" | custom-call | flops 2147483648 | bytes 20971520 | tf_op jit(solution)/shard_map/far_first/pallas_call | solution.py:617
  162.3 0.0 collective-permute-done.2
  162.4 1.8 basis.1.inverse
  164.2 3.6 %all-to-all-done.2.returned = bf16[32,32,512]{2,1,0:T(8,128)(2,1)S(1)} async-done(((bf16[32,32,512]{2,1,0:T(8,128)(2,1)}), bf16[32,32,512]{2,1,0:T(8,128)(2,1)S(1)}, u32[]{:S(2)}, u32[]{:S(2)}) %all-to-all-start.2) | async-done | bytes 1048608 | tf_op jit(solution)/shard_map/all_to_all | solution.py:872
  167.8 5.3 %forward.1 = (bf16[32,12288]{1,0:T(8,128)(2,1)S(1)}, f32[8,128]{1,0:T(8,128)S(1)}, bf16[32,32,512]{2,1,0:T(8,128)(2,1)}) custom-call(s32[192]{0:T(256)S(1)} %get-tuple-element.23.table, f32[32,12288]{1,0:T(8,128)S(1)} %far_first.1.own, bf16[32,32,512]{2,1,0:T(8,128)(2,1)S(1)} %all-to-all-done.2.returned, f32[32,32]{1,0:T(8,128)S(1)} %basis.1.inverse), custom_call_target="tpu_custom_call" | custom-call | flops 100000000 | bytes 5242880 | tf_op jit(solution)/shard_map/forward/pallas_call | solution.py:733
  173.1 5.3 %all-to-all-start.3 = ((bf16[32,32,512]{2,1,0:T(8,128)(2,1)}), bf16[32,32,512]{2,1,0:T(8,128)(2,1)S(1)}, u32[]{:S(2)}, u32[]{:S(2)}) async-start(bf16[32,32,512]{2,1,0:T(8,128)(2,1)} %get-tuple-element.36), calls=%async_computation.3 | async-start | bytes 2097152 | tf_op jit(solution)/shard_map/all_to_all | solution.py:872
  178.4 5.8 %own_apply.1 = (f32[32,12288]{1,0:T(8,128)}, s32[1]{0:T(128)}) custom-call(bf16[33,512,512]{2,1,0:T(8,128)(2,1)} %get-tuple-element.34.tiles.local_tiles, bf16[32,12288]{1,0:T(8,128)(2,1)S(1)} %get-tuple-element.35.rounded), custom_call_target="tpu_custom_call" | custom-call | flops 1610612736 | bytes 13631488 | tf_op jit(solution)/shard_map/own_apply/pallas_call | solution.py:545
  184.2 6.5 %far_back.1 = bf16[32,32,512]{2,1,0:T(8,128)(2,1)} custom-call(s32[32]{0:T(128)S(1)} %fusion.wanted, bf16[32,512,512]{2,1,0:T(8,128)(2,1)} %get-tuple-element.28.tiles.far_tiles, bf16[32,12288]{1,0:T(8,128)(2,1)S(1)} %get-tuple-element.35.rounded, s32[1]{0:T(128)} %get-tuple-element.38.after), custom_call_target="tpu_custom_call" | custom-call | flops 2147483648 | bytes 17825792 | tf_op jit(solution)/shard_map/far_back/pallas_call | solution.py:582
  190.6 4.9 %all-to-all-done.3.far_vecs = bf16[32,32,512]{2,1,0:T(8,128)(2,1)S(1)} async-done(((bf16[32,32,512]{2,1,0:T(8,128)(2,1)}), bf16[32,32,512]{2,1,0:T(8,128)(2,1)S(1)}, u32[]{:S(2)}, u32[]{:S(2)}) %all-to-all-start.3) | async-done | bytes 1048608 | tf_op jit(solution)/shard_map/all_to_all | solution.py:872
  195.6 4.6 %all-to-all-start.4 = ((bf16[32,32,512]{2,1,0:T(8,128)(2,1)}), bf16[32,32,512]{2,1,0:T(8,128)(2,1)}, u32[]{:S(2)}, u32[]{:S(2)}) async-start(bf16[32,32,512]{2,1,0:T(8,128)(2,1)} %far_back.1), calls=%async_computation.4 | async-start | bytes 2097152 | tf_op jit(solution)/shard_map/all_to_all | solution.py:872
  200.2 8.7 %rest_apply.1.own = f32[32,12288]{1,0:T(8,128)S(1)} custom-call(s32[192]{0:T(256)S(1)} %get-tuple-element.23.table, s32[32]{0:T(128)S(1)} %fusion.wanted, bf16[33,512,512]{2,1,0:T(8,128)(2,1)} %get-tuple-element.34.tiles.local_tiles, bf16[32,512,512]{2,1,0:T(8,128)(2,1)} %get-tuple-element.28.tiles.far_tiles, ...), custom_call_target="tpu_custom_call" | custom-call | flops 2684354560 | bytes 25165824 | tf_op jit(solution)/shard_map/rest_apply/pallas_call | solution.py:667
  209.0 8.6 %all-to-all-done.4.returned = bf16[32,32,512]{2,1,0:T(8,128)(2,1)} async-done(((bf16[32,32,512]{2,1,0:T(8,128)(2,1)}), bf16[32,32,512]{2,1,0:T(8,128)(2,1)}, u32[]{:S(2)}, u32[]{:S(2)}) %all-to-all-start.4) | async-done | bytes 1048608 | tf_op jit(solution)/shard_map/all_to_all | solution.py:872
  217.5 2.7 %assemble.1 = (f32[32,12288]{1,0:T(8,128)S(1)}, f32[8,128]{1,0:T(8,128)S(1)}) custom-call(s32[192]{0:T(256)S(1)} %get-tuple-element.23.table, f32[32,12288]{1,0:T(8,128)S(1)} %rest_apply.1.own, bf16[32,32,512]{2,1,0:T(8,128)(2,1)} %all-to-all-done.4.returned), custom_call_target="tpu_custom_call" | custom-call | flops 100000000 | bytes 5242880 | tf_op jit(solution)/shard_map/assemble/pallas_call | solution.py:758
  220.3 3.0 %collective-permute-start.5 = (f32[16,128]{1,0:T(8,128)S(1)}, f32[16,128]{1,0:T(8,128)S(1)}, u32[]{:S(2)}, u32[]{:S(2)}) collective-permute-start(f32[16,128]{1,0:T(8,128)S(1)} %constant_dynamic-update-slice_fusion), channel_id=1, source_target_pairs={{0,96},{32,64},{64,32},{96,0},{1,97},{33,65},{65,33},{97,1},{2,98}... | collective-permute-start | bytes 24584 | tf_op jit(solution)/shard_map/ppermute | solution.py:861
  223.3 0.7 collective-permute-start.3
  223.9 0.4 collective-permute-done.5
  224.3 3.0 %collective-permute-done.4 = f32[16,128]{1,0:T(8,128)S(1)} collective-permute-done((f32[16,128]{1,0:T(8,128)S(1)}, f32[16,128]{1,0:T(8,128)S(1)}, u32[]{:S(2)}, u32[]{:S(2)}) %collective-permute-start.4) | collective-permute-done | bytes 8224 | tf_op jit(solution)/shard_map/ppermute | solution.py:861
  227.3 13.8 %all_to_all.30.grams = f32[32,16,128]{2,1,0:T(8,128)S(1)} all-to-all(f32[32,16,128]{2,1,0:T(8,128)S(1)} %broadcast_in_dim.3), channel_id=1, replica_groups=mesh['gx'=4,'gy'=32] {'gy'}, dimensions={0} | all-to-all | bytes 524288 | tf_op jit(solution)/shard_map/all_to_all | solution.py:872
  241.1 5.4 %last.1 = f32[32,12288]{1,0:T(8,128)} custom-call(f32[32,16,128]{2,1,0:T(8,128)S(1)} %all_to_all.30.grams, f32[32,12288]{1,0:T(8,128)S(1)} %get-tuple-element.40.image), custom_call_target="tpu_custom_call" | custom-call | flops 100000000 | bytes 4194304 | tf_op jit(solution)/shard_map/last/pallas_call | solution.py:843
  (12 shorter events, 0.1 us)
Async XLA Ops:
  6.7 112.0 %all-to-all-start = ((bf16[32,528,256]{2,1,0:T(8,128)(2,1)}), bf16[32,528,256]{2,1,0:T(8,128)(2,1)}, u32[]{:S(2)}, u32[]{:S(2)}) async-start(bf16[32,528,256]{2,1,0:T(8,128)(2,1)} %get-tuple-element.24), calls=%async_computation | async-start | bytes 17301504 | tf_op jit(solution)/shard_map/all_to_all | solution.py:872
  118.7 27.6 %all-to-all-start.1 = ((bf16[32,32,512]{2,1,0:T(8,128)(2,1)}), bf16[32,32,512]{2,1,0:T(8,128)(2,1)S(1)}, u32[]{:S(2)}, u32[]{:S(2)}) async-start(bf16[32,32,512]{2,1,0:T(8,128)(2,1)} %get-tuple-element.29), calls=%async_computation.1 | async-start | bytes 2097152 | tf_op jit(solution)/shard_map/all_to_all | solution.py:872
  146.3 9.0 %copy-start = (bf16[32,32,512]{2,1,0:T(8,128)(2,1)}, bf16[32,32,512]{2,1,0:T(8,128)(2,1)S(1)}, u32[]{:S(2)}) copy-start(bf16[32,32,512]{2,1,0:T(8,128)(2,1)S(1)} %all-to-all-done.1.far_vecs) | copy-start | bytes 3145732
  146.3 21.5 %all-to-all-start.2 = ((bf16[32,32,512]{2,1,0:T(8,128)(2,1)}), bf16[32,32,512]{2,1,0:T(8,128)(2,1)S(1)}, u32[]{:S(2)}, u32[]{:S(2)}) async-start(bf16[32,32,512]{2,1,0:T(8,128)(2,1)} %get-tuple-element.31), calls=%async_computation.2 | async-start | bytes 2097152 | tf_op jit(solution)/shard_map/all_to_all | solution.py:872
  150.6 11.7 %collective-permute-start.2 = (f32[8,128]{1,0:T(8,128)S(1)}, f32[8,128]{1,0:T(8,128)S(1)}, u32[]{:S(2)}, u32[]{:S(2)}) collective-permute-start(f32[8,128]{1,0:T(8,128)S(1)} %get-tuple-element.32), channel_id=1, source_target_pairs={{0,96},{32,64},{64,32},{96,0},{1,97},{33,65},{65,33},{97,1},{2,98}... | collective-permute-start | bytes 12296 | tf_op jit(solution)/shard_map/ppermute | solution.py:861
  154.6 7.7 %collective-permute-start.1 = (f32[8,128]{1,0:T(8,128)S(1)}, f32[8,128]{1,0:T(8,128)S(1)}, u32[]{:S(2)}, u32[]{:S(2)}) collective-permute-start(f32[8,128]{1,0:T(8,128)S(1)} %get-tuple-element.32), channel_id=1, source_target_pairs={{0,64},{32,96},{64,0},{96,32},{1,65},{33,97},{65,1},{97,33},{2,66}... | collective-permute-start | bytes 12296 | tf_op jit(solution)/shard_map/ppermute | solution.py:861
  154.6 7.7 %collective-permute-start = (f32[8,128]{1,0:T(8,128)S(1)}, f32[8,128]{1,0:T(8,128)S(1)}, u32[]{:S(2)}, u32[]{:S(2)}) collective-permute-start(f32[8,128]{1,0:T(8,128)S(1)} %get-tuple-element.32), channel_id=1, source_target_pairs={{0,32},{32,0},{64,96},{96,64},{1,33},{33,1},{65,97},{97,65},{2,34}... | collective-permute-start | bytes 12296 | tf_op jit(solution)/shard_map/ppermute | solution.py:861
  155.3 1.2 copy-start.1
  173.1 22.5 %all-to-all-start.3 = ((bf16[32,32,512]{2,1,0:T(8,128)(2,1)}), bf16[32,32,512]{2,1,0:T(8,128)(2,1)S(1)}, u32[]{:S(2)}, u32[]{:S(2)}) async-start(bf16[32,32,512]{2,1,0:T(8,128)(2,1)} %get-tuple-element.36), calls=%async_computation.3 | async-start | bytes 2097152 | tf_op jit(solution)/shard_map/all_to_all | solution.py:872
  195.6 22.0 %all-to-all-start.4 = ((bf16[32,32,512]{2,1,0:T(8,128)(2,1)}), bf16[32,32,512]{2,1,0:T(8,128)(2,1)}, u32[]{:S(2)}, u32[]{:S(2)}) async-start(bf16[32,32,512]{2,1,0:T(8,128)(2,1)} %far_back.1), calls=%async_computation.4 | async-start | bytes 2097152 | tf_op jit(solution)/shard_map/all_to_all | solution.py:872
  220.3 4.0 %collective-permute-start.5 = (f32[16,128]{1,0:T(8,128)S(1)}, f32[16,128]{1,0:T(8,128)S(1)}, u32[]{:S(2)}, u32[]{:S(2)}) collective-permute-start(f32[16,128]{1,0:T(8,128)S(1)} %constant_dynamic-update-slice_fusion), channel_id=1, source_target_pairs={{0,96},{32,64},{64,32},{96,0},{1,97},{33,65},{65,33},{97,1},{2,98}... | collective-permute-start | bytes 24584 | tf_op jit(solution)/shard_map/ppermute | solution.py:861
  223.3 4.0 %collective-permute-start.4 = (f32[16,128]{1,0:T(8,128)S(1)}, f32[16,128]{1,0:T(8,128)S(1)}, u32[]{:S(2)}, u32[]{:S(2)}) collective-permute-start(f32[16,128]{1,0:T(8,128)S(1)} %constant_dynamic-update-slice_fusion), channel_id=1, source_target_pairs={{0,64},{32,96},{64,0},{96,32},{1,65},{33,97},{65,1},{97,33},{2,66}... | collective-permute-start | bytes 24584 | tf_op jit(solution)/shard_map/ppermute | solution.py:861
  223.3 4.0 %collective-permute-start.3 = (f32[16,128]{1,0:T(8,128)S(1)}, f32[16,128]{1,0:T(8,128)S(1)}, u32[]{:S(2)}, u32[]{:S(2)}) collective-permute-start(f32[16,128]{1,0:T(8,128)S(1)} %constant_dynamic-update-slice_fusion), channel_id=1, source_target_pairs={{0,32},{32,0},{64,96},{96,64},{1,33},{33,1},{65,97},{97,65},{2,34}... | collective-permute-start | bytes 24584 | tf_op jit(solution)/shard_map/ppermute | solution.py:861
